TPU v7x, 512 devices: a whole 4x4x16 slice. The times are simulated.
512 devices in a mesh: replica: 64 (over x, y, z_lo), fsdp: 8 (over z_hi, core).
Axes of the slice: x: 4, y: 4, z: 16 (z_hi: 4, z_lo: 4; z = z_hi * 4 + z_lo), core: 2. Of those that a mesh axis runs over, the one named last changes fastest.
Arguments:
- tokens: bfloat16 [131072, 4096], P(('replica', 'fsdp')), may hold values from -6 to 6
- w_key: float32 [4096, 512], P('fsdp'), may hold values from -0.09375 to 0.09375
- targets: bfloat16 [131072, 512], P(('replica', 'fsdp')), may hold values from -6 to 6
- frag_outer: float32 [4096, 1024], P(('fsdp', 'replica')), may hold values from -6 to 6
- frag_local: bfloat16 [262144, 1024], P(('replica', 'fsdp')), may hold values from -6 to 6
- frag_moment: float32 [4096, 1024], P(('fsdp', 'replica')), may hold values from -6 to 6
Outputs:
- new_key: float32 [262144, 512], P(('replica', 'fsdp'))
- new_outer: float32 [4096, 1024], P(('fsdp', 'replica'))
- new_moment: float32 [4096, 1024], P(('fsdp', 'replica'))
All inputs are finite; a program needn't handle non-finite values.
Results may differ from a plain program's by a relative error of at most 0.017.
Values may be sent and summed in bfloat16 or wider, within the bound.
No kernel may reach another device: no remote copies, remote signals or barrier semaphores. Data moves between devices by JAX's collectives and lax.ppermute only.
A program may use at most 64 MiB of HBM per device.

v0:
```python
import jax
import jax.numpy as jnp
from jax import lax
from jax.sharding import PartitionSpec as P

INNER_RATE = 4.0
OUTER_RATE = 0.7
MOMENTUM = 0.9


def on_device(tokens, w_key, targets, frag_outer, frag_local, frag_moment):
    width = tokens.shape[1]
    columns = tokens
    keys = jnp.dot(
        columns,
        lax.all_gather(w_key.astype(jnp.bfloat16), "fsdp", axis=0, tiled=True),
        preferred_element_type=jnp.float32,
    )
    errors = (keys - targets.astype(jnp.float32)).astype(jnp.bfloat16)
    columns = tokens
    grad = lax.psum_scatter(
        jnp.dot(columns.T, errors, preferred_element_type=jnp.float32).astype(jnp.bfloat16),
        "fsdp",
        scatter_dimension=0,
        tiled=True,
    ).astype(jnp.float32)
    new_key = w_key - INNER_RATE / width * grad
    replicas = lax.axis_size("replica")
    owned = frag_outer.shape[0]
    pieces = lax.all_to_all(frag_local, "replica", split_axis=0, concat_axis=0, tiled=True)
    mine = pieces.astype(jnp.float32).reshape(replicas, owned, -1).sum(0)
    mean = frag_outer - mine / replicas
    new_moment = MOMENTUM * frag_moment + mean
    new_outer = frag_outer - OUTER_RATE * (mean + MOMENTUM * new_moment)
    return (new_key, new_outer, new_moment)


def solution(mesh):
    in_specs = (
        P(("replica", "fsdp"), None),
        P("fsdp", None),
        P(("replica", "fsdp"), None),
        P(("fsdp", "replica"), None),
        P(("replica", "fsdp"), None),
        P(("fsdp", "replica"), None),
    )
    out_specs = (
        P(("replica", "fsdp"), None),
        P(("fsdp", "replica"), None),
        P(("fsdp", "replica"), None),
    )
    return jax.shard_map(
        on_device, mesh=mesh, in_specs=in_specs, out_specs=out_specs, check_vma=False
    )
```

profile of v0, /device:TPU:89, one launch (start us, length us, event | category | flops | bytes accessed | tf_op | source)
XLA Modules:
  0.0 249.1 jit_solution(3685921377128351681)
XLA Ops:
  7.2 0.0 copy-start
  7.2 0.0 all-gather.2.cloned.1.call-start
  7.2 2.2 convert_element_type.22
  9.4 0.0 all-gather.2.cloned.1.call-update
  9.5 0.0 reduce-scatter.2.cloned.1.call-start
  9.5 98.6 %all-gather.2.cloned.1.call-done = bf16[4096,512]{1,0:T(8,128)(2,1)} async-done(((bf16[512,512]{1,0:T(8,128)(2,1)}), bf16[4096,512]{1,0:T(8,128)(2,1)}) %all-gather.2.cloned.1.call-update) | async-done | bytes 4194320 | tf_op jit(solution)/shard_map/all_gather | solution.py:16
  108.1 0.0 copy-done
  108.1 6.7 %fusion = bf16[4096,512]{0,1:T(8,128)(2,1)} fusion(bf16[256,4096]{1,0:T(8,128)(2,1)S(1)} %copy-done, bf16[4096,512]{1,0:T(8,128)(2,1)} %all-gather.2.cloned.1.call-done, bf16[256,512]{1,0:T(8,128)(2,1)} %param.8), kind=kOutput, calls=%fused_computation.1 | convolution fusion | flops 2149974016 | bytes 10747904 | tf_op jit(solution)/shard_map/dot_general | solution.py:22
  114.8 0.0 copy-start.1
  114.8 0.0 copy-start.2
  114.8 0.0 copy-start.3
  114.8 0.0 reduce-scatter.2.cloned.1.call-update
  114.8 10.6 %all-to-all-start = ((bf16[64,8,1024]{2,1,0:T(8,128)(2,1)}), bf16[64,8,1024]{2,1,0:T(8,128)(2,1)}, u32[]{:S(2)}, u32[]{:S(2)}) async-start(bf16[64,8,1024]{2,1,0:T(8,128)(2,1)} %bitcast.6), calls=%async_computation.1 | async-start | bytes 2097152 | tf_op jit(solution)/shard_map/all_to_all | solution.py:30
  125.5 0.0 copy-done.1
  125.5 1.3 copy.9
  126.8 73.1 %all-to-all-done = bf16[64,8,1024]{2,1,0:T(8,128)(2,1)} async-done(((bf16[64,8,1024]{2,1,0:T(8,128)(2,1)}), bf16[64,8,1024]{2,1,0:T(8,128)(2,1)}, u32[]{:S(2)}, u32[]{:S(2)}) %all-to-all-start) | async-done | bytes 1048608 | tf_op jit(solution)/shard_map/all_to_all | solution.py:30
  199.9 1.4 convert_reduce_fusion
  201.3 0.0 copy-done.2
  201.3 0.0 copy-done.3
  201.3 0.6 multiply_subtract_fusion.1
  201.9 37.5 %reduce-scatter.2.cloned.1.call-done = bf16[512,512]{0,1:T(8,128)(2,1)} async-done(((bf16[4096,512]{0,1:T(8,128)(2,1)}), bf16[512,512]{0,1:T(8,128)(2,1)}) %reduce-scatter.2.cloned.1.call-update) | async-done | bytes 524304 | tf_op jit(solution)/shard_map/reduce_scatter | solution.py:21
  239.4 1.5 multiply_subtract_fusion
  241.0 1.3 copy.10
Async XLA Ops:
  7.2 101.0 %copy-start = (bf16[256,4096]{1,0:T(8,128)(2,1)S(1)}, bf16[256,4096]{1,0:T(8,128)(2,1)}, u32[]{:S(2)}) copy-start(bf16[256,4096]{1,0:T(8,128)(2,1)} %param.6) | copy-start | bytes 6291460
  7.2 100.9 %all-gather.2.cloned.1.call-start = ((), (), s32[]{:S(2)}) async-start(), calls=%async_computation.2 | async-start | bytes 4718592 | tf_op jit(solution)/shard_map/all_gather | solution.py:16
  9.5 230.0 %reduce-scatter.2.cloned.1.call-start = ((), (), s32[]{:S(2)}) async-start(), calls=%async_computation.3 | async-start | bytes 4718592 | tf_op jit(solution)/shard_map/reduce_scatter | solution.py:21
  114.8 10.7 %copy-start.1 = (f32[512,512]{1,0:T(8,128)S(1)}, f32[512,512]{1,0:T(8,128)}, u32[]{:S(2)}) copy-start(f32[512,512]{1,0:T(8,128)} %param.7) | copy-start | bytes 3145732
  114.8 86.5 %copy-start.2 = (f32[8,1024]{1,0:T(8,128)S(1)}, f32[8,1024]{1,0:T(8,128)}, u32[]{:S(2)}) copy-start(f32[8,1024]{1,0:T(8,128)} %param.9) | copy-start | bytes 98308
  114.8 86.5 %copy-start.3 = (f32[8,1024]{1,0:T(8,128)S(1)}, f32[8,1024]{1,0:T(8,128)}, u32[]{:S(2)}) copy-start(f32[8,1024]{1,0:T(8,128)} %param.11) | copy-start | bytes 98308
  114.8 85.1 %all-to-all-start = ((bf16[64,8,1024]{2,1,0:T(8,128)(2,1)}), bf16[64,8,1024]{2,1,0:T(8,128)(2,1)}, u32[]{:S(2)}, u32[]{:S(2)}) async-start(bf16[64,8,1024]{2,1,0:T(8,128)(2,1)} %bitcast.6), calls=%async_computation.1 | async-start | bytes 2097152 | tf_op jit(solution)/shard_map/all_to_all | solution.py:30
Sparse Core Ops, SparseCore 0:
  10.7 97.3 all-gather.1
  114.9 124.4 reduce-scatter.1
where the time goes:
time: 249 us
  waiting for transfers between devices  209 us (84%)
  between operations  14.1 us (6%)
  starting transfers between devices  10.7 us (4%)
  matrix products  6.67 us (3%)
  other arithmetic  5.78 us (2%)
  local copies, waits for them, and re-layouts  2.64 us (1%)
    all_gather x1, waiting for transfers between devices, on_device(): lax.all_gather(w_key.astype(jnp.bfloat16), 'fsdp', axis=0, tiled=True)  98.6 us
    all_to_all x1, waiting for transfers between devices, on_device(): lax.all_to_all(frag_local, 'replica', split_axis=0, concat_axis=0, tiled=...  73.1 us
    reduce_scatter x1, waiting for transfers between devices, on_device(): lax.psum_scatter(jnp.dot(columns.T, errors, preferred_element_type=jnp.fl...  37.5 us
    all_to_all x1, starting transfers between devices, on_device(): lax.all_to_all(frag_local, 'replica', split_axis=0, concat_axis=0, tiled=...  10.6 us
    dot_general x1, matrix products, on_device(): jnp.dot(columns.T, errors, preferred_element_type=jnp.float32)  6.67 us
  transfers between devices with their start and end apart: 3, of which 3 were waited for; matrix products, arithmetic and copies ran while one was open for 1% of the time, Pallas kernels for 0%

commit v1 on v0

v1 whole, which is shorter than its diff:
```python
import jax
import jax.numpy as jnp
from jax import lax
from jax.experimental import pallas as pl
from jax.experimental.pallas import tpu as pltpu
from jax.sharding import Mesh, PartitionSpec as P

INNER_RATE = 4.0
OUTER_RATE = 0.7
MOMENTUM = 0.9

X, Y, ZL, ZH = 4, 4, 4, 4
PARAMS = pltpu.CompilerParams(vmem_limit_bytes=40 * 1024 * 1024)
SWAP = [(0, 1), (1, 0)]


def shift(a, step):
    return lax.ppermute(a, "zh", [(i, (i + step) % ZH) for i in range(ZH)])


def transpose_kernel(place, own, mate, out):
    zh, core = place[0], place[1]
    width = out.shape[1]
    tokens = own.shape[0]
    for j in range(ZH):
        block = lax.rem(zh + j, ZH) * 2 + core
        columns = pl.ds(pl.multiple_of(block * width, width), width)
        out[j, :, :tokens] = own[:, columns].T
        out[j, :, tokens:] = mate[:, columns].T


def error_kernel(own, mate, w, goal_own, goal_mate, out):
    shards, depth = w.shape[1], w.shape[0] * w.shape[2]
    tokens = own.shape[0]
    width = w.shape[3]
    for half, (x, goal) in enumerate(((own, goal_own), (mate, goal_mate))):
        keys = jnp.zeros((tokens, width), jnp.float32)
        for f in range(shards):
            keys += jnp.dot(
                x[:, f * depth : (f + 1) * depth],
                w[:, f].reshape(depth, width),
                preferred_element_type=jnp.float32,
            )
        errors = keys - goal[...].astype(jnp.float32)
        out[half * tokens : (half + 1) * tokens, :] = errors.astype(jnp.bfloat16)


def gradient_kernel(place, xt, err_own, err_mate, first, second, third, own, *, order):
    core = place[1]
    tokens = err_own.shape[0] // 2
    mine = err_own[...]
    other = jnp.concatenate([err_mate[tokens:, :], err_mate[:tokens, :]], axis=0)
    low = jnp.where(core == 0, mine, other)
    high = jnp.where(core == 0, other, mine)
    errors = jnp.concatenate([low, high], axis=1)
    for j, out in zip(order, (first, second, third, own), strict=True):
        part = jnp.dot(xt[j], errors, preferred_element_type=jnp.float32)
        out[...] = part.astype(out.dtype)


def finish_kernel(w, own_a, own_b, plain_a, plain_b, sum_a, sum_b, out, *, rate):
    lanes = own_a.shape[1] // 2
    for h, (own, plain, total) in enumerate(((own_a, plain_a, sum_a), (own_b, plain_b, sum_b))):
        grad = own[...] + plain[...].astype(jnp.float32) + total[...].astype(jnp.float32)
        for core in range(2):
            at = (core * 2 + h) * lanes
            out[:, at : at + lanes] = w[:, at : at + lanes] - rate * grad[:, core * lanes : (core + 1) * lanes]


def on_device(tokens, w_key, targets, frag_outer, frag_local, frag_moment):
    rows, width = tokens.shape
    own_rows, columns = w_key.shape
    half, lanes = columns // 2, columns // 4
    spots = X * Y
    core = lax.axis_index("c")
    zh = lax.axis_index("zh")
    spot = lax.axis_index("x") * Y + lax.axis_index("y")
    place = jnp.stack([zh, core]).astype(jnp.int32)
    smem = pl.BlockSpec(memory_space=pltpu.SMEM)
    vmem = pl.BlockSpec(memory_space=pltpu.VMEM)

    piece = own_rows // spots
    mine = lax.dynamic_slice_in_dim(w_key, spot * piece, piece, 0).astype(jnp.bfloat16)
    column = lax.all_gather(mine, ("zh", "c"), axis=0, tiled=True)
    column = lax.dynamic_slice_in_dim(column, core * half, half, 1)
    column = column.reshape(ZH * 2, piece, 2, lanes)

    def spread(part):
        copies = jnp.broadcast_to(part[None], (spots,) + part.shape)
        return lax.all_to_all(copies, ("x", "y"), 0, 0, tiled=True)

    key_a = spread(column[:, :, 0])
    key_b = spread(column[:, :, 1])

    mate = lax.ppermute(tokens, "c", SWAP)
    for_mate = lax.dynamic_slice_in_dim(targets, (1 - core) * half, half, 1)
    goal_own = lax.dynamic_slice_in_dim(targets, core * half, half, 1)
    goal_mate = lax.ppermute(for_mate, "c", SWAP)
    xt = pl.pallas_call(
        transpose_kernel,
        out_shape=jax.ShapeDtypeStruct((ZH, own_rows, 2 * rows), jnp.bfloat16),
        in_specs=[smem, vmem, vmem],
        out_specs=vmem,
        compiler_params=PARAMS,
    )(place, tokens, mate)

    def errors(key, at):
        return pl.pallas_call(
            error_kernel,
            out_shape=jax.ShapeDtypeStruct((2 * rows, lanes), jnp.bfloat16),
            in_specs=[vmem] * 5,
            out_specs=vmem,
            compiler_params=PARAMS,
        )(tokens, mate, key, goal_own[:, at : at + lanes], goal_mate[:, at : at + lanes])

    def gradient(err, order):
        err_mate = lax.ppermute(err, "c", SWAP)
        short = jax.ShapeDtypeStruct((own_rows, half), jnp.bfloat16)
        full = jax.ShapeDtypeStruct((own_rows, half), jnp.float32)

        def kernel(*refs):
            gradient_kernel(*refs, order=order)

        return pl.pallas_call(
            kernel,
            out_shape=(short, short, full, full),
            in_specs=[smem] + [vmem] * 3,
            out_specs=(vmem,) * 4,
            compiler_params=PARAMS,
        )(place, xt, err, err_mate)

    far_a, near_a, via_a, own_a = gradient(errors(key_a, 0), (2, 3, 1, 0))
    far_a = shift(far_a, 1)
    plain_a = shift(near_a, -1)
    far_b, near_b, via_b, own_b = gradient(errors(key_b, lanes), (2, 1, 3, 0))
    far_b = shift(far_b, -1)
    plain_b = shift(near_b, 1)
    sum_a = shift((via_a + far_a.astype(jnp.float32)).astype(jnp.bfloat16), 1)
    sum_b = shift((via_b + far_b.astype(jnp.float32)).astype(jnp.bfloat16), -1)

    rate = INNER_RATE / width

    def finish(*refs):
        finish_kernel(*refs, rate=rate)

    new_key = pl.pallas_call(
        finish,
        out_shape=jax.ShapeDtypeStruct(w_key.shape, jnp.float32),
        in_specs=[vmem] * 7,
        out_specs=vmem,
        compiler_params=PARAMS,
    )(w_key, own_a, own_b, plain_a, plain_b, sum_a, sum_b)

    owned = frag_outer.shape[0]
    pieces = lax.all_to_all(frag_local, ("x", "y"), 0, 0, tiled=True)
    part = pieces.astype(jnp.float32).reshape(spots, ZL * owned, -1).sum(0)
    part = lax.all_to_all(part, "zl", 0, 0, tiled=True)
    total = part.reshape(ZL, owned, -1).sum(0)
    mean = frag_outer - total / (spots * ZL)
    new_moment = MOMENTUM * frag_moment + mean
    new_outer = frag_outer - OUTER_RATE * (mean + MOMENTUM * new_moment)
    return (new_key, new_outer, new_moment)


def solution(mesh):
    grid = Mesh(mesh.devices.reshape(X, Y, ZL, ZH, 2), ("x", "y", "zl", "zh", "c"))
    replica, fsdp = ("x", "y", "zl"), ("zh", "c")
    in_specs = (
        P(replica + fsdp, None),
        P(fsdp, None),
        P(replica + fsdp, None),
        P(fsdp + replica, None),
        P(replica + fsdp, None),
        P(fsdp + replica, None),
    )
    out_specs = (
        P(replica + fsdp, None),
        P(fsdp + replica, None),
        P(fsdp + replica, None),
    )
    return jax.shard_map(
        on_device, mesh=grid, in_specs=in_specs, out_specs=out_specs, check_vma=False
    )
```

time: 249 us -> 188 us (0.76)
  the two profiles are of different devices: /device:TPU:89 before, /device:TPU:38 now
where the time goes in v1:
time: 188 us; the launch traced here: 187 us
  waiting for transfers between devices  57.2 us (30%)
  starting transfers between devices  55.5 us (30%)
  blocking collectives  45.9 us (24%)
  Pallas kernels  13.6 us (7%)
  other arithmetic  7.01 us (4%)
  local copies, waits for them, and re-layouts  6.72 us (4%)
    ppermute x6, starting transfers between devices, shift(): return lax.ppermute(a, 'zh', [(i, (i + step) % ZH) for i in range(ZH)])  29.3 us
    all_to_all x1, waiting for transfers between devices, on_device(): part = lax.all_to_all(part, 'zl', 0, 0, tiled=True)  26.2 us
    all_gather x1, blocking collectives, on_device(): column = lax.all_gather(mine, ('zh', 'c'), axis=0, tiled=True)  25.8 us
    all_to_all x1, blocking collectives, spread(): return lax.all_to_all(copies, ('x', 'y'), 0, 0, tiled=True)  20.1 us
    ppermute x6, waiting for transfers between devices, shift(): return lax.ppermute(a, 'zh', [(i, (i + step) % ZH) for i in range(ZH)])  16.5 us
    all_to_all x1, waiting for transfers between devices, spread(): return lax.all_to_all(copies, ('x', 'y'), 0, 0, tiled=True)  14 us
    all_to_all x1, starting transfers between devices, spread(): return lax.all_to_all(copies, ('x', 'y'), 0, 0, tiled=True)  7.43 us
    all_to_all x1, starting transfers between devices, on_device(): pieces = lax.all_to_all(frag_local, ('x', 'y'), 0, 0, tiled=True)  6.27 us
  transfers between devices with their start and end apart: 13, of which 7 were waited for; matrix products, arithmetic and copies ran while one was open for 5% of the time, Pallas kernels for 6%

profile of v1, /device:TPU:38, one launch (start us, length us, event | category | flops | bytes accessed | tf_op | source)
XLA Modules:
  0.0 186.9 jit_solution(18095472398880064207)
XLA Ops:
  0.6 0.9 dynamic-slice_convert_fusion
  1.5 25.8 %all_gather.3 = bf16[256,512]{1,0:T(8,128)(2,1)S(1)} all-gather(bf16[32,512]{1,0:T(8,128)(2,1)S(1)} %dynamic-slice_convert_fusion), channel_id=1, replica_groups=mesh['x'=4,'y'=4,'zl'=4,'zh'=4,'c'=2] {'zh','c'}, dimensions={0}, use_global_device_ids=true | all-gather | bytes 294912 | tf_op jit(solution)/shard_map/all_gather | solution.py:84
  27.3 0.0 copy-start
  27.3 0.2 fusion.1
  27.6 1.2 broadcast_in_dim.15
  28.8 7.4 %all-to-all-start = ((bf16[16,8,32,128]{3,2,1,0:T(8,128)(2,1)}), bf16[16,8,32,128]{3,2,1,0:T(8,128)(2,1)S(1)}, u32[]{:S(2)}, u32[]{:S(2)}) async-start(bf16[16,8,32,128]{3,2,1,0:T(8,128)(2,1)} %broadcast_in_dim.15), calls=%async_computation | async-start | bytes 2097152 | tf_op jit(solution)/shard_map/all_to_all | solution.py:90
  36.2 1.9 %collective-permute-start = (bf16[256,4096]{1,0:T(8,128)(2,1)S(1)}, bf16[256,4096]{1,0:T(8,128)(2,1)}, u32[]{:S(2)}, u32[]{:S(2)}) collective-permute-start(bf16[256,4096]{1,0:T(8,128)(2,1)S(1)} %copy-done), channel_id=1, source_target_pairs={{0,1},{1,0},{2,3},{3,2},{4,5},{5,4},{6,7},{7,6},{8,9},{9,8},{10,11... | collective-permute-start | bytes 6291464 | tf_op jit(solution)/shard_map/ppermute | solution.py:95
  38.1 14.0 %all-to-all-done.w = bf16[16,8,32,128]{3,2,1,0:T(8,128)(2,1)S(1)} async-done(((bf16[16,8,32,128]{3,2,1,0:T(8,128)(2,1)}), bf16[16,8,32,128]{3,2,1,0:T(8,128)(2,1)S(1)}, u32[]{:S(2)}, u32[]{:S(2)}) %all-to-all-start) | async-done | bytes 1048608 | tf_op jit(solution)/shard_map/all_to_all | solution.py:90
  52.1 0.2 broadcast_in_dim.17
  52.3 0.0 copy-start.5
  52.3 20.1 %all_to_all.28.w = bf16[16,8,32,128]{3,2,1,0:T(8,128)(2,1)} all-to-all(bf16[16,8,32,128]{3,2,1,0:T(8,128)(2,1)S(1)} %broadcast_in_dim.17), channel_id=1, replica_groups=mesh['x'=4,'y'=4,'zl'=4,'zh'=4,'c'=2] {'x','y'}, dimensions={0} | all-to-all | bytes 2097152 | tf_op jit(solution)/shard_map/all_to_all | solution.py:90
  72.4 6.3 %all-to-all-start.2 = ((bf16[16,32,1024]{2,1,0:T(8,128)(2,1)}), bf16[16,32,1024]{2,1,0:T(8,128)(2,1)}, u32[]{:S(2)}, u32[]{:S(2)}) async-start(bf16[16,32,1024]{2,1,0:T(8,128)(2,1)} %bitcast.10), calls=%async_computation.2 | async-start | bytes 2097152 | tf_op jit(solution)/shard_map/all_to_all | solution.py:155
  78.7 0.7 constant_dynamic-slice_fusion.1
  79.4 1.9 %collective-permute-start.1 = (bf16[256,256]{1,0:T(8,128)(2,1)}, bf16[256,256]{1,0:T(8,128)(2,1)S(1)}, u32[]{:S(2)}, u32[]{:S(2)}) collective-permute-start(bf16[256,256]{1,0:T(8,128)(2,1)} %constant_dynamic-slice_fusion.1), channel_id=1, source_target_pairs={{0,1},{1,0},{2,3},{3,2},{4,5},{5,4},{6,7},{7,6},{8,9},{9,8},{10,11... | collective-permute-start | bytes 393224 | tf_op jit(solution)/shard_map/ppermute | solution.py:98
  81.3 0.9 constant_dynamic-slice_fusion.2
  82.2 0.6 collective-permute-done.1
  82.8 0.0 collective-permute-done.mate
  82.9 1.2 copy-done.1
  84.1 2.8 %shard_map.88.refs_2_ = bf16[512,128]{1,0:T(8,128)(2,1)S(1)} custom-call(bf16[256,4096]{1,0:T(8,128)(2,1)S(1)} %copy-done, bf16[256,4096]{1,0:T(8,128)(2,1)} %collective-permute-done.mate, bf16[16,8,32,128]{3,2,1,0:T(8,128)(2,1)S(1)} %copy-done.1, bf16[256,128]{1,0:T(8,128)(2,1)S(1)} %get-tuple-element.21.goal_own, ...), custom_call_target="tpu_custom_call" | custom-call | tf_op jit(solution)/shard_map/pallas_call | solution.py:108
  86.9 2.1 %collective-permute-start.3 = (bf16[512,128]{1,0:T(8,128)(2,1)S(1)}, bf16[512,128]{1,0:T(8,128)(2,1)S(1)}, u32[]{:S(2)}, u32[]{:S(2)}) collective-permute-start(bf16[512,128]{1,0:T(8,128)(2,1)S(1)} %shard_map.88.refs_2_), channel_id=1, source_target_pairs={{0,1},{1,0},{2,3},{3,2},{4,5},{5,4},{6,7},{7,6},{8,9},{9,8},{10,11... | collective-permute-start | bytes 393224 | tf_op jit(solution)/shard_map/ppermute | solution.py:117
  89.0 2.8 %shard_map.86.refs_2_ = bf16[512,128]{1,0:T(8,128)(2,1)S(1)} custom-call(bf16[256,4096]{1,0:T(8,128)(2,1)S(1)} %copy-done, bf16[256,4096]{1,0:T(8,128)(2,1)} %collective-permute-done.mate, bf16[16,8,32,128]{3,2,1,0:T(8,128)(2,1)S(1)} %all-to-all-done.w, bf16[256,128]{1,0:T(8,128)(2,1)S(1)} %get-tuple-element.22.goal_own, ...), custom_call_target="tpu_custom_call" | custom-call | tf_op jit(solution)/shard_map/pallas_call | solution.py:108
  91.8 2.3 %collective-permute-start.2 = (bf16[512,128]{1,0:T(8,128)(2,1)S(1)}, bf16[512,128]{1,0:T(8,128)(2,1)S(1)}, u32[]{:S(2)}, u32[]{:S(2)}) collective-permute-start(bf16[512,128]{1,0:T(8,128)(2,1)S(1)} %shard_map.86.refs_2_), channel_id=1, source_target_pairs={{0,1},{1,0},{2,3},{3,2},{4,5},{5,4},{6,7},{7,6},{8,9},{9,8},{10,11... | collective-permute-start | bytes 393224 | tf_op jit(solution)/shard_map/ppermute | solution.py:117
  94.1 0.1 pad_add_fusion.place.refs_0_
  94.2 2.2 %shard_map.85.refs_1_ = bf16[4,512,512]{2,1,0:T(8,128)(2,1)S(1)} custom-call(s32[2]{0:T(128)S(1)} %pad_add_fusion.place.refs_0_, bf16[256,4096]{1,0:T(8,128)(2,1)S(1)} %copy-done, bf16[256,4096]{1,0:T(8,128)(2,1)} %collective-permute-done.mate), custom_call_target="tpu_custom_call" | custom-call | tf_op jit(solution)/shard_map/pallas_call | solution.py:99
  96.4 1.8 shard_map.89
  98.2 0.7 copy-done.3
  98.9 4.3 %collective-permute-start.8 = (bf16[512,256]{1,0:T(8,128)(2,1)}, bf16[512,256]{1,0:T(8,128)(2,1)}, u32[]{:S(2)}, u32[]{:S(2)}) collective-permute-start(bf16[512,256]{1,0:T(8,128)(2,1)} %get-tuple-element.18), channel_id=1, source_target_pairs={{0,6},{2,0},{4,2},{6,4},{1,7},{3,1},{5,3},{7,5},{8,14},{10,8},{12,... | collective-permute-start | bytes 786440 | tf_op jit(solution)/shard_map/ppermute | solution.py:18
  103.2 0.0 collective-permute-done.2.refs_3_
  103.2 1.8 shard_map.87
  105.0 0.7 copy-done.4
  105.7 5.6 %collective-permute-start.6 = (bf16[512,256]{1,0:T(8,128)(2,1)}, bf16[512,256]{1,0:T(8,128)(2,1)}, u32[]{:S(2)}, u32[]{:S(2)}) collective-permute-start(bf16[512,256]{1,0:T(8,128)(2,1)} %get-tuple-element.16), channel_id=1, source_target_pairs={{0,2},{2,4},{4,6},{6,0},{1,3},{3,5},{5,7},{7,1},{8,10},{10,12},{12... | collective-permute-start | bytes 786440 | tf_op jit(solution)/shard_map/ppermute | solution.py:18
  111.3 0.0 all-to-all-done.2
  111.3 2.1 %convert_reduce_fusion = f32[32,1024]{1,0:T(8,128)} fusion(bf16[16,32,1024]{2,1,0:T(8,128)(2,1)} %all-to-all-done.2), kind=kLoop, calls=%fused_computation | loop fusion | flops 1015808 | bytes 1179648 | tf_op jit(solution)/shard_map/reduce_sum | solution.py:156
  113.4 4.3 %all-to-all-start.3 = ((f32[4,8,1024]{2,1,0:T(8,128)}), f32[4,8,1024]{2,1,0:T(8,128)S(1)}, u32[]{:S(2)}, u32[]{:S(2)}) async-start(f32[4,8,1024]{2,1,0:T(8,128)} %bitcast.3), calls=%async_computation.3 | async-start | bytes 262144 | tf_op jit(solution)/shard_map/all_to_all | solution.py:157
  117.7 4.3 %collective-permute-start.5 = (bf16[512,256]{1,0:T(8,128)(2,1)}, bf16[512,256]{1,0:T(8,128)(2,1)S(1)}, u32[]{:S(2)}, u32[]{:S(2)}) collective-permute-start(bf16[512,256]{1,0:T(8,128)(2,1)} %copy-done.3), channel_id=1, source_target_pairs={{0,2},{2,4},{4,6},{6,0},{1,3},{3,5},{5,7},{7,1},{8,10},{10,12},{12... | collective-permute-start | bytes 786440 | tf_op jit(solution)/shard_map/ppermute | solution.py:18
  122.0 5.4 %collective-permute-start.4 = (bf16[512,256]{1,0:T(8,128)(2,1)}, bf16[512,256]{1,0:T(8,128)(2,1)}, u32[]{:S(2)}, u32[]{:S(2)}) collective-permute-start(bf16[512,256]{1,0:T(8,128)(2,1)} %copy-done.4), channel_id=1, source_target_pairs={{0,6},{2,0},{4,2},{6,4},{1,7},{3,1},{5,3},{7,5},{8,14},{10,8},{12,... | collective-permute-start | bytes 786440 | tf_op jit(solution)/shard_map/ppermute | solution.py:18
  127.5 3.4 %collective-permute-done.8 = bf16[512,256]{1,0:T(8,128)(2,1)} collective-permute-done((bf16[512,256]{1,0:T(8,128)(2,1)}, bf16[512,256]{1,0:T(8,128)(2,1)}, u32[]{:S(2)}, u32[]{:S(2)}) %collective-permute-start.8) | collective-permute-done | bytes 262176 | tf_op jit(solution)/shard_map/ppermute | solution.py:18
  130.9 1.7 add_convert_fusion
  132.6 4.4 %collective-permute-start.9 = (bf16[512,256]{1,0:T(8,128)(2,1)}, bf16[512,256]{1,0:T(8,128)(2,1)S(1)}, u32[]{:S(2)}, u32[]{:S(2)}) collective-permute-start(bf16[512,256]{1,0:T(8,128)(2,1)} %add_convert_fusion), channel_id=1, source_target_pairs={{0,6},{2,0},{4,2},{6,4},{1,7},{3,1},{5,3},{7,5},{8,14},{10,8},{12,... | collective-permute-start | bytes 786440 | tf_op jit(solution)/shard_map/ppermute | solution.py:18
  137.0 0.9 collective-permute-done.6
  137.9 1.7 add_convert_fusion.1
  139.6 5.4 %collective-permute-start.7 = (bf16[512,256]{1,0:T(8,128)(2,1)}, bf16[512,256]{1,0:T(8,128)(2,1)S(1)}, u32[]{:S(2)}, u32[]{:S(2)}) collective-permute-start(bf16[512,256]{1,0:T(8,128)(2,1)} %add_convert_fusion.1), channel_id=1, source_target_pairs={{0,2},{2,4},{4,6},{6,0},{1,3},{3,5},{5,7},{7,1},{8,10},{10,12},{12... | collective-permute-start | bytes 786440 | tf_op jit(solution)/shard_map/ppermute | solution.py:18
  145.0 26.2 %all-to-all-done.3 = f32[4,8,1024]{2,1,0:T(8,128)S(1)} async-done(((f32[4,8,1024]{2,1,0:T(8,128)}), f32[4,8,1024]{2,1,0:T(8,128)S(1)}, u32[]{:S(2)}, u32[]{:S(2)}) %all-to-all-start.3) | async-done | bytes 131104 | tf_op jit(solution)/shard_map/all_to_all | solution.py:157
  171.2 1.4 multiply_subtract_fusion
  172.6 7.0 %collective-permute-done.5.refs_4_ = bf16[512,256]{1,0:T(8,128)(2,1)S(1)} collective-permute-done((bf16[512,256]{1,0:T(8,128)(2,1)}, bf16[512,256]{1,0:T(8,128)(2,1)S(1)}, u32[]{:S(2)}, u32[]{:S(2)}) %collective-permute-start.5) | collective-permute-done | bytes 262176 | tf_op jit(solution)/shard_map/ppermute | solution.py:18
  179.6 0.0 collective-permute-done.4.refs_3_
  179.6 5.1 %collective-permute-done.7.refs_5_ = bf16[512,256]{1,0:T(8,128)(2,1)S(1)} collective-permute-done((bf16[512,256]{1,0:T(8,128)(2,1)}, bf16[512,256]{1,0:T(8,128)(2,1)S(1)}, u32[]{:S(2)}, u32[]{:S(2)}) %collective-permute-start.7) | collective-permute-done | bytes 262176 | tf_op jit(solution)/shard_map/ppermute | solution.py:18
  184.7 2.2 %shard_map.90 = f32[512,512]{1,0:T(8,128)} custom-call(f32[512,512]{1,0:T(8,128)S(1)} %copy-done.2, f32[512,256]{1,0:T(8,128)S(1)} %get-tuple-element.11.refs_1_, f32[512,256]{1,0:T(8,128)S(1)} %get-tuple-element.12.refs_2_, bf16[512,256]{1,0:T(8,128)(2,1)} %collective-permute-done.4.refs_3_, bf16[512,256]{1,0:T(8,128)(2,1)S(1)} %collective-permute-done.5.refs_4_, ...), custom_call_target="tpu_custom_call" | custom-call | tf_op jit(solution)/shard_map/pallas_call | solution.py:146
  (15 shorter events, 0.1 us)
Async XLA Ops:
  27.3 8.9 %copy-start = (bf16[256,4096]{1,0:T(8,128)(2,1)S(1)}, bf16[256,4096]{1,0:T(8,128)(2,1)}, u32[]{:S(2)}) copy-start(bf16[256,4096]{1,0:T(8,128)(2,1)} %own.5) | copy-start | bytes 6291460
  28.8 23.4 %all-to-all-start = ((bf16[16,8,32,128]{3,2,1,0:T(8,128)(2,1)}), bf16[16,8,32,128]{3,2,1,0:T(8,128)(2,1)S(1)}, u32[]{:S(2)}, u32[]{:S(2)}) async-start(bf16[16,8,32,128]{3,2,1,0:T(8,128)(2,1)} %broadcast_in_dim.15), calls=%async_computation | async-start | bytes 2097152 | tf_op jit(solution)/shard_map/all_to_all | solution.py:90
  36.2 46.7 %collective-permute-start = (bf16[256,4096]{1,0:T(8,128)(2,1)S(1)}, bf16[256,4096]{1,0:T(8,128)(2,1)}, u32[]{:S(2)}, u32[]{:S(2)}) collective-permute-start(bf16[256,4096]{1,0:T(8,128)(2,1)S(1)} %copy-done), channel_id=1, source_target_pairs={{0,1},{1,0},{2,3},{3,2},{4,5},{5,4},{6,7},{7,6},{8,9},{9,8},{10,11... | collective-permute-start | bytes 6291464 | tf_op jit(solution)/shard_map/ppermute | solution.py:95
  52.3 26.4 %copy-start.5 = (bf16[256,512]{1,0:T(8,128)(2,1)S(1)}, bf16[256,512]{1,0:T(8,128)(2,1)}, u32[]{:S(2)}) copy-start(bf16[256,512]{1,0:T(8,128)(2,1)} %param.8) | copy-start | bytes 786436
  72.4 38.9 %all-to-all-start.2 = ((bf16[16,32,1024]{2,1,0:T(8,128)(2,1)}), bf16[16,32,1024]{2,1,0:T(8,128)(2,1)}, u32[]{:S(2)}, u32[]{:S(2)}) async-start(bf16[16,32,1024]{2,1,0:T(8,128)(2,1)} %bitcast.10), calls=%async_computation.2 | async-start | bytes 2097152 | tf_op jit(solution)/shard_map/all_to_all | solution.py:155
  79.4 3.4 %collective-permute-start.1 = (bf16[256,256]{1,0:T(8,128)(2,1)}, bf16[256,256]{1,0:T(8,128)(2,1)S(1)}, u32[]{:S(2)}, u32[]{:S(2)}) collective-permute-start(bf16[256,256]{1,0:T(8,128)(2,1)} %constant_dynamic-slice_fusion.1), channel_id=1, source_target_pairs={{0,1},{1,0},{2,3},{3,2},{4,5},{5,4},{6,7},{7,6},{8,9},{9,8},{10,11... | collective-permute-start | bytes 393224 | tf_op jit(solution)/shard_map/ppermute | solution.py:98
  82.9 1.2 copy-start.1
  86.9 9.5 %collective-permute-start.3 = (bf16[512,128]{1,0:T(8,128)(2,1)S(1)}, bf16[512,128]{1,0:T(8,128)(2,1)S(1)}, u32[]{:S(2)}, u32[]{:S(2)}) collective-permute-start(bf16[512,128]{1,0:T(8,128)(2,1)S(1)} %shard_map.88.refs_2_), channel_id=1, source_target_pairs={{0,1},{1,0},{2,3},{3,2},{4,5},{5,4},{6,7},{7,6},{8,9},{9,8},{10,11... | collective-permute-start | bytes 393224 | tf_op jit(solution)/shard_map/ppermute | solution.py:117
  91.8 11.4 %collective-permute-start.2 = (bf16[512,128]{1,0:T(8,128)(2,1)S(1)}, bf16[512,128]{1,0:T(8,128)(2,1)S(1)}, u32[]{:S(2)}, u32[]{:S(2)}) collective-permute-start(bf16[512,128]{1,0:T(8,128)(2,1)S(1)} %shard_map.86.refs_2_), channel_id=1, source_target_pairs={{0,1},{1,0},{2,3},{3,2},{4,5},{5,4},{6,7},{7,6},{8,9},{9,8},{10,11... | collective-permute-start | bytes 393224 | tf_op jit(solution)/shard_map/ppermute | solution.py:117
  98.2 0.7 copy-start.3
  98.9 32.0 %collective-permute-start.8 = (bf16[512,256]{1,0:T(8,128)(2,1)}, bf16[512,256]{1,0:T(8,128)(2,1)}, u32[]{:S(2)}, u32[]{:S(2)}) collective-permute-start(bf16[512,256]{1,0:T(8,128)(2,1)} %get-tuple-element.18), channel_id=1, source_target_pairs={{0,6},{2,0},{4,2},{6,4},{1,7},{3,1},{5,3},{7,5},{8,14},{10,8},{12,... | collective-permute-start | bytes 786440 | tf_op jit(solution)/shard_map/ppermute | solution.py:18
  105.0 0.7 copy-start.4
  105.7 79.0 %copy-start.2 = (f32[512,512]{1,0:T(8,128)S(1)}, f32[512,512]{1,0:T(8,128)}, u32[]{:S(2)}) copy-start(f32[512,512]{1,0:T(8,128)} %refs_0_.1) | copy-start | bytes 3145732
  105.7 32.2 %collective-permute-start.6 = (bf16[512,256]{1,0:T(8,128)(2,1)}, bf16[512,256]{1,0:T(8,128)(2,1)}, u32[]{:S(2)}, u32[]{:S(2)}) collective-permute-start(bf16[512,256]{1,0:T(8,128)(2,1)} %get-tuple-element.16), channel_id=1, source_target_pairs={{0,2},{2,4},{4,6},{6,0},{1,3},{3,5},{5,7},{7,1},{8,10},{10,12},{12... | collective-permute-start | bytes 786440 | tf_op jit(solution)/shard_map/ppermute | solution.py:18
  113.4 57.7 %all-to-all-start.3 = ((f32[4,8,1024]{2,1,0:T(8,128)}), f32[4,8,1024]{2,1,0:T(8,128)S(1)}, u32[]{:S(2)}, u32[]{:S(2)}) async-start(f32[4,8,1024]{2,1,0:T(8,128)} %bitcast.3), calls=%async_computation.3 | async-start | bytes 262144 | tf_op jit(solution)/shard_map/all_to_all | solution.py:157
  117.7 61.9 %collective-permute-start.5 = (bf16[512,256]{1,0:T(8,128)(2,1)}, bf16[512,256]{1,0:T(8,128)(2,1)S(1)}, u32[]{:S(2)}, u32[]{:S(2)}) collective-permute-start(bf16[512,256]{1,0:T(8,128)(2,1)} %copy-done.3), channel_id=1, source_target_pairs={{0,2},{2,4},{4,6},{6,0},{1,3},{3,5},{5,7},{7,1},{8,10},{10,12},{12... | collective-permute-start | bytes 786440 | tf_op jit(solution)/shard_map/ppermute | solution.py:18
  122.0 57.6 %collective-permute-start.4 = (bf16[512,256]{1,0:T(8,128)(2,1)}, bf16[512,256]{1,0:T(8,128)(2,1)}, u32[]{:S(2)}, u32[]{:S(2)}) collective-permute-start(bf16[512,256]{1,0:T(8,128)(2,1)} %copy-done.4), channel_id=1, source_target_pairs={{0,6},{2,0},{4,2},{6,4},{1,7},{3,1},{5,3},{7,5},{8,14},{10,8},{12,... | collective-permute-start | bytes 786440 | tf_op jit(solution)/shard_map/ppermute | solution.py:18
  132.6 47.0 %collective-permute-start.9 = (bf16[512,256]{1,0:T(8,128)(2,1)}, bf16[512,256]{1,0:T(8,128)(2,1)S(1)}, u32[]{:S(2)}, u32[]{:S(2)}) collective-permute-start(bf16[512,256]{1,0:T(8,128)(2,1)} %add_convert_fusion), channel_id=1, source_target_pairs={{0,6},{2,0},{4,2},{6,4},{1,7},{3,1},{5,3},{7,5},{8,14},{10,8},{12,... | collective-permute-start | bytes 786440 | tf_op jit(solution)/shard_map/ppermute | solution.py:18
  139.6 45.1 %collective-permute-start.7 = (bf16[512,256]{1,0:T(8,128)(2,1)}, bf16[512,256]{1,0:T(8,128)(2,1)S(1)}, u32[]{:S(2)}, u32[]{:S(2)}) collective-permute-start(bf16[512,256]{1,0:T(8,128)(2,1)} %add_convert_fusion.1), channel_id=1, source_target_pairs={{0,2},{2,4},{4,6},{6,0},{1,3},{3,5},{5,7},{7,1},{8,10},{10,12},{12... | collective-permute-start | bytes 786440 | tf_op jit(solution)/shard_map/ppermute | solution.py:18

commit v2 on v1

v2 whole, which is shorter than its diff:
```python
import functools

import jax
import jax.numpy as jnp
from jax import lax
from jax.experimental import pallas as pl
from jax.experimental.pallas import tpu as pltpu
from jax.sharding import Mesh, PartitionSpec as P

INNER_RATE = 4.0
OUTER_RATE = 0.7
MOMENTUM = 0.9

X, Y, ZL, ZH = 4, 4, 4, 4
PARAMS = pltpu.CompilerParams(vmem_limit_bytes=16 * 1024 * 1024)
SWAP = [(0, 1), (1, 0)]


def cost(flops, touched):
    return pl.CostEstimate(flops=flops, bytes_accessed=touched, transcendentals=0)


def shift(a, step):
    return lax.ppermute(a, "zh", [(i, (i + step) % ZH) for i in range(ZH)])


def transpose_kernel(place, own, mate, order, out, both):
    del order
    zh, core = place[0], place[1]
    width = out.shape[1]
    tokens = own.shape[0]
    both[:tokens] = own[...]
    both[tokens:] = mate[...]
    for j in range(ZH):
        block = lax.rem(zh + j, ZH) * 2 + core
        columns = pl.ds(pl.multiple_of(block * width, width), width)
        out[j, :, :tokens] = own[:, columns].T
        out[j, :, tokens:] = mate[:, columns].T


def spread_kernel(place, column, out):
    width = out.shape[3]
    at = place[1] * width
    part = column[:, pl.ds(pl.multiple_of(at, width), width)].reshape(out.shape[1:])
    for i in range(out.shape[0]):
        out[i] = part


def error_kernel(place, both, w, goal_own, goal_mate, out):
    shards, depth = w.shape[1], w.shape[0] * w.shape[2]
    tokens = goal_own.shape[0]
    width = w.shape[3]
    columns = pl.ds(pl.multiple_of(place[1] * width, width), width)
    for i, goal in enumerate((goal_own, goal_mate)):
        at = slice(i * tokens, (i + 1) * tokens)
        keys = jnp.zeros((tokens, width), jnp.float32)
        for f in range(shards):
            keys += jnp.dot(
                both[at, f * depth : (f + 1) * depth],
                w[:, f].reshape(depth, width),
                preferred_element_type=jnp.float32,
            )
        errors = keys - goal[:, columns].astype(jnp.float32)
        out[at, :] = errors.astype(jnp.bfloat16)


def errors_of(place, err_own, err_mate):
    tokens = err_own.shape[0] // 2
    mine = err_own[...]
    other = jnp.concatenate([err_mate[tokens:, :], err_mate[:tokens, :]], axis=0)
    low = jnp.where(place[1] == 0, mine, other)
    high = jnp.where(place[1] == 0, other, mine)
    return jnp.concatenate([low, high], axis=1)


def far_kernel(place, xt, err_own, err_mate, order, up, down):
    del order
    rows = up.shape[0]
    part = jnp.dot(xt[2], errors_of(place, err_own, err_mate), preferred_element_type=jnp.float32)
    up[...] = part[:rows].astype(up.dtype)
    down[...] = part[rows:].astype(down.dtype)


def near_kernel(place, xt, err_own, err_mate, w, part, order, up, down, base, same, *, rate):
    del order
    same[...] = part[...]
    errors = errors_of(place, err_own, err_mate)
    up[...] = jnp.dot(xt[1], errors, preferred_element_type=jnp.float32)
    down[...] = jnp.dot(xt[3], errors, preferred_element_type=jnp.float32)
    base[...] = w[...] - rate * jnp.dot(xt[0], errors, preferred_element_type=jnp.float32)


def pass_kernel(part, far, out, *, half):
    rows = far.shape[0]
    at, rest = half * rows, (1 - half) * rows
    out[:rows] = (part[at : at + rows] + far[...].astype(jnp.float32)).astype(out.dtype)
    out[rows:] = part[rest : rest + rows].astype(out.dtype)


def finish_kernel(base, up, down, out, *, rate):
    rows = up.shape[0] // 2
    for h, (total, plain) in enumerate(((up, down), (down, up))):
        at = slice(h * rows, (h + 1) * rows)
        grad = plain[rows:].astype(jnp.float32) + total[:rows].astype(jnp.float32)
        out[at, :] = base[at, :] - rate * grad


def sort_kernel(place, given, order, keep, one, two, three, held):
    del order
    spread, rows, wide = held.shape
    owned = given.shape[0] // (spread * X * Y)
    for at in range(0, rows, 2 * owned):
        block = given[at * spread : (at + 2 * owned) * spread].astype(jnp.float32)
        block = block.reshape(2, spread, owned, wide)
        for i in range(spread):
            held[i, at : at + 2 * owned] = block[:, i].reshape(2 * owned, wide).astype(held.dtype)
    for j, out in enumerate((keep, one, two, three)):
        out[...] = held[place[2] ^ j]


def reduce_kernel(keep, one, two, three, out):
    out[...] = (keep[...].astype(jnp.float32) + one[...].astype(jnp.float32)) + (
        two[...].astype(jnp.float32) + three[...].astype(jnp.float32)
    )


def on_device(tokens, w_key, targets, frag_outer, frag_local, frag_moment):
    rows, width = tokens.shape
    own_rows, columns = w_key.shape
    half = columns // 2
    spots = X * Y
    core = lax.axis_index("c")
    zh = lax.axis_index("zh")
    spot = lax.axis_index("x") * Y + lax.axis_index("y")
    place = jnp.stack([zh, core, lax.axis_index("zl")]).astype(jnp.int32)
    smem = pl.BlockSpec(memory_space=pltpu.SMEM)
    vmem = pl.BlockSpec(memory_space=pltpu.VMEM)
    anywhere = pl.BlockSpec(memory_space=pl.ANY)

    piece = own_rows // spots
    mine = lax.dynamic_slice_in_dim(w_key, spot * piece, piece, 0).astype(jnp.bfloat16)
    column = lax.all_gather(mine, ("zh", "c"), axis=0, tiled=True)
    copies = pl.pallas_call(
        spread_kernel,
        out_shape=jax.ShapeDtypeStruct((spots, ZH * 2, piece, half), jnp.bfloat16),
        in_specs=[smem, vmem],
        out_specs=vmem,
        compiler_params=PARAMS,
    )(place, column)
    key = lax.all_to_all(copies, ("x", "y"), 0, 0, tiled=True)

    mate = lax.ppermute(tokens, "c", SWAP)
    goal_mate = lax.ppermute(targets, "c", SWAP)
    xt, both = pl.pallas_call(
        transpose_kernel,
        out_shape=(
            jax.ShapeDtypeStruct((ZH, own_rows, 2 * rows), jnp.bfloat16),
            jax.ShapeDtypeStruct((2 * rows, width), jnp.bfloat16),
        ),
        in_specs=[smem, vmem, vmem, anywhere],
        out_specs=(vmem,) * 2,
        compiler_params=PARAMS,
        cost_estimate=cost(0, 16 * rows * width),
    )(place, tokens, mate, column)

    owned, wide = frag_outer.shape
    block = jax.ShapeDtypeStruct((spots * owned, wide), jnp.bfloat16)
    parts = pl.pallas_call(
        sort_kernel,
        out_shape=(block,) * ZL,
        in_specs=[smem, vmem, anywhere],
        out_specs=(vmem,) * ZL,
        scratch_shapes=[pltpu.VMEM((ZL,) + block.shape, block.dtype)],
        compiler_params=PARAMS,
    )(place, frag_local, column)
    parts = [lax.ppermute(p, "zl", [(i, i ^ j) for i in range(ZL)]) if j else p for j, p in enumerate(parts)]
    part = pl.pallas_call(
        reduce_kernel,
        out_shape=jax.ShapeDtypeStruct(block.shape, jnp.float32),
        in_specs=[vmem] * ZL,
        out_specs=vmem,
        compiler_params=PARAMS,
    )(*parts)

    err = pl.pallas_call(
        error_kernel,
        out_shape=jax.ShapeDtypeStruct((2 * rows, half), jnp.bfloat16),
        in_specs=[smem] + [vmem] * 4,
        out_specs=vmem,
        compiler_params=PARAMS,
        cost_estimate=cost(4 * rows * width * half, 8 * rows * width),
    )(place, both, key, targets, goal_mate)
    err_mate = lax.ppermute(err, "c", SWAP)
    rate = INNER_RATE / width
    short = jax.ShapeDtypeStruct((own_rows // 2, columns), jnp.bfloat16)
    long = jax.ShapeDtypeStruct((own_rows, columns), jnp.bfloat16)
    full = jax.ShapeDtypeStruct((own_rows, columns), jnp.float32)
    out_up, out_down = pl.pallas_call(
        far_kernel,
        out_shape=(short,) * 2,
        in_specs=[smem] + [vmem] * 3 + [anywhere],
        out_specs=(vmem,) * 2,
        compiler_params=PARAMS,
    )(place, xt, err, err_mate, part)

    far_up = shift(out_up, 1)
    far_down = shift(out_down, -1)
    up, down, base, part = pl.pallas_call(
        functools.partial(near_kernel, rate=rate),
        out_shape=(full,) * 3 + (jax.ShapeDtypeStruct(part.shape, part.dtype),),
        in_specs=[smem] + [vmem] * 5 + [anywhere],
        out_specs=(vmem,) * 4,
        compiler_params=PARAMS,
    )(place, xt, err, err_mate, w_key, part, out_up)

    def passed(part, far, half):
        return pl.pallas_call(
            functools.partial(pass_kernel, half=half),
            out_shape=long,
            in_specs=[vmem] * 2,
            out_specs=vmem,
            compiler_params=PARAMS,
        )(part, far)

    up = shift(passed(up, far_up, 0), 1)
    down = shift(passed(down, far_down, 1), -1)
    new_key = pl.pallas_call(
        functools.partial(finish_kernel, rate=rate),
        out_shape=full,
        in_specs=[vmem] * 3,
        out_specs=vmem,
        compiler_params=PARAMS,
    )(base, up, down)
    part = lax.all_to_all(part.reshape(spots, owned, wide), ("x", "y"), 0, 0, tiled=True)
    mean = frag_outer - part.sum(0) / (spots * ZL)
    new_moment = MOMENTUM * frag_moment + mean
    new_outer = frag_outer - OUTER_RATE * (mean + MOMENTUM * new_moment)
    return (new_key, new_outer, new_moment)


def solution(mesh):
    grid = Mesh(mesh.devices.reshape(X, Y, ZL, ZH, 2), ("x", "y", "zl", "zh", "c"))
    replica, fsdp = ("x", "y", "zl"), ("zh", "c")
    in_specs = (
        P(replica + fsdp, None),
        P(fsdp, None),
        P(replica + fsdp, None),
        P(fsdp + replica, None),
        P(replica + fsdp, None),
        P(fsdp + replica, None),
    )
    out_specs = (
        P(replica + fsdp, None),
        P(fsdp + replica, None),
        P(fsdp + replica, None),
    )
    return jax.shard_map(
        on_device, mesh=grid, in_specs=in_specs, out_specs=out_specs, check_vma=False
    )
```

time: 188 us -> 170 us (0.904)
  the two profiles are of different devices: /device:TPU:38 before, /device:TPU:65 now
where the time goes in v2:
time: 170 us; the launch traced here: 169 us
  waiting for transfers between devices  68.3 us (40%)
  starting transfers between devices  47.2 us (28%)
  blocking collectives  25 us (15%)
  Pallas kernels  13 us (8%)
  local copies, waits for them, and re-layouts  12.5 us (7%)
  other arithmetic  1.79 us (1%)
    ppermute x4, waiting for transfers between devices, shift(): return lax.ppermute(a, 'zh', [(i, (i + step) % ZH) for i in range(ZH)])  59.4 us
    all_gather x1, blocking collectives, on_device(): column = lax.all_gather(mine, ('zh', 'c'), axis=0, tiled=True)  25 us
    ppermute x4, starting transfers between devices, shift(): return lax.ppermute(a, 'zh', [(i, (i + step) % ZH) for i in range(ZH)])  18.4 us
    unnamed x32, local copies, waits for them, and re-layouts  11.7 us
    ppermute x3, starting transfers between devices, on_device(): lax.ppermute(p, 'zl', [(i, i ^ j) for i in range(ZL)])  8.36 us
    all_to_all x1, waiting for transfers between devices, on_device(): key = lax.all_to_all(copies, ('x', 'y'), 0, 0, tiled=True)  7.97 us
    all_to_all x1, starting transfers between devices, on_device(): key = lax.all_to_all(copies, ('x', 'y'), 0, 0, tiled=True)  6.89 us
    all_to_all x1, starting transfers between devices, on_device(): lax.all_to_all(part.reshape(spots, owned, wide), ('x', 'y'), 0, 0, tiled=...  4.72 us
  transfers between devices with their start and end apart: 12, of which 5 were waited for; matrix products, arithmetic and copies ran while one was open for 2% of the time, Pallas kernels for 6%

profile of v2, /device:TPU:65, one launch (start us, length us, event | category | flops | bytes accessed | tf_op | source)
XLA Modules:
  0.0 168.8 jit_solution(212822911037459979)
XLA Ops:
  0.6 2.6 %collective-permute-start = (bf16[256,4096]{1,0:T(8,128)(2,1)}, bf16[256,4096]{1,0:T(8,128)(2,1)}, u32[]{:S(2)}, u32[]{:S(2)}) collective-permute-start(bf16[256,4096]{1,0:T(8,128)(2,1)} %own.1), channel_id=1, source_target_pairs={{0,1},{1,0},{2,3},{3,2},{4,5},{5,4},{6,7},{7,6},{8,9},{9,8},{10,11... | collective-permute-start | bytes 6291464 | tf_op jit(solution)/shard_map/ppermute | solution.py:152
  3.2 0.9 dynamic-slice_convert_fusion
  4.1 0.1 pad_add_fusion.place
  4.2 25.0 %all_gather.3.order.column = bf16[256,512]{1,0:T(8,128)(2,1)S(1)} all-gather(bf16[32,512]{1,0:T(8,128)(2,1)S(1)} %dynamic-slice_convert_fusion), channel_id=1, replica_groups=mesh['x'=4,'y'=4,'zl'=4,'zh'=4,'c'=2] {'zh','c'}, dimensions={0}, use_global_device_ids=true | all-gather | bytes 294912 | tf_op jit(solution)/shard_map/all_gather | solution.py:142
  29.2 0.7 shard_map.86
  29.9 1.4 copy-done
  31.3 6.9 %all-to-all-start = ((bf16[16,8,32,256]{3,2,1,0:T(8,128)(2,1)}), bf16[16,8,32,256]{3,2,1,0:T(8,128)(2,1)S(1)}, u32[]{:S(2)}, u32[]{:S(2)}) async-start(bf16[16,8,32,256]{3,2,1,0:T(8,128)(2,1)} %copy-done), calls=%async_computation | async-start | bytes 4194304 | tf_op jit(solution)/shard_map/all_to_all | solution.py:150
  38.2 2.4 %collective-permute-start.1 = (bf16[256,512]{1,0:T(8,128)(2,1)}, bf16[256,512]{1,0:T(8,128)(2,1)S(1)}, u32[]{:S(2)}, u32[]{:S(2)}) collective-permute-start(bf16[256,512]{1,0:T(8,128)(2,1)} %goal_own.1), channel_id=1, source_target_pairs={{0,1},{1,0},{2,3},{3,2},{4,5},{5,4},{6,7},{7,6},{8,9},{9,8},{10,11... | collective-permute-start | bytes 786440 | tf_op jit(solution)/shard_map/ppermute | solution.py:153
  40.6 1.6 shard_map.88
  42.2 0.7 copy-done.12
  42.9 2.5 %collective-permute-start.3 = (bf16[128,1024]{1,0:T(8,128)(2,1)}, bf16[128,1024]{1,0:T(8,128)(2,1)S(1)}, u32[]{:S(2)}, u32[]{:S(2)}) collective-permute-start(bf16[128,1024]{1,0:T(8,128)(2,1)} %get-tuple-element.18), channel_id=1, source_target_pairs={{0,8},{8,0},{16,24},{24,16},{1,9},{9,1},{17,25},{25,17},{2,10},{10... | collective-permute-start | bytes 786440 | tf_op jit(solution)/shard_map/ppermute | solution.py:176
  45.4 3.1 %collective-permute-start.4 = (bf16[128,1024]{1,0:T(8,128)(2,1)}, bf16[128,1024]{1,0:T(8,128)(2,1)S(1)}, u32[]{:S(2)}, u32[]{:S(2)}) collective-permute-start(bf16[128,1024]{1,0:T(8,128)(2,1)} %get-tuple-element.19), channel_id=1, source_target_pairs={{0,16},{8,24},{16,0},{24,8},{1,17},{9,25},{17,1},{25,9},{2,18},{10... | collective-permute-start | bytes 786440 | tf_op jit(solution)/shard_map/ppermute | solution.py:176
  48.5 2.7 %collective-permute-start.5 = (bf16[128,1024]{1,0:T(8,128)(2,1)}, bf16[128,1024]{1,0:T(8,128)(2,1)S(1)}, u32[]{:S(2)}, u32[]{:S(2)}) collective-permute-start(bf16[128,1024]{1,0:T(8,128)(2,1)} %get-tuple-element.20), channel_id=1, source_target_pairs={{0,24},{8,16},{16,8},{24,0},{1,25},{9,17},{17,9},{25,1},{2,26},{10... | collective-permute-start | bytes 786440 | tf_op jit(solution)/shard_map/ppermute | solution.py:176
  51.3 0.0 collective-permute-done.mate
  51.3 0.0 copy-start.5
  51.3 1.6 copy-done.5
  52.9 2.5 %shard_map.85 = (bf16[4,512,512]{2,1,0:T(8,128)(2,1)S(1)}, bf16[512,4096]{1,0:T(8,128)(2,1)S(1)}) custom-call(s32[3]{0:T(128)S(1)} %pad_add_fusion.place, bf16[256,4096]{1,0:T(8,128)(2,1)S(1)} %copy-done.5, bf16[256,4096]{1,0:T(8,128)(2,1)} %collective-permute-done.mate, bf16[256,512]{1,0:T(8,128)(2,1)S(1)} %all_gather.3.order.column), custom_call_target="tpu_custom_call" | custom-call | bytes 16777216 | tf_op jit(solution)/shard_map/pallas_call | solution.py:154
  55.4 1.4 copy-done.1
  56.7 2.0 %copy-done.3 = bf16[512,4096]{1,0:T(8,128)(2,1)} copy-done((bf16[512,4096]{1,0:T(8,128)(2,1)}, bf16[512,4096]{1,0:T(8,128)(2,1)S(1)}, u32[]{:S(2)}) %copy-start.3) | copy-done | bytes 4194328
  58.7 0.0 collective-permute-done.1.goal_mate
  58.7 0.7 copy-done.10
  59.4 8.0 %all-to-all-done.w = bf16[16,8,32,256]{3,2,1,0:T(8,128)(2,1)S(1)} async-done(((bf16[16,8,32,256]{3,2,1,0:T(8,128)(2,1)}), bf16[16,8,32,256]{3,2,1,0:T(8,128)(2,1)S(1)}, u32[]{:S(2)}, u32[]{:S(2)}) %all-to-all-start) | async-done | bytes 2097184 | tf_op jit(solution)/shard_map/all_to_all | solution.py:150
  67.4 2.2 %copy-done.4 = bf16[512,4096]{1,0:T(8,128)(2,1)S(1)} copy-done((bf16[512,4096]{1,0:T(8,128)(2,1)S(1)}, bf16[512,4096]{1,0:T(8,128)(2,1)}, u32[]{:S(2)}) %copy-start.4) | copy-done | bytes 4194328
  69.6 0.9 copy-done.11
  70.5 1.8 %shard_map.87.err_own = bf16[512,256]{1,0:T(8,128)(2,1)S(1)} custom-call(s32[3]{0:T(128)S(1)} %pad_add_fusion.place, bf16[512,4096]{1,0:T(8,128)(2,1)S(1)} %copy-done.4, bf16[16,8,32,256]{3,2,1,0:T(8,128)(2,1)S(1)} %all-to-all-done.w, bf16[256,512]{1,0:T(8,128)(2,1)S(1)} %copy-done.9, bf16[256,512]{1,0:T(8,128)(2,1)S(1)} %copy-done.11), custom_call_target="tpu_custom_call" | custom-call | flops 1073741824 | bytes 8388608 | tf_op jit(solution)/shard_map/pallas_call | solution.py:185
  72.3 4.0 %collective-permute-start.2 = (bf16[512,256]{1,0:T(8,128)(2,1)S(1)}, bf16[512,256]{1,0:T(8,128)(2,1)S(1)}, u32[]{:S(2)}, u32[]{:S(2)}) collective-permute-start(bf16[512,256]{1,0:T(8,128)(2,1)S(1)} %shard_map.87.err_own), channel_id=1, source_target_pairs={{0,1},{1,0},{2,3},{3,2},{4,5},{5,4},{6,7},{7,6},{8,9},{9,8},{10,11... | collective-permute-start | bytes 786440 | tf_op jit(solution)/shard_map/ppermute | solution.py:193
  76.3 0.0 collective-permute-done.3.one
  76.3 0.0 collective-permute-done.4.two
  76.3 0.0 collective-permute-done.5.three
  76.3 0.0 copy-start.6
  76.3 0.1 shard_map.89.order.part
  76.5 1.0 collective-permute-done.2.err_mate
  77.4 1.7 %shard_map.90 = (bf16[256,512]{1,0:T(8,128)(2,1)}, bf16[256,512]{1,0:T(8,128)(2,1)}) custom-call(s32[3]{0:T(128)S(1)} %pad_add_fusion.place, bf16[4,512,512]{2,1,0:T(8,128)(2,1)S(1)} %copy-done.2, bf16[512,256]{1,0:T(8,128)(2,1)S(1)} %shard_map.87.err_own, bf16[512,256]{1,0:T(8,128)(2,1)S(1)} %collective-permute-done.2.err_mate, ...), custom_call_target="tpu_custom_call" | custom-call | tf_op jit(solution)/shard_map/pallas_call | solution.py:198
  79.1 3.9 %collective-permute-start.6 = (bf16[256,512]{1,0:T(8,128)(2,1)}, bf16[256,512]{1,0:T(8,128)(2,1)}, u32[]{:S(2)}, u32[]{:S(2)}) collective-permute-start(bf16[256,512]{1,0:T(8,128)(2,1)} %get-tuple-element.21.order), channel_id=1, source_target_pairs={{0,2},{2,4},{4,6},{6,0},{1,3},{3,5},{5,7},{7,1},{8,10},{10,12},{12... | collective-permute-start | bytes 786440 | tf_op jit(solution)/shard_map/ppermute | solution.py:24
  83.0 5.3 %collective-permute-start.8 = (bf16[256,512]{1,0:T(8,128)(2,1)}, bf16[256,512]{1,0:T(8,128)(2,1)S(1)}, u32[]{:S(2)}, u32[]{:S(2)}) collective-permute-start(bf16[256,512]{1,0:T(8,128)(2,1)} %get-tuple-element.25), channel_id=1, source_target_pairs={{0,6},{2,0},{4,2},{6,4},{1,7},{3,1},{5,3},{7,5},{8,14},{10,8},{12,... | collective-permute-start | bytes 786440 | tf_op jit(solution)/shard_map/ppermute | solution.py:24
  88.3 1.6 shard_map.91
  89.9 0.8 copy-done.8
  90.7 4.7 %all-to-all-start.1 = ((f32[16,8,1024]{2,1,0:T(8,128)}), f32[16,8,1024]{2,1,0:T(8,128)}, u32[]{:S(2)}, u32[]{:S(2)}) async-start(f32[16,8,1024]{2,1,0:T(8,128)} %bitcast.4), calls=%async_computation.1 | async-start | bytes 1048576 | tf_op jit(solution)/shard_map/all_to_all | solution.py:234
  95.4 13.3 %collective-permute-done.6.far = bf16[256,512]{1,0:T(8,128)(2,1)} collective-permute-done((bf16[256,512]{1,0:T(8,128)(2,1)}, bf16[256,512]{1,0:T(8,128)(2,1)}, u32[]{:S(2)}, u32[]{:S(2)}) %collective-permute-start.6) | collective-permute-done | bytes 262176 | tf_op jit(solution)/shard_map/ppermute | solution.py:24
  108.8 1.8 %shard_map.92 = bf16[512,512]{1,0:T(8,128)(2,1)} custom-call(f32[512,512]{1,0:T(8,128)S(1)} %get-tuple-element.23.part, bf16[256,512]{1,0:T(8,128)(2,1)} %collective-permute-done.6.far), custom_call_target="tpu_custom_call" | custom-call | tf_op jit(solution)/shard_map/pallas_call | solution.py:217
  110.6 3.8 %collective-permute-start.7 = (bf16[512,512]{1,0:T(8,128)(2,1)}, bf16[512,512]{1,0:T(8,128)(2,1)S(1)}, u32[]{:S(2)}, u32[]{:S(2)}) collective-permute-start(bf16[512,512]{1,0:T(8,128)(2,1)} %shard_map.92), channel_id=1, source_target_pairs={{0,2},{2,4},{4,6},{6,0},{1,3},{3,5},{5,7},{7,1},{8,10},{10,12},{12... | collective-permute-start | bytes 1572872 | tf_op jit(solution)/shard_map/ppermute | solution.py:24
  114.3 0.1 shard_map.93
  114.4 5.4 %collective-permute-start.9 = (bf16[512,512]{1,0:T(8,128)(2,1)S(1)}, bf16[512,512]{1,0:T(8,128)(2,1)S(1)}, u32[]{:S(2)}, u32[]{:S(2)}) collective-permute-start(bf16[512,512]{1,0:T(8,128)(2,1)S(1)} %shard_map.93), channel_id=1, source_target_pairs={{0,6},{2,0},{4,2},{6,4},{1,7},{3,1},{5,3},{7,5},{8,14},{10,8},{12,... | collective-permute-start | bytes 1572872 | tf_op jit(solution)/shard_map/ppermute | solution.py:24
  119.9 1.1 reduce_sum.9
  121.0 0.6 multiply_subtract_fusion
  121.6 25.7 %collective-permute-done.7.up = bf16[512,512]{1,0:T(8,128)(2,1)S(1)} collective-permute-done((bf16[512,512]{1,0:T(8,128)(2,1)}, bf16[512,512]{1,0:T(8,128)(2,1)S(1)}, u32[]{:S(2)}, u32[]{:S(2)}) %collective-permute-start.7) | collective-permute-done | bytes 524320 | tf_op jit(solution)/shard_map/ppermute | solution.py:24
  147.3 20.4 %collective-permute-done.9.down = bf16[512,512]{1,0:T(8,128)(2,1)S(1)} collective-permute-done((bf16[512,512]{1,0:T(8,128)(2,1)S(1)}, bf16[512,512]{1,0:T(8,128)(2,1)S(1)}, u32[]{:S(2)}, u32[]{:S(2)}) %collective-permute-start.9) | collective-permute-done | bytes 524320 | tf_op jit(solution)/shard_map/ppermute | solution.py:24
  167.7 1.1 shard_map.94
  (23 shorter events, 0.0 us)
Async XLA Ops:
  0.6 50.7 %collective-permute-start = (bf16[256,4096]{1,0:T(8,128)(2,1)}, bf16[256,4096]{1,0:T(8,128)(2,1)}, u32[]{:S(2)}, u32[]{:S(2)}) collective-permute-start(bf16[256,4096]{1,0:T(8,128)(2,1)} %own.1), channel_id=1, source_target_pairs={{0,1},{1,0},{2,3},{3,2},{4,5},{5,4},{6,7},{7,6},{8,9},{9,8},{10,11... | collective-permute-start | bytes 6291464 | tf_op jit(solution)/shard_map/ppermute | solution.py:152
  29.9 1.4 copy-start
  31.3 9.3 %copy-start.7 = (bf16[512,1024]{1,0:T(8,128)(2,1)S(1)}, bf16[512,1024]{1,0:T(8,128)(2,1)}, u32[]{:S(2)}) copy-start(bf16[512,1024]{1,0:T(8,128)(2,1)} %given.1) | copy-start | bytes 3145732
  31.3 36.0 %all-to-all-start = ((bf16[16,8,32,256]{3,2,1,0:T(8,128)(2,1)}), bf16[16,8,32,256]{3,2,1,0:T(8,128)(2,1)S(1)}, u32[]{:S(2)}, u32[]{:S(2)}) async-start(bf16[16,8,32,256]{3,2,1,0:T(8,128)(2,1)} %copy-done), calls=%async_computation | async-start | bytes 4194304 | tf_op jit(solution)/shard_map/all_to_all | solution.py:150
  38.2 20.5 %collective-permute-start.1 = (bf16[256,512]{1,0:T(8,128)(2,1)}, bf16[256,512]{1,0:T(8,128)(2,1)S(1)}, u32[]{:S(2)}, u32[]{:S(2)}) collective-permute-start(bf16[256,512]{1,0:T(8,128)(2,1)} %goal_own.1), channel_id=1, source_target_pairs={{0,1},{1,0},{2,3},{3,2},{4,5},{5,4},{6,7},{7,6},{8,9},{9,8},{10,11... | collective-permute-start | bytes 786440 | tf_op jit(solution)/shard_map/ppermute | solution.py:153
  42.2 0.7 copy-start.12
  42.9 33.4 %collective-permute-start.3 = (bf16[128,1024]{1,0:T(8,128)(2,1)}, bf16[128,1024]{1,0:T(8,128)(2,1)S(1)}, u32[]{:S(2)}, u32[]{:S(2)}) collective-permute-start(bf16[128,1024]{1,0:T(8,128)(2,1)} %get-tuple-element.18), channel_id=1, source_target_pairs={{0,8},{8,0},{16,24},{24,16},{1,9},{9,1},{17,25},{25,17},{2,10},{10... | collective-permute-start | bytes 786440 | tf_op jit(solution)/shard_map/ppermute | solution.py:176
  45.4 30.9 %collective-permute-start.4 = (bf16[128,1024]{1,0:T(8,128)(2,1)}, bf16[128,1024]{1,0:T(8,128)(2,1)S(1)}, u32[]{:S(2)}, u32[]{:S(2)}) collective-permute-start(bf16[128,1024]{1,0:T(8,128)(2,1)} %get-tuple-element.19), channel_id=1, source_target_pairs={{0,16},{8,24},{16,0},{24,8},{1,17},{9,25},{17,1},{25,9},{2,18},{10... | collective-permute-start | bytes 786440 | tf_op jit(solution)/shard_map/ppermute | solution.py:176
  48.5 27.8 %collective-permute-start.5 = (bf16[128,1024]{1,0:T(8,128)(2,1)}, bf16[128,1024]{1,0:T(8,128)(2,1)S(1)}, u32[]{:S(2)}, u32[]{:S(2)}) collective-permute-start(bf16[128,1024]{1,0:T(8,128)(2,1)} %get-tuple-element.20), channel_id=1, source_target_pairs={{0,24},{8,16},{16,8},{24,0},{1,25},{9,17},{17,9},{25,1},{2,26},{10... | collective-permute-start | bytes 786440 | tf_op jit(solution)/shard_map/ppermute | solution.py:176
  51.3 1.6 copy-start.5
  52.9 14.5 %copy-start.9 = (bf16[256,512]{1,0:T(8,128)(2,1)S(1)}, bf16[256,512]{1,0:T(8,128)(2,1)}, u32[]{:S(2)}) copy-start(bf16[256,512]{1,0:T(8,128)(2,1)} %goal_own.1) | copy-start | bytes 786436
  55.4 1.4 copy-start.1
  56.7 2.0 %copy-start.3 = (bf16[512,4096]{1,0:T(8,128)(2,1)}, bf16[512,4096]{1,0:T(8,128)(2,1)S(1)}, u32[]{:S(2)}) copy-start(bf16[512,4096]{1,0:T(8,128)(2,1)S(1)} %get-tuple-element.16.both) | copy-start | bytes 12582916
  58.7 0.7 copy-start.10
  67.4 2.2 %copy-start.4 = (bf16[512,4096]{1,0:T(8,128)(2,1)S(1)}, bf16[512,4096]{1,0:T(8,128)(2,1)}, u32[]{:S(2)}) copy-start(bf16[512,4096]{1,0:T(8,128)(2,1)} %copy-done.3) | copy-start | bytes 12582916
  69.6 0.9 copy-start.11
  70.5 5.8 %copy-start.13 = (bf16[128,1024]{1,0:T(8,128)(2,1)S(1)}, bf16[128,1024]{1,0:T(8,128)(2,1)}, u32[]{:S(2)}) copy-start(bf16[128,1024]{1,0:T(8,128)(2,1)} %copy-done.12) | copy-start | bytes 786436
  70.5 6.9 %copy-start.2 = (bf16[4,512,512]{2,1,0:T(8,128)(2,1)S(1)}, bf16[4,512,512]{2,1,0:T(8,128)(2,1)}, u32[]{:S(2)}) copy-start(bf16[4,512,512]{2,1,0:T(8,128)(2,1)} %copy-done.1) | copy-start | bytes 6291460
  72.3 5.1 %collective-permute-start.2 = (bf16[512,256]{1,0:T(8,128)(2,1)S(1)}, bf16[512,256]{1,0:T(8,128)(2,1)S(1)}, u32[]{:S(2)}, u32[]{:S(2)}) collective-permute-start(bf16[512,256]{1,0:T(8,128)(2,1)S(1)} %shard_map.87.err_own), channel_id=1, source_target_pairs={{0,1},{1,0},{2,3},{3,2},{4,5},{5,4},{6,7},{7,6},{8,9},{9,8},{10,11... | collective-permute-start | bytes 786440 | tf_op jit(solution)/shard_map/ppermute | solution.py:193
  76.3 12.0 %copy-start.6 = (f32[512,512]{1,0:T(8,128)S(1)}, f32[512,512]{1,0:T(8,128)}, u32[]{:S(2)}) copy-start(f32[512,512]{1,0:T(8,128)} %w.1) | copy-start | bytes 3145732
  79.1 29.6 %collective-permute-start.6 = (bf16[256,512]{1,0:T(8,128)(2,1)}, bf16[256,512]{1,0:T(8,128)(2,1)}, u32[]{:S(2)}, u32[]{:S(2)}) collective-permute-start(bf16[256,512]{1,0:T(8,128)(2,1)} %get-tuple-element.21.order), channel_id=1, source_target_pairs={{0,2},{2,4},{4,6},{6,0},{1,3},{3,5},{5,7},{7,1},{8,10},{10,12},{12... | collective-permute-start | bytes 786440 | tf_op jit(solution)/shard_map/ppermute | solution.py:24
  83.0 31.4 %collective-permute-start.8 = (bf16[256,512]{1,0:T(8,128)(2,1)}, bf16[256,512]{1,0:T(8,128)(2,1)S(1)}, u32[]{:S(2)}, u32[]{:S(2)}) collective-permute-start(bf16[256,512]{1,0:T(8,128)(2,1)} %get-tuple-element.25), channel_id=1, source_target_pairs={{0,6},{2,0},{4,2},{6,4},{1,7},{3,1},{5,3},{7,5},{8,14},{10,8},{12,... | collective-permute-start | bytes 786440 | tf_op jit(solution)/shard_map/ppermute | solution.py:24
  89.9 0.8 copy-start.8
  90.7 29.1 %all-to-all-start.1 = ((f32[16,8,1024]{2,1,0:T(8,128)}), f32[16,8,1024]{2,1,0:T(8,128)}, u32[]{:S(2)}, u32[]{:S(2)}) async-start(f32[16,8,1024]{2,1,0:T(8,128)} %bitcast.4), calls=%async_computation.1 | async-start | bytes 1048576 | tf_op jit(solution)/shard_map/all_to_all | solution.py:234
  108.7 12.2 %copy-start.14 = (f32[8,1024]{1,0:T(8,128)S(1)}, f32[8,1024]{1,0:T(8,128)}, u32[]{:S(2)}) copy-start(f32[8,1024]{1,0:T(8,128)} %param.9) | copy-start | bytes 98308
  108.8 12.2 %copy-start.15 = (f32[8,1024]{1,0:T(8,128)S(1)}, f32[8,1024]{1,0:T(8,128)}, u32[]{:S(2)}) copy-start(f32[8,1024]{1,0:T(8,128)} %param.11) | copy-start | bytes 98308
  110.6 36.7 %collective-permute-start.7 = (bf16[512,512]{1,0:T(8,128)(2,1)}, bf16[512,512]{1,0:T(8,128)(2,1)S(1)}, u32[]{:S(2)}, u32[]{:S(2)}) collective-permute-start(bf16[512,512]{1,0:T(8,128)(2,1)} %shard_map.92), channel_id=1, source_target_pairs={{0,2},{2,4},{4,6},{6,0},{1,3},{3,5},{5,7},{7,1},{8,10},{10,12},{12... | collective-permute-start | bytes 1572872 | tf_op jit(solution)/shard_map/ppermute | solution.py:24
  114.4 53.3 %collective-permute-start.9 = (bf16[512,512]{1,0:T(8,128)(2,1)S(1)}, bf16[512,512]{1,0:T(8,128)(2,1)S(1)}, u32[]{:S(2)}, u32[]{:S(2)}) collective-permute-start(bf16[512,512]{1,0:T(8,128)(2,1)S(1)} %shard_map.93), channel_id=1, source_target_pairs={{0,6},{2,0},{4,2},{6,4},{1,7},{3,1},{5,3},{7,5},{8,14},{10,8},{12,... | collective-permute-start | bytes 1572872 | tf_op jit(solution)/shard_map/ppermute | solution.py:24

commit v3 on v2

--- a/solution.py
+++ b/solution.py
@@ -20,20 +20,38 @@
     return pl.CostEstimate(flops=flops, bytes_accessed=touched, transcendentals=0)
 
 
-def shift(a, step):
-    return lax.ppermute(a, "zh", [(i, (i + step) % ZH) for i in range(ZH)])
+def round_z(a, cross):
+    pairs = []
+    for zh in range(ZH):
+        for core in range(2):
+            there = (zh + 1 - 2 * core) % ZH
+            pairs.append((zh * 2 + core, there * 2 + (core ^ cross)))
+    return lax.ppermute(a, ("zh", "c"), pairs)
 
 
 def transpose_kernel(place, own, mate, order, out, both):
     del order
     zh, core = place[0], place[1]
+    other = 1 - core
     width = out.shape[1]
     tokens = own.shape[0]
     both[:tokens] = own[...]
     both[tokens:] = mate[...]
-    for j in range(ZH):
-        block = lax.rem(zh + j, ZH) * 2 + core
-        columns = pl.ds(pl.multiple_of(block * width, width), width)
+    far = lax.rem(zh + 2, ZH)
+    near = lax.rem(zh + 1 + 2 * core, ZH)
+    for j, (chip, block, half) in enumerate(
+        (
+            (far, core, core),
+            (far, other, core),
+            (near, core, core),
+            (near, core, other),
+            (near, other, core),
+            (near, other, other),
+            (zh, core, 0),
+            (zh, core, 1),
+        )
+    ):
+        columns = pl.ds(pl.multiple_of(((chip * 2 + block) * 2 + half) * width, width), width)
         out[j, :, :tokens] = own[:, columns].T
         out[j, :, tokens:] = mate[:, columns].T
 
@@ -73,35 +91,38 @@
     return jnp.concatenate([low, high], axis=1)
 
 
-def far_kernel(place, xt, err_own, err_mate, order, up, down):
-    del order
-    rows = up.shape[0]
-    part = jnp.dot(xt[2], errors_of(place, err_own, err_mate), preferred_element_type=jnp.float32)
-    up[...] = part[:rows].astype(up.dtype)
-    down[...] = part[rows:].astype(down.dtype)
-
-
-def near_kernel(place, xt, err_own, err_mate, w, part, order, up, down, base, same, *, rate):
+def far_kernel(place, xt, err_own, err_mate, order, *outs):
+    del order
+    errors = errors_of(place, err_own, err_mate)
+    for i, out in enumerate(outs):
+        out[...] = jnp.dot(xt[i], errors, preferred_element_type=jnp.float32).astype(out.dtype)
+
+
+def near_kernel(place, xt, err_own, err_mate, w, part, order, via_a, near_a, via_b, near_b, base, same, *, rate):
     del order
     same[...] = part[...]
     errors = errors_of(place, err_own, err_mate)
-    up[...] = jnp.dot(xt[1], errors, preferred_element_type=jnp.float32)
-    down[...] = jnp.dot(xt[3], errors, preferred_element_type=jnp.float32)
-    base[...] = w[...] - rate * jnp.dot(xt[0], errors, preferred_element_type=jnp.float32)
-
-
-def pass_kernel(part, far, out, *, half):
+    for i, out in enumerate((via_a, near_a, via_b, near_b)):
+        out[...] = jnp.dot(xt[2 + i], errors, preferred_element_type=jnp.float32).astype(out.dtype)
+    rows = xt.shape[1]
+    for h in range(2):
+        at = slice(h * rows, (h + 1) * rows)
+        base[at, :] = w[at, :] - rate * jnp.dot(xt[6 + h], errors, preferred_element_type=jnp.float32)
+
+
+def pass_kernel(via, near, far, out):
     rows = far.shape[0]
-    at, rest = half * rows, (1 - half) * rows
-    out[:rows] = (part[at : at + rows] + far[...].astype(jnp.float32)).astype(out.dtype)
-    out[rows:] = part[rest : rest + rows].astype(out.dtype)
-
-
-def finish_kernel(base, up, down, out, *, rate):
-    rows = up.shape[0] // 2
-    for h, (total, plain) in enumerate(((up, down), (down, up))):
+    out[:rows] = (via[...] + far[...].astype(jnp.float32)).astype(out.dtype)
+    out[rows:] = near[...]
+
+
+def finish_kernel(place, base, straight, crossed, out, *, rate):
+    rows = base.shape[0] // 2
+    for h in range(2):
+        first = place[1] ^ h
         at = slice(h * rows, (h + 1) * rows)
-        grad = plain[rows:].astype(jnp.float32) + total[:rows].astype(jnp.float32)
+        grad = straight[pl.ds(pl.multiple_of(first * rows, rows), rows), :].astype(jnp.float32)
+        grad += crossed[pl.ds(pl.multiple_of((1 - first) * rows, rows), rows), :].astype(jnp.float32)
         out[at, :] = base[at, :] - rate * grad
 
 
@@ -154,7 +175,7 @@
     xt, both = pl.pallas_call(
         transpose_kernel,
         out_shape=(
-            jax.ShapeDtypeStruct((ZH, own_rows, 2 * rows), jnp.bfloat16),
+            jax.ShapeDtypeStruct((2 * ZH, own_rows // 2, 2 * rows), jnp.bfloat16),
             jax.ShapeDtypeStruct((2 * rows, width), jnp.bfloat16),
         ),
         in_specs=[smem, vmem, vmem, anywhere],
@@ -193,9 +214,10 @@
     err_mate = lax.ppermute(err, "c", SWAP)
     rate = INNER_RATE / width
     short = jax.ShapeDtypeStruct((own_rows // 2, columns), jnp.bfloat16)
+    middle = jax.ShapeDtypeStruct((own_rows // 2, columns), jnp.float32)
     long = jax.ShapeDtypeStruct((own_rows, columns), jnp.bfloat16)
     full = jax.ShapeDtypeStruct((own_rows, columns), jnp.float32)
-    out_up, out_down = pl.pallas_call(
+    out_a, out_b = pl.pallas_call(
         far_kernel,
         out_shape=(short,) * 2,
         in_specs=[smem] + [vmem] * 3 + [anywhere],
@@ -203,34 +225,35 @@
         compiler_params=PARAMS,
     )(place, xt, err, err_mate, part)
 
-    far_up = shift(out_up, 1)
-    far_down = shift(out_down, -1)
-    up, down, base, part = pl.pallas_call(
+    far_a = round_z(out_a, 0)
+    far_b = round_z(out_b, 0)
+    via_a, near_a, via_b, near_b, base, part = pl.pallas_call(
         functools.partial(near_kernel, rate=rate),
-        out_shape=(full,) * 3 + (jax.ShapeDtypeStruct(part.shape, part.dtype),),
+        out_shape=(middle, short, middle, short, full, jax.ShapeDtypeStruct(part.shape, part.dtype)),
         in_specs=[smem] + [vmem] * 5 + [anywhere],
-        out_specs=(vmem,) * 4,
-        compiler_params=PARAMS,
-    )(place, xt, err, err_mate, w_key, part, out_up)
-
-    def passed(part, far, half):
+        out_specs=(vmem,) * 6,
+        compiler_params=PARAMS,
+    )(place, xt, err, err_mate, w_key, part, out_a)
+
+    def passed(via, near, far):
         return pl.pallas_call(
-            functools.partial(pass_kernel, half=half),
+            pass_kernel,
             out_shape=long,
-            in_specs=[vmem] * 2,
+            in_specs=[vmem] * 3,
             out_specs=vmem,
             compiler_params=PARAMS,
-        )(part, far)
-
-    up = shift(passed(up, far_up, 0), 1)
-    down = shift(passed(down, far_down, 1), -1)
+        )(via, near, far)
+
+    straight = round_z(passed(via_a, near_a, far_a), 0)
+    crossed = round_z(passed(via_b, near_b, far_b), 1)
     new_key = pl.pallas_call(
         functools.partial(finish_kernel, rate=rate),
         out_shape=full,
-        in_specs=[vmem] * 3,
-        out_specs=vmem,
-        compiler_params=PARAMS,
-    )(base, up, down)
+        in_specs=[smem] + [vmem] * 3,
+        out_specs=vmem,
+        compiler_params=PARAMS,
+    )(place, base, straight, crossed)
+
     part = lax.all_to_all(part.reshape(spots, owned, wide), ("x", "y"), 0, 0, tiled=True)
     mean = frag_outer - part.sum(0) / (spots * ZL)
     new_moment = MOMENTUM * frag_moment + mean

time: 170 us -> 161 us (0.947)
  the two profiles are of different devices: /device:TPU:65 before, /device:TPU:1 now
where the time goes in v3:
time: 161 us; the launch traced here: 160 us
  waiting for transfers between devices  59.2 us (37%)
  starting transfers between devices  51.2 us (32%)
  blocking collectives  21.4 us (13%)
  local copies, waits for them, and re-layouts  13.4 us (8%)
  Pallas kernels  12.5 us (8%)
  other arithmetic  1.79 us (1%)
    ppermute x4, waiting for transfers between devices, round_z(): return lax.ppermute(a, ('zh', 'c'), pairs)  51.2 us
    all_gather x1, blocking collectives, on_device(): column = lax.all_gather(mine, ('zh', 'c'), axis=0, tiled=True)  21.4 us
    ppermute x4, starting transfers between devices, round_z(): return lax.ppermute(a, ('zh', 'c'), pairs)  15.2 us
    unnamed x34, local copies, waits for them, and re-layouts  12.6 us
    ppermute x3, starting transfers between devices, on_device(): lax.ppermute(p, 'zl', [(i, i ^ j) for i in range(ZL)])  9.26 us
    ppermute x1, starting transfers between devices, on_device(): mate = lax.ppermute(tokens, 'c', SWAP)  8.79 us
    all_to_all x1, waiting for transfers between devices, on_device(): key = lax.all_to_all(copies, ('x', 'y'), 0, 0, tiled=True)  7.08 us
    all_to_all x1, starting transfers between devices, on_device(): key = lax.all_to_all(copies, ('x', 'y'), 0, 0, tiled=True)  6.89 us
  transfers between devices with their start and end apart: 12, of which 6 were waited for; matrix products, arithmetic and copies ran while one was open for 2% of the time, Pallas kernels for 6%

profile of v3, /device:TPU:1, one launch (start us, length us, event | category | flops | bytes accessed | tf_op | source)
XLA Modules:
  0.0 160.4 jit_solution(12536732768577995085)
XLA Ops:
  0.6 8.8 %collective-permute-start = (bf16[256,4096]{1,0:T(8,128)(2,1)}, bf16[256,4096]{1,0:T(8,128)(2,1)}, u32[]{:S(2)}, u32[]{:S(2)}) collective-permute-start(bf16[256,4096]{1,0:T(8,128)(2,1)} %own.1), channel_id=1, source_target_pairs={{0,1},{1,0},{2,3},{3,2},{4,5},{5,4},{6,7},{7,6},{8,9},{9,8},{10,11... | collective-permute-start | bytes 6291464 | tf_op jit(solution)/shard_map/ppermute | solution.py:173
  9.4 0.9 dynamic-slice_convert_fusion
  10.3 0.1 pad_add_fusion.place
  10.4 21.4 %all_gather.3.order.column = bf16[256,512]{1,0:T(8,128)(2,1)S(1)} all-gather(bf16[32,512]{1,0:T(8,128)(2,1)S(1)} %dynamic-slice_convert_fusion), channel_id=1, replica_groups=mesh['x'=4,'y'=4,'zl'=4,'zh'=4,'c'=2] {'zh','c'}, dimensions={0}, use_global_device_ids=true | all-gather | bytes 294912 | tf_op jit(solution)/shard_map/all_gather | solution.py:163
  31.7 0.7 shard_map.86
  32.5 1.4 copy-done
  33.9 6.9 %all-to-all-start = ((bf16[16,8,32,256]{3,2,1,0:T(8,128)(2,1)}), bf16[16,8,32,256]{3,2,1,0:T(8,128)(2,1)S(1)}, u32[]{:S(2)}, u32[]{:S(2)}) async-start(bf16[16,8,32,256]{3,2,1,0:T(8,128)(2,1)} %copy-done), calls=%async_computation | async-start | bytes 4194304 | tf_op jit(solution)/shard_map/all_to_all | solution.py:171
  40.8 2.4 %collective-permute-start.1 = (bf16[256,512]{1,0:T(8,128)(2,1)}, bf16[256,512]{1,0:T(8,128)(2,1)S(1)}, u32[]{:S(2)}, u32[]{:S(2)}) collective-permute-start(bf16[256,512]{1,0:T(8,128)(2,1)} %goal_own.1), channel_id=1, source_target_pairs={{0,1},{1,0},{2,3},{3,2},{4,5},{5,4},{6,7},{7,6},{8,9},{9,8},{10,11... | collective-permute-start | bytes 786440 | tf_op jit(solution)/shard_map/ppermute | solution.py:174
  43.1 1.6 shard_map.88
  44.7 0.7 copy-done.11
  45.4 2.6 %collective-permute-start.3 = (bf16[128,1024]{1,0:T(8,128)(2,1)}, bf16[128,1024]{1,0:T(8,128)(2,1)S(1)}, u32[]{:S(2)}, u32[]{:S(2)}) collective-permute-start(bf16[128,1024]{1,0:T(8,128)(2,1)} %get-tuple-element.20), channel_id=1, source_target_pairs={{0,8},{8,0},{16,24},{24,16},{1,9},{9,1},{17,25},{25,17},{2,10},{10... | collective-permute-start | bytes 786440 | tf_op jit(solution)/shard_map/ppermute | solution.py:197
  48.1 3.1 %collective-permute-start.4 = (bf16[128,1024]{1,0:T(8,128)(2,1)}, bf16[128,1024]{1,0:T(8,128)(2,1)S(1)}, u32[]{:S(2)}, u32[]{:S(2)}) collective-permute-start(bf16[128,1024]{1,0:T(8,128)(2,1)} %get-tuple-element.21), channel_id=1, source_target_pairs={{0,16},{8,24},{16,0},{24,8},{1,17},{9,25},{17,1},{25,9},{2,18},{10... | collective-permute-start | bytes 786440 | tf_op jit(solution)/shard_map/ppermute | solution.py:197
  51.2 3.5 %collective-permute-start.5 = (bf16[128,1024]{1,0:T(8,128)(2,1)}, bf16[128,1024]{1,0:T(8,128)(2,1)S(1)}, u32[]{:S(2)}, u32[]{:S(2)}) collective-permute-start(bf16[128,1024]{1,0:T(8,128)(2,1)} %get-tuple-element.22), channel_id=1, source_target_pairs={{0,24},{8,16},{16,8},{24,0},{1,25},{9,17},{17,9},{25,1},{2,26},{10... | collective-permute-start | bytes 786440 | tf_op jit(solution)/shard_map/ppermute | solution.py:197
  54.7 0.0 collective-permute-done.mate
  54.7 0.0 copy-start.5
  54.7 1.6 copy-done.5
  56.3 2.5 %shard_map.85 = (bf16[8,256,512]{2,1,0:T(8,128)(2,1)S(1)}, bf16[512,4096]{1,0:T(8,128)(2,1)S(1)}) custom-call(s32[3]{0:T(128)S(1)} %pad_add_fusion.place, bf16[256,4096]{1,0:T(8,128)(2,1)S(1)} %copy-done.5, bf16[256,4096]{1,0:T(8,128)(2,1)} %collective-permute-done.mate, bf16[256,512]{1,0:T(8,128)(2,1)S(1)} %all_gather.3.order.column), custom_call_target="tpu_custom_call" | custom-call | bytes 16777216 | tf_op jit(solution)/shard_map/pallas_call | solution.py:175
  58.8 1.4 copy-done.1
  60.2 2.0 %copy-done.3 = bf16[512,4096]{1,0:T(8,128)(2,1)} copy-done((bf16[512,4096]{1,0:T(8,128)(2,1)}, bf16[512,4096]{1,0:T(8,128)(2,1)S(1)}, u32[]{:S(2)}) %copy-start.3) | copy-done | bytes 4194328
  62.1 0.7 copy-done.9
  62.8 7.1 %all-to-all-done.w = bf16[16,8,32,256]{3,2,1,0:T(8,128)(2,1)S(1)} async-done(((bf16[16,8,32,256]{3,2,1,0:T(8,128)(2,1)}), bf16[16,8,32,256]{3,2,1,0:T(8,128)(2,1)S(1)}, u32[]{:S(2)}, u32[]{:S(2)}) %all-to-all-start) | async-done | bytes 2097184 | tf_op jit(solution)/shard_map/all_to_all | solution.py:171
  69.9 2.2 %copy-done.4 = bf16[512,4096]{1,0:T(8,128)(2,1)S(1)} copy-done((bf16[512,4096]{1,0:T(8,128)(2,1)S(1)}, bf16[512,4096]{1,0:T(8,128)(2,1)}, u32[]{:S(2)}) %copy-start.4) | copy-done | bytes 4194328
  72.1 0.9 copy-done.10
  73.1 1.8 %shard_map.87.err_own = bf16[512,256]{1,0:T(8,128)(2,1)S(1)} custom-call(s32[3]{0:T(128)S(1)} %pad_add_fusion.place, bf16[512,4096]{1,0:T(8,128)(2,1)S(1)} %copy-done.4, bf16[16,8,32,256]{3,2,1,0:T(8,128)(2,1)S(1)} %all-to-all-done.w, bf16[256,512]{1,0:T(8,128)(2,1)S(1)} %copy-done.8, bf16[256,512]{1,0:T(8,128)(2,1)S(1)} %copy-done.10), custom_call_target="tpu_custom_call" | custom-call | flops 1073741824 | bytes 8388608 | tf_op jit(solution)/shard_map/pallas_call | solution.py:206
  74.8 4.0 %collective-permute-start.2 = (bf16[512,256]{1,0:T(8,128)(2,1)S(1)}, bf16[512,256]{1,0:T(8,128)(2,1)S(1)}, u32[]{:S(2)}, u32[]{:S(2)}) collective-permute-start(bf16[512,256]{1,0:T(8,128)(2,1)S(1)} %shard_map.87.err_own), channel_id=1, source_target_pairs={{0,1},{1,0},{2,3},{3,2},{4,5},{5,4},{6,7},{7,6},{8,9},{9,8},{10,11... | collective-permute-start | bytes 786440 | tf_op jit(solution)/shard_map/ppermute | solution.py:214
  78.9 0.0 copy-start.6
  78.9 0.1 shard_map.89.order.part
  79.0 1.0 collective-permute-done.2.err_mate
  80.0 1.7 %shard_map.90 = (bf16[256,512]{1,0:T(8,128)(2,1)S(1)}, bf16[256,512]{1,0:T(8,128)(2,1)}) custom-call(s32[3]{0:T(128)S(1)} %pad_add_fusion.place, bf16[8,256,512]{2,1,0:T(8,128)(2,1)S(1)} %copy-done.2, bf16[512,256]{1,0:T(8,128)(2,1)S(1)} %shard_map.87.err_own, bf16[512,256]{1,0:T(8,128)(2,1)S(1)} %collective-permute-done.2.err_mate, ...), custom_call_target="tpu_custom_call" | custom-call | tf_op jit(solution)/shard_map/pallas_call | solution.py:220
  81.7 4.1 %collective-permute-start.6 = (bf16[256,512]{1,0:T(8,128)(2,1)S(1)}, bf16[256,512]{1,0:T(8,128)(2,1)S(1)}, u32[]{:S(2)}, u32[]{:S(2)}) collective-permute-start(bf16[256,512]{1,0:T(8,128)(2,1)S(1)} %get-tuple-element.23.order), channel_id=1, source_target_pairs={{0,2},{1,7},{2,4},{3,1},{4,6},{5,3},{6,0},{7,5},{8,10},{9,15},{10,... | collective-permute-start | bytes 786440 | tf_op jit(solution)/shard_map/ppermute | solution.py:29
  85.8 5.1 %collective-permute-start.8 = (bf16[256,512]{1,0:T(8,128)(2,1)}, bf16[256,512]{1,0:T(8,128)(2,1)S(1)}, u32[]{:S(2)}, u32[]{:S(2)}) collective-permute-start(bf16[256,512]{1,0:T(8,128)(2,1)} %get-tuple-element.29), channel_id=1, source_target_pairs={{0,2},{1,7},{2,4},{3,1},{4,6},{5,3},{6,0},{7,5},{8,10},{9,15},{10,... | collective-permute-start | bytes 786440 | tf_op jit(solution)/shard_map/ppermute | solution.py:29
  90.9 2.3 %shard_map.91 = (f32[256,512]{1,0:T(8,128)S(1)}, bf16[256,512]{1,0:T(8,128)(2,1)S(1)}, f32[256,512]{1,0:T(8,128)S(1)}, bf16[256,512]{1,0:T(8,128)(2,1)S(1)}, f32...) custom-call(s32[3]{0:T(128)S(1)} %pad_add_fusion.place, bf16[8,256,512]{2,1,0:T(8,128)(2,1)S(1)} %copy-done.2, ...), custom_call_target="tpu_custom_call" | custom-call | tf_op jit(solution)/shard_map/pallas_call | solution.py:230
  93.2 0.7 copy-done.13
  93.9 4.7 %all-to-all-start.1 = ((f32[16,8,1024]{2,1,0:T(8,128)}), f32[16,8,1024]{2,1,0:T(8,128)}, u32[]{:S(2)}, u32[]{:S(2)}) async-start(f32[16,8,1024]{2,1,0:T(8,128)} %bitcast.3), calls=%async_computation.1 | async-start | bytes 1048576 | tf_op jit(solution)/shard_map/all_to_all | solution.py:257
  98.6 0.0 copy-start.15
  98.6 0.0 copy-start.16
  98.6 7.1 %collective-permute-done.6.far = bf16[256,512]{1,0:T(8,128)(2,1)S(1)} collective-permute-done((bf16[256,512]{1,0:T(8,128)(2,1)S(1)}, bf16[256,512]{1,0:T(8,128)(2,1)S(1)}, u32[]{:S(2)}, u32[]{:S(2)}) %collective-permute-start.6) | collective-permute-done | bytes 262176 | tf_op jit(solution)/shard_map/ppermute | solution.py:29
  105.7 0.1 shard_map.92
  105.8 4.1 %collective-permute-start.7 = (bf16[512,512]{1,0:T(8,128)(2,1)S(1)}, bf16[512,512]{1,0:T(8,128)(2,1)S(1)}, u32[]{:S(2)}, u32[]{:S(2)}) collective-permute-start(bf16[512,512]{1,0:T(8,128)(2,1)S(1)} %shard_map.92), channel_id=1, source_target_pairs={{0,2},{1,7},{2,4},{3,1},{4,6},{5,3},{6,0},{7,5},{8,10},{9,15},{10,... | collective-permute-start | bytes 1572872 | tf_op jit(solution)/shard_map/ppermute | solution.py:29
  109.9 8.7 %collective-permute-done.8.far = bf16[256,512]{1,0:T(8,128)(2,1)S(1)} collective-permute-done((bf16[256,512]{1,0:T(8,128)(2,1)}, bf16[256,512]{1,0:T(8,128)(2,1)S(1)}, u32[]{:S(2)}, u32[]{:S(2)}) %collective-permute-start.8) | collective-permute-done | bytes 262176 | tf_op jit(solution)/shard_map/ppermute | solution.py:29
  118.5 0.9 copy-done.14
  119.5 0.1 shard_map.93
  119.5 1.9 %collective-permute-start.9 = (bf16[512,512]{1,0:T(8,128)(2,1)S(1)}, bf16[512,512]{1,0:T(8,128)(2,1)S(1)}, u32[]{:S(2)}, u32[]{:S(2)}) collective-permute-start(bf16[512,512]{1,0:T(8,128)(2,1)S(1)} %shard_map.93), channel_id=1, source_target_pairs={{0,3},{1,6},{2,5},{3,0},{4,7},{5,2},{6,1},{7,4},{8,11},{9,14},{10,... | collective-permute-start | bytes 1572872 | tf_op jit(solution)/shard_map/ppermute | solution.py:29
  121.5 1.1 reduce_sum.9
  122.6 0.6 multiply_subtract_fusion
  123.2 2.0 %collective-permute-done.7.straight = bf16[512,512]{1,0:T(8,128)(2,1)S(1)} collective-permute-done((bf16[512,512]{1,0:T(8,128)(2,1)S(1)}, bf16[512,512]{1,0:T(8,128)(2,1)S(1)}, u32[]{:S(2)}, u32[]{:S(2)}) %collective-permute-start.7) | collective-permute-done | bytes 524320 | tf_op jit(solution)/shard_map/ppermute | solution.py:29
  125.2 33.4 %collective-permute-done.9.crossed = bf16[512,512]{1,0:T(8,128)(2,1)S(1)} collective-permute-done((bf16[512,512]{1,0:T(8,128)(2,1)S(1)}, bf16[512,512]{1,0:T(8,128)(2,1)S(1)}, u32[]{:S(2)}, u32[]{:S(2)}) %collective-permute-start.9) | collective-permute-done | bytes 524320 | tf_op jit(solution)/shard_map/ppermute | solution.py:29
  158.7 1.7 %shard_map.94 = f32[512,512]{1,0:T(8,128)} custom-call(s32[3]{0:T(128)S(1)} %pad_add_fusion.place, f32[512,512]{1,0:T(8,128)S(1)} %get-tuple-element.24.base, bf16[512,512]{1,0:T(8,128)(2,1)S(1)} %collective-permute-done.7.straight, bf16[512,512]{1,0:T(8,128)(2,1)S(1)} %collective-permute-done.9.crossed), custom_call_target="tpu_custom_call" | custom-call | tf_op jit(solution)/shard_map/pallas_call | solution.py:249
  (25 shorter events, 0.0 us)
Async XLA Ops:
  0.6 54.1 %collective-permute-start = (bf16[256,4096]{1,0:T(8,128)(2,1)}, bf16[256,4096]{1,0:T(8,128)(2,1)}, u32[]{:S(2)}, u32[]{:S(2)}) collective-permute-start(bf16[256,4096]{1,0:T(8,128)(2,1)} %own.1), channel_id=1, source_target_pairs={{0,1},{1,0},{2,3},{3,2},{4,5},{5,4},{6,7},{7,6},{8,9},{9,8},{10,11... | collective-permute-start | bytes 6291464 | tf_op jit(solution)/shard_map/ppermute | solution.py:173
  32.5 1.4 copy-start
  33.9 9.3 %copy-start.7 = (bf16[512,1024]{1,0:T(8,128)(2,1)S(1)}, bf16[512,1024]{1,0:T(8,128)(2,1)}, u32[]{:S(2)}) copy-start(bf16[512,1024]{1,0:T(8,128)(2,1)} %given.1) | copy-start | bytes 3145732
  33.9 36.0 %all-to-all-start = ((bf16[16,8,32,256]{3,2,1,0:T(8,128)(2,1)}), bf16[16,8,32,256]{3,2,1,0:T(8,128)(2,1)S(1)}, u32[]{:S(2)}, u32[]{:S(2)}) async-start(bf16[16,8,32,256]{3,2,1,0:T(8,128)(2,1)} %copy-done), calls=%async_computation | async-start | bytes 4194304 | tf_op jit(solution)/shard_map/all_to_all | solution.py:171
  40.8 21.4 %collective-permute-start.1 = (bf16[256,512]{1,0:T(8,128)(2,1)}, bf16[256,512]{1,0:T(8,128)(2,1)S(1)}, u32[]{:S(2)}, u32[]{:S(2)}) collective-permute-start(bf16[256,512]{1,0:T(8,128)(2,1)} %goal_own.1), channel_id=1, source_target_pairs={{0,1},{1,0},{2,3},{3,2},{4,5},{5,4},{6,7},{7,6},{8,9},{9,8},{10,11... | collective-permute-start | bytes 786440 | tf_op jit(solution)/shard_map/ppermute | solution.py:174
  44.7 0.7 copy-start.11
  45.4 33.4 %collective-permute-start.3 = (bf16[128,1024]{1,0:T(8,128)(2,1)}, bf16[128,1024]{1,0:T(8,128)(2,1)S(1)}, u32[]{:S(2)}, u32[]{:S(2)}) collective-permute-start(bf16[128,1024]{1,0:T(8,128)(2,1)} %get-tuple-element.20), channel_id=1, source_target_pairs={{0,8},{8,0},{16,24},{24,16},{1,9},{9,1},{17,25},{25,17},{2,10},{10... | collective-permute-start | bytes 786440 | tf_op jit(solution)/shard_map/ppermute | solution.py:197
  48.1 30.8 %collective-permute-start.4 = (bf16[128,1024]{1,0:T(8,128)(2,1)}, bf16[128,1024]{1,0:T(8,128)(2,1)S(1)}, u32[]{:S(2)}, u32[]{:S(2)}) collective-permute-start(bf16[128,1024]{1,0:T(8,128)(2,1)} %get-tuple-element.21), channel_id=1, source_target_pairs={{0,16},{8,24},{16,0},{24,8},{1,17},{9,25},{17,1},{25,9},{2,18},{10... | collective-permute-start | bytes 786440 | tf_op jit(solution)/shard_map/ppermute | solution.py:197
  51.2 27.7 %collective-permute-start.5 = (bf16[128,1024]{1,0:T(8,128)(2,1)}, bf16[128,1024]{1,0:T(8,128)(2,1)S(1)}, u32[]{:S(2)}, u32[]{:S(2)}) collective-permute-start(bf16[128,1024]{1,0:T(8,128)(2,1)} %get-tuple-element.22), channel_id=1, source_target_pairs={{0,24},{8,16},{16,8},{24,0},{1,25},{9,17},{17,9},{25,1},{2,26},{10... | collective-permute-start | bytes 786440 | tf_op jit(solution)/shard_map/ppermute | solution.py:197
  54.7 1.6 copy-start.5
  56.3 13.6 %copy-start.8 = (bf16[256,512]{1,0:T(8,128)(2,1)S(1)}, bf16[256,512]{1,0:T(8,128)(2,1)}, u32[]{:S(2)}) copy-start(bf16[256,512]{1,0:T(8,128)(2,1)} %goal_own.1) | copy-start | bytes 786436
  58.8 1.4 copy-start.1
  60.2 2.0 %copy-start.3 = (bf16[512,4096]{1,0:T(8,128)(2,1)}, bf16[512,4096]{1,0:T(8,128)(2,1)S(1)}, u32[]{:S(2)}) copy-start(bf16[512,4096]{1,0:T(8,128)(2,1)S(1)} %get-tuple-element.18.both) | copy-start | bytes 12582916
  62.1 0.7 copy-start.9
  69.9 2.2 %copy-start.4 = (bf16[512,4096]{1,0:T(8,128)(2,1)S(1)}, bf16[512,4096]{1,0:T(8,128)(2,1)}, u32[]{:S(2)}) copy-start(bf16[512,4096]{1,0:T(8,128)(2,1)} %copy-done.3) | copy-start | bytes 12582916
  72.1 0.9 copy-start.10
  73.1 5.8 %copy-start.12 = (bf16[128,1024]{1,0:T(8,128)(2,1)S(1)}, bf16[128,1024]{1,0:T(8,128)(2,1)}, u32[]{:S(2)}) copy-start(bf16[128,1024]{1,0:T(8,128)(2,1)} %copy-done.11) | copy-start | bytes 786436
  73.1 6.9 %copy-start.2 = (bf16[8,256,512]{2,1,0:T(8,128)(2,1)S(1)}, bf16[8,256,512]{2,1,0:T(8,128)(2,1)}, u32[]{:S(2)}) copy-start(bf16[8,256,512]{2,1,0:T(8,128)(2,1)} %copy-done.1) | copy-start | bytes 6291460
  74.8 5.1 %collective-permute-start.2 = (bf16[512,256]{1,0:T(8,128)(2,1)S(1)}, bf16[512,256]{1,0:T(8,128)(2,1)S(1)}, u32[]{:S(2)}, u32[]{:S(2)}) collective-permute-start(bf16[512,256]{1,0:T(8,128)(2,1)S(1)} %shard_map.87.err_own), channel_id=1, source_target_pairs={{0,1},{1,0},{2,3},{3,2},{4,5},{5,4},{6,7},{7,6},{8,9},{9,8},{10,11... | collective-permute-start | bytes 786440 | tf_op jit(solution)/shard_map/ppermute | solution.py:214
  78.9 12.0 %copy-start.6 = (f32[512,512]{1,0:T(8,128)S(1)}, f32[512,512]{1,0:T(8,128)}, u32[]{:S(2)}) copy-start(f32[512,512]{1,0:T(8,128)} %w.1) | copy-start | bytes 3145732
  81.7 24.0 %collective-permute-start.6 = (bf16[256,512]{1,0:T(8,128)(2,1)S(1)}, bf16[256,512]{1,0:T(8,128)(2,1)S(1)}, u32[]{:S(2)}, u32[]{:S(2)}) collective-permute-start(bf16[256,512]{1,0:T(8,128)(2,1)S(1)} %get-tuple-element.23.order), channel_id=1, source_target_pairs={{0,2},{1,7},{2,4},{3,1},{4,6},{5,3},{6,0},{7,5},{8,10},{9,15},{10,... | collective-permute-start | bytes 786440 | tf_op jit(solution)/shard_map/ppermute | solution.py:29
  85.8 32.8 %collective-permute-start.8 = (bf16[256,512]{1,0:T(8,128)(2,1)}, bf16[256,512]{1,0:T(8,128)(2,1)S(1)}, u32[]{:S(2)}, u32[]{:S(2)}) collective-permute-start(bf16[256,512]{1,0:T(8,128)(2,1)} %get-tuple-element.29), channel_id=1, source_target_pairs={{0,2},{1,7},{2,4},{3,1},{4,6},{5,3},{6,0},{7,5},{8,10},{9,15},{10,... | collective-permute-start | bytes 786440 | tf_op jit(solution)/shard_map/ppermute | solution.py:29
  93.2 0.7 copy-start.13
  93.9 27.6 %all-to-all-start.1 = ((f32[16,8,1024]{2,1,0:T(8,128)}), f32[16,8,1024]{2,1,0:T(8,128)}, u32[]{:S(2)}, u32[]{:S(2)}) async-start(f32[16,8,1024]{2,1,0:T(8,128)} %bitcast.3), calls=%async_computation.1 | async-start | bytes 1048576 | tf_op jit(solution)/shard_map/all_to_all | solution.py:257
  98.6 24.0 %copy-start.15 = (f32[8,1024]{1,0:T(8,128)S(1)}, f32[8,1024]{1,0:T(8,128)}, u32[]{:S(2)}) copy-start(f32[8,1024]{1,0:T(8,128)} %param.9) | copy-start | bytes 98308
  98.6 24.0 %copy-start.16 = (f32[8,1024]{1,0:T(8,128)S(1)}, f32[8,1024]{1,0:T(8,128)}, u32[]{:S(2)}) copy-start(f32[8,1024]{1,0:T(8,128)} %param.11) | copy-start | bytes 98308
  105.8 19.4 %collective-permute-start.7 = (bf16[512,512]{1,0:T(8,128)(2,1)S(1)}, bf16[512,512]{1,0:T(8,128)(2,1)S(1)}, u32[]{:S(2)}, u32[]{:S(2)}) collective-permute-start(bf16[512,512]{1,0:T(8,128)(2,1)S(1)} %shard_map.92), channel_id=1, source_target_pairs={{0,2},{1,7},{2,4},{3,1},{4,6},{5,3},{6,0},{7,5},{8,10},{9,15},{10,... | collective-permute-start | bytes 1572872 | tf_op jit(solution)/shard_map/ppermute | solution.py:29
  118.5 1.0 copy-start.14
  119.5 39.1 %collective-permute-start.9 = (bf16[512,512]{1,0:T(8,128)(2,1)S(1)}, bf16[512,512]{1,0:T(8,128)(2,1)S(1)}, u32[]{:S(2)}, u32[]{:S(2)}) collective-permute-start(bf16[512,512]{1,0:T(8,128)(2,1)S(1)} %shard_map.93), channel_id=1, source_target_pairs={{0,3},{1,6},{2,5},{3,0},{4,7},{5,2},{6,1},{7,4},{8,11},{9,14},{10,... | collective-permute-start | bytes 1572872 | tf_op jit(solution)/shard_map/ppermute | solution.py:29

commit v4 on v3

--- a/solution.py
+++ b/solution.py
@@ -29,31 +29,29 @@
     return lax.ppermute(a, ("zh", "c"), pairs)
 
 
-def transpose_kernel(place, own, mate, order, out, both):
+def transpose_kernel(place, own, targets, mate, goal, order, far_xt, near_xt, own_xt, both):
     del order
     zh, core = place[0], place[1]
     other = 1 - core
-    width = out.shape[1]
-    tokens = own.shape[0]
-    both[:tokens] = own[...]
-    both[tokens:] = mate[...]
+    width = far_xt.shape[1]
+    tokens, deep = own.shape
+    half = targets.shape[1] // 2
+    both[:tokens, :deep] = own[...]
+    both[tokens:, :deep] = mate[...]
+    columns = pl.ds(pl.multiple_of(core * half, half), half)
+    both[:tokens, deep:] = targets[:, columns]
+    both[tokens:, deep:] = goal[:, columns]
     far = lax.rem(zh + 2, ZH)
     near = lax.rem(zh + 1 + 2 * core, ZH)
-    for j, (chip, block, half) in enumerate(
-        (
-            (far, core, core),
-            (far, other, core),
-            (near, core, core),
-            (near, core, other),
-            (near, other, core),
-            (near, other, other),
-            (zh, core, 0),
-            (zh, core, 1),
-        )
+    for out, places in (
+        (far_xt, ((far, core, core), (far, other, core))),
+        (near_xt, ((near, core, core), (near, core, other), (near, other, core), (near, other, other))),
+        (own_xt, ((zh, core, 0), (zh, core, 1))),
     ):
-        columns = pl.ds(pl.multiple_of(((chip * 2 + block) * 2 + half) * width, width), width)
-        out[j, :, :tokens] = own[:, columns].T
-        out[j, :, tokens:] = mate[:, columns].T
+        for j, (chip, block, half) in enumerate(places):
+            columns = pl.ds(pl.multiple_of(((chip * 2 + block) * 2 + half) * width, width), width)
+            out[j, :, :tokens] = own[:, columns].T
+            out[j, :, tokens:] = mate[:, columns].T
 
 
 def spread_kernel(place, column, out):
@@ -64,12 +62,11 @@
         out[i] = part
 
 
-def error_kernel(place, both, w, goal_own, goal_mate, out):
+def error_kernel(both, w, out):
     shards, depth = w.shape[1], w.shape[0] * w.shape[2]
-    tokens = goal_own.shape[0]
+    tokens = both.shape[0] // 2
     width = w.shape[3]
-    columns = pl.ds(pl.multiple_of(place[1] * width, width), width)
-    for i, goal in enumerate((goal_own, goal_mate)):
+    for i in range(2):
         at = slice(i * tokens, (i + 1) * tokens)
         keys = jnp.zeros((tokens, width), jnp.float32)
         for f in range(shards):
@@ -78,7 +75,7 @@
                 w[:, f].reshape(depth, width),
                 preferred_element_type=jnp.float32,
             )
-        errors = keys - goal[:, columns].astype(jnp.float32)
+        errors = keys - both[at, shards * depth :].astype(jnp.float32)
         out[at, :] = errors.astype(jnp.bfloat16)
 
 
@@ -98,16 +95,16 @@
         out[...] = jnp.dot(xt[i], errors, preferred_element_type=jnp.float32).astype(out.dtype)
 
 
-def near_kernel(place, xt, err_own, err_mate, w, part, order, via_a, near_a, via_b, near_b, base, same, *, rate):
+def near_kernel(place, xt, own_xt, err_own, err_mate, w, part, order, via_a, near_a, via_b, near_b, base, same, *, rate):
     del order
     same[...] = part[...]
     errors = errors_of(place, err_own, err_mate)
     for i, out in enumerate((via_a, near_a, via_b, near_b)):
-        out[...] = jnp.dot(xt[2 + i], errors, preferred_element_type=jnp.float32).astype(out.dtype)
+        out[...] = jnp.dot(xt[i], errors, preferred_element_type=jnp.float32).astype(out.dtype)
     rows = xt.shape[1]
     for h in range(2):
         at = slice(h * rows, (h + 1) * rows)
-        base[at, :] = w[at, :] - rate * jnp.dot(xt[6 + h], errors, preferred_element_type=jnp.float32)
+        base[at, :] = w[at, :] - rate * jnp.dot(own_xt[h], errors, preferred_element_type=jnp.float32)
 
 
 def pass_kernel(via, near, far, out):
@@ -171,18 +168,19 @@
     key = lax.all_to_all(copies, ("x", "y"), 0, 0, tiled=True)
 
     mate = lax.ppermute(tokens, "c", SWAP)
-    goal_mate = lax.ppermute(targets, "c", SWAP)
-    xt, both = pl.pallas_call(
+    goal = lax.ppermute(targets, "c", SWAP)
+
+    def turned(pieces):
+        return jax.ShapeDtypeStruct((pieces, own_rows // 2, 2 * rows), jnp.bfloat16)
+
+    far_xt, near_xt, own_xt, both = pl.pallas_call(
         transpose_kernel,
-        out_shape=(
-            jax.ShapeDtypeStruct((2 * ZH, own_rows // 2, 2 * rows), jnp.bfloat16),
-            jax.ShapeDtypeStruct((2 * rows, width), jnp.bfloat16),
-        ),
-        in_specs=[smem, vmem, vmem, anywhere],
-        out_specs=(vmem,) * 2,
+        out_shape=(turned(2), turned(4), turned(2), jax.ShapeDtypeStruct((2 * rows, width + half), jnp.bfloat16)),
+        in_specs=[smem] + [vmem] * 4 + [anywhere],
+        out_specs=(vmem,) * 4,
         compiler_params=PARAMS,
         cost_estimate=cost(0, 16 * rows * width),
-    )(place, tokens, mate, column)
+    )(place, tokens, targets, mate, goal, column)
 
     owned, wide = frag_outer.shape
     block = jax.ShapeDtypeStruct((spots * owned, wide), jnp.bfloat16)
@@ -206,11 +204,11 @@
     err = pl.pallas_call(
         error_kernel,
         out_shape=jax.ShapeDtypeStruct((2 * rows, half), jnp.bfloat16),
-        in_specs=[smem] + [vmem] * 4,
+        in_specs=[vmem] * 2,
         out_specs=vmem,
         compiler_params=PARAMS,
         cost_estimate=cost(4 * rows * width * half, 8 * rows * width),
-    )(place, both, key, targets, goal_mate)
+    )(both, key)
     err_mate = lax.ppermute(err, "c", SWAP)
     rate = INNER_RATE / width
     short = jax.ShapeDtypeStruct((own_rows // 2, columns), jnp.bfloat16)
@@ -223,17 +221,17 @@
         in_specs=[smem] + [vmem] * 3 + [anywhere],
         out_specs=(vmem,) * 2,
         compiler_params=PARAMS,
-    )(place, xt, err, err_mate, part)
+    )(place, far_xt, err, err_mate, part)
 
     far_a = round_z(out_a, 0)
     far_b = round_z(out_b, 0)
     via_a, near_a, via_b, near_b, base, part = pl.pallas_call(
         functools.partial(near_kernel, rate=rate),
         out_shape=(middle, short, middle, short, full, jax.ShapeDtypeStruct(part.shape, part.dtype)),
-        in_specs=[smem] + [vmem] * 5 + [anywhere],
+        in_specs=[smem] + [vmem] * 6 + [anywhere],
         out_specs=(vmem,) * 6,
         compiler_params=PARAMS,
-    )(place, xt, err, err_mate, w_key, part, out_a)
+    )(place, near_xt, own_xt, err, err_mate, w_key, part, out_a)
 
     def passed(via, near, far):
         return pl.pallas_call(

time: 161 us -> 159 us (0.988)
  the two profiles are of different devices: /device:TPU:1 before, /device:TPU:65 now
where the time goes in v4:
time: 159 us; the launch traced here: 158 us
  waiting for transfers between devices  52.7 us (33%)
  starting transfers between devices  46.6 us (29%)
  blocking collectives  25 us (16%)
  local copies, waits for them, and re-layouts  15.9 us (10%)
  Pallas kernels  14.6 us (9%)
  other arithmetic  1.79 us (1%)
    ppermute x4, waiting for transfers between devices, round_z(): return lax.ppermute(a, ('zh', 'c'), pairs)  45.3 us
    all_gather x1, blocking collectives, on_device(): column = lax.all_gather(mine, ('zh', 'c'), axis=0, tiled=True)  25 us
    ppermute x4, starting transfers between devices, round_z(): return lax.ppermute(a, ('zh', 'c'), pairs)  17.4 us
    unnamed x44, local copies, waits for them, and re-layouts  15.1 us
    ppermute x3, starting transfers between devices, on_device(): lax.ppermute(p, 'zl', [(i, i ^ j) for i in range(ZL)])  8.36 us
    all_to_all x1, waiting for transfers between devices, on_device(): key = lax.all_to_all(copies, ('x', 'y'), 0, 0, tiled=True)  7.43 us
    all_to_all x1, starting transfers between devices, on_device(): key = lax.all_to_all(copies, ('x', 'y'), 0, 0, tiled=True)  6.89 us
    all_to_all x1, starting transfers between devices, on_device(): lax.all_to_all(part.reshape(spots, owned, wide), ('x', 'y'), 0, 0, tiled=...  4.85 us
  transfers between devices with their start and end apart: 12, of which 4 were waited for; matrix products, arithmetic and copies ran while one was open for 2% of the time, Pallas kernels for 8%

profile of v4, /device:TPU:65, one launch (start us, length us, event | category | flops | bytes accessed | tf_op | source)
XLA Modules:
  0.0 157.6 jit_solution(11883049787826742444)
XLA Ops:
  0.6 2.6 %collective-permute-start = (bf16[256,4096]{1,0:T(8,128)(2,1)}, bf16[256,4096]{1,0:T(8,128)(2,1)}, u32[]{:S(2)}, u32[]{:S(2)}) collective-permute-start(bf16[256,4096]{1,0:T(8,128)(2,1)} %own.1), channel_id=1, source_target_pairs={{0,1},{1,0},{2,3},{3,2},{4,5},{5,4},{6,7},{7,6},{8,9},{9,8},{10,11... | collective-permute-start | bytes 6291464 | tf_op jit(solution)/shard_map/ppermute | solution.py:170
  3.2 0.9 dynamic-slice_convert_fusion
  4.1 0.1 pad_add_fusion.place
  4.2 25.0 %all_gather.3.order.column = bf16[256,512]{1,0:T(8,128)(2,1)S(1)} all-gather(bf16[32,512]{1,0:T(8,128)(2,1)S(1)} %dynamic-slice_convert_fusion), channel_id=1, replica_groups=mesh['x'=4,'y'=4,'zl'=4,'zh'=4,'c'=2] {'zh','c'}, dimensions={0}, use_global_device_ids=true | all-gather | bytes 294912 | tf_op jit(solution)/shard_map/all_gather | solution.py:160
  29.2 2.1 %shard_map.86 = bf16[16,8,32,256]{3,2,1,0:T(8,128)(2,1)} custom-call(s32[3]{0:T(128)S(1)} %pad_add_fusion.place, bf16[256,512]{1,0:T(8,128)(2,1)S(1)} %all_gather.3.order.column), custom_call_target="tpu_custom_call" | custom-call | tf_op jit(solution)/shard_map/pallas_call | solution.py:161
  31.3 6.9 %all-to-all-start = ((bf16[16,8,32,256]{3,2,1,0:T(8,128)(2,1)}), bf16[16,8,32,256]{3,2,1,0:T(8,128)(2,1)S(1)}, u32[]{:S(2)}, u32[]{:S(2)}) async-start(bf16[16,8,32,256]{3,2,1,0:T(8,128)(2,1)} %shard_map.86), calls=%async_computation | async-start | bytes 4194304 | tf_op jit(solution)/shard_map/all_to_all | solution.py:168
  38.2 2.4 %collective-permute-start.1 = (bf16[256,512]{1,0:T(8,128)(2,1)}, bf16[256,512]{1,0:T(8,128)(2,1)S(1)}, u32[]{:S(2)}, u32[]{:S(2)}) collective-permute-start(bf16[256,512]{1,0:T(8,128)(2,1)} %targets.1), channel_id=1, source_target_pairs={{0,1},{1,0},{2,3},{3,2},{4,5},{5,4},{6,7},{7,6},{8,9},{9,8},{10,11... | collective-permute-start | bytes 786440 | tf_op jit(solution)/shard_map/ppermute | solution.py:171
  40.6 1.6 shard_map.88
  42.1 0.7 copy-done.12
  42.8 2.5 %collective-permute-start.3 = (bf16[128,1024]{1,0:T(8,128)(2,1)}, bf16[128,1024]{1,0:T(8,128)(2,1)}, u32[]{:S(2)}, u32[]{:S(2)}) collective-permute-start(bf16[128,1024]{1,0:T(8,128)(2,1)} %get-tuple-element.23), channel_id=1, source_target_pairs={{0,8},{8,0},{16,24},{24,16},{1,9},{9,1},{17,25},{25,17},{2,10},{10... | collective-permute-start | bytes 786440 | tf_op jit(solution)/shard_map/ppermute | solution.py:195
  45.4 3.1 %collective-permute-start.4 = (bf16[128,1024]{1,0:T(8,128)(2,1)}, bf16[128,1024]{1,0:T(8,128)(2,1)}, u32[]{:S(2)}, u32[]{:S(2)}) collective-permute-start(bf16[128,1024]{1,0:T(8,128)(2,1)} %get-tuple-element.24), channel_id=1, source_target_pairs={{0,16},{8,24},{16,0},{24,8},{1,17},{9,25},{17,1},{25,9},{2,18},{10... | collective-permute-start | bytes 786440 | tf_op jit(solution)/shard_map/ppermute | solution.py:195
  48.5 2.7 %collective-permute-start.5 = (bf16[128,1024]{1,0:T(8,128)(2,1)}, bf16[128,1024]{1,0:T(8,128)(2,1)}, u32[]{:S(2)}, u32[]{:S(2)}) collective-permute-start(bf16[128,1024]{1,0:T(8,128)(2,1)} %get-tuple-element.25), channel_id=1, source_target_pairs={{0,24},{8,16},{16,8},{24,0},{1,25},{9,17},{17,9},{25,1},{2,26},{10... | collective-permute-start | bytes 786440 | tf_op jit(solution)/shard_map/ppermute | solution.py:195
  51.3 0.0 copy-start.2
  51.3 1.6 %copy-done.2 = bf16[256,4096]{1,0:T(8,128)(2,1)S(1)} copy-done((bf16[256,4096]{1,0:T(8,128)(2,1)S(1)}, bf16[256,4096]{1,0:T(8,128)(2,1)}, u32[]{:S(2)}) %copy-start.2) | copy-done | bytes 2097176
  52.9 0.9 copy-done.11
  53.8 2.4 %shard_map.85 = (bf16[2,256,512]{2,1,0:T(8,128)(2,1)S(1)}, bf16[4,256,512]{2,1,0:T(8,128)(2,1)S(1)}, bf16[2,256,512]{2,1,0:T(8,128)(2,1)S(1)}, bf16[512,4352]{1,0:T(8,128)(2,1)S(1)}) custom-call(s32[3]{0:T(128)S(1)} %pad_add_fusion.place, bf16[256,4096]{1,0:T(8,128)(2,1)S(1)} %copy-done.2, bf16[256,512]{1,0:T(8,128)(2,1)S(1)} %copy-done.11, ...), custom_call_target="tpu_custom_call" | custom-call | bytes 16777216 | tf_op jit(solution)/shard_map/pallas_call | solution.py:176
  56.2 2.1 %copy-done = bf16[512,4352]{1,0:T(8,128)(2,1)} copy-done((bf16[512,4352]{1,0:T(8,128)(2,1)}, bf16[512,4352]{1,0:T(8,128)(2,1)S(1)}, u32[]{:S(2)}) %copy-start) | copy-done | bytes 4456472
  58.3 0.8 copy-done.5
  59.1 0.8 copy-done.9
  59.9 7.4 %all-to-all-done.w = bf16[16,8,32,256]{3,2,1,0:T(8,128)(2,1)S(1)} async-done(((bf16[16,8,32,256]{3,2,1,0:T(8,128)(2,1)}), bf16[16,8,32,256]{3,2,1,0:T(8,128)(2,1)S(1)}, u32[]{:S(2)}, u32[]{:S(2)}) %all-to-all-start) | async-done | bytes 2097184 | tf_op jit(solution)/shard_map/all_to_all | solution.py:168
  67.3 2.3 %copy-done.1 = bf16[512,4352]{1,0:T(8,128)(2,1)S(1)} copy-done((bf16[512,4352]{1,0:T(8,128)(2,1)S(1)}, bf16[512,4352]{1,0:T(8,128)(2,1)}, u32[]{:S(2)}) %copy-start.1) | copy-done | bytes 4456472
  69.6 1.2 shard_map.87.err_own
  70.8 0.0 copy-start.3
  70.9 0.0 copy-start.6
  70.9 4.1 %collective-permute-start.2 = (bf16[512,256]{1,0:T(8,128)(2,1)S(1)}, bf16[512,256]{1,0:T(8,128)(2,1)S(1)}, u32[]{:S(2)}, u32[]{:S(2)}) collective-permute-start(bf16[512,256]{1,0:T(8,128)(2,1)S(1)} %shard_map.87.err_own), channel_id=1, source_target_pairs={{0,1},{1,0},{2,3},{3,2},{4,5},{5,4},{6,7},{7,6},{8,9},{9,8},{10,11... | collective-permute-start | bytes 786440 | tf_op jit(solution)/shard_map/ppermute | solution.py:212
  75.0 1.2 shard_map.89.order.part
  76.3 1.0 shard_map.90
  77.3 3.9 %collective-permute-start.8 = (bf16[256,512]{1,0:T(8,128)(2,1)S(1)}, bf16[256,512]{1,0:T(8,128)(2,1)S(1)}, u32[]{:S(2)}, u32[]{:S(2)}) collective-permute-start(bf16[256,512]{1,0:T(8,128)(2,1)S(1)} %get-tuple-element.33), channel_id=1, source_target_pairs={{0,2},{1,7},{2,4},{3,1},{4,6},{5,3},{6,0},{7,5},{8,10},{9,15},{10,... | collective-permute-start | bytes 786440 | tf_op jit(solution)/shard_map/ppermute | solution.py:29
  81.1 5.3 %collective-permute-start.6 = (bf16[256,512]{1,0:T(8,128)(2,1)S(1)}, bf16[256,512]{1,0:T(8,128)(2,1)}, u32[]{:S(2)}, u32[]{:S(2)}) collective-permute-start(bf16[256,512]{1,0:T(8,128)(2,1)S(1)} %get-tuple-element.27.order), channel_id=1, source_target_pairs={{0,2},{1,7},{2,4},{3,1},{4,6},{5,3},{6,0},{7,5},{8,10},{9,15},{10,... | collective-permute-start | bytes 786440 | tf_op jit(solution)/shard_map/ppermute | solution.py:29
  86.5 2.3 %shard_map.91 = (f32[256,512]{1,0:T(8,128)S(1)}, bf16[256,512]{1,0:T(8,128)(2,1)S(1)}, f32[256,512]{1,0:T(8,128)S(1)}, bf16[256,512]{1,0:T(8,128)(2,1)S(1)}, f32...) custom-call(s32[3]{0:T(128)S(1)} %pad_add_fusion.place, bf16[4,256,512]{2,1,0:T(8,128)(2,1)S(1)} %get-tuple-element.19.xt, ...), custom_call_target="tpu_custom_call" | custom-call | tf_op jit(solution)/shard_map/pallas_call | solution.py:228
  88.8 0.8 copy-done.7
  89.6 0.7 copy-done.14
  90.3 0.7 copy-done.18
  91.0 4.8 %all-to-all-start.1 = ((f32[16,8,1024]{2,1,0:T(8,128)}), f32[16,8,1024]{2,1,0:T(8,128)}, u32[]{:S(2)}, u32[]{:S(2)}) async-start(f32[16,8,1024]{2,1,0:T(8,128)} %bitcast.3), calls=%async_computation.1 | async-start | bytes 1048576 | tf_op jit(solution)/shard_map/all_to_all | solution.py:255
  95.9 4.0 %collective-permute-done.8.far = bf16[256,512]{1,0:T(8,128)(2,1)S(1)} collective-permute-done((bf16[256,512]{1,0:T(8,128)(2,1)S(1)}, bf16[256,512]{1,0:T(8,128)(2,1)S(1)}, u32[]{:S(2)}, u32[]{:S(2)}) %collective-permute-start.8) | collective-permute-done | bytes 262176 | tf_op jit(solution)/shard_map/ppermute | solution.py:29
  99.9 0.7 copy-done.16
  100.6 1.0 copy-done.8
  101.6 0.9 copy-done.17
  102.6 0.9 copy-done.19
  103.5 0.1 shard_map.93
  103.6 4.7 %collective-permute-start.9 = (bf16[512,512]{1,0:T(8,128)(2,1)S(1)}, bf16[512,512]{1,0:T(8,128)(2,1)S(1)}, u32[]{:S(2)}, u32[]{:S(2)}) collective-permute-start(bf16[512,512]{1,0:T(8,128)(2,1)S(1)} %shard_map.93), channel_id=1, source_target_pairs={{0,3},{1,6},{2,5},{3,0},{4,7},{5,2},{6,1},{7,4},{8,11},{9,14},{10,... | collective-permute-start | bytes 1572872 | tf_op jit(solution)/shard_map/ppermute | solution.py:29
  108.3 1.0 shard_map.92
  109.3 3.6 %collective-permute-start.7 = (bf16[512,512]{1,0:T(8,128)(2,1)S(1)}, bf16[512,512]{1,0:T(8,128)(2,1)S(1)}, u32[]{:S(2)}, u32[]{:S(2)}) collective-permute-start(bf16[512,512]{1,0:T(8,128)(2,1)S(1)} %shard_map.92), channel_id=1, source_target_pairs={{0,2},{1,7},{2,4},{3,1},{4,6},{5,3},{6,0},{7,5},{8,10},{9,15},{10,... | collective-permute-start | bytes 1572872 | tf_op jit(solution)/shard_map/ppermute | solution.py:29
  112.9 1.1 reduce_sum.9
  114.0 0.6 multiply_subtract_fusion
  114.6 32.9 %collective-permute-done.9.crossed = bf16[512,512]{1,0:T(8,128)(2,1)S(1)} collective-permute-done((bf16[512,512]{1,0:T(8,128)(2,1)S(1)}, bf16[512,512]{1,0:T(8,128)(2,1)S(1)}, u32[]{:S(2)}, u32[]{:S(2)}) %collective-permute-start.9) | collective-permute-done | bytes 524320 | tf_op jit(solution)/shard_map/ppermute | solution.py:29
  147.6 8.3 %collective-permute-done.7.straight = bf16[512,512]{1,0:T(8,128)(2,1)S(1)} collective-permute-done((bf16[512,512]{1,0:T(8,128)(2,1)S(1)}, bf16[512,512]{1,0:T(8,128)(2,1)S(1)}, u32[]{:S(2)}, u32[]{:S(2)}) %collective-permute-start.7) | collective-permute-done | bytes 524320 | tf_op jit(solution)/shard_map/ppermute | solution.py:29
  155.9 1.7 %shard_map.94 = f32[512,512]{1,0:T(8,128)} custom-call(s32[3]{0:T(128)S(1)} %pad_add_fusion.place, f32[512,512]{1,0:T(8,128)S(1)} %get-tuple-element.28.base, bf16[512,512]{1,0:T(8,128)(2,1)S(1)} %collective-permute-done.7.straight, bf16[512,512]{1,0:T(8,128)(2,1)S(1)} %collective-permute-done.9.crossed), custom_call_target="tpu_custom_call" | custom-call | tf_op jit(solution)/shard_map/pallas_call | solution.py:247
  (35 shorter events, 0.1 us)
Async XLA Ops:
  0.6 50.6 %collective-permute-start = (bf16[256,4096]{1,0:T(8,128)(2,1)}, bf16[256,4096]{1,0:T(8,128)(2,1)}, u32[]{:S(2)}, u32[]{:S(2)}) collective-permute-start(bf16[256,4096]{1,0:T(8,128)(2,1)} %own.1), channel_id=1, source_target_pairs={{0,1},{1,0},{2,3},{3,2},{4,5},{5,4},{6,7},{7,6},{8,9},{9,8},{10,11... | collective-permute-start | bytes 6291464 | tf_op jit(solution)/shard_map/ppermute | solution.py:170
  31.3 9.3 %copy-start.4 = (bf16[512,1024]{1,0:T(8,128)(2,1)S(1)}, bf16[512,1024]{1,0:T(8,128)(2,1)}, u32[]{:S(2)}) copy-start(bf16[512,1024]{1,0:T(8,128)(2,1)} %given.1) | copy-start | bytes 3145732
  31.3 36.0 %all-to-all-start = ((bf16[16,8,32,256]{3,2,1,0:T(8,128)(2,1)}), bf16[16,8,32,256]{3,2,1,0:T(8,128)(2,1)S(1)}, u32[]{:S(2)}, u32[]{:S(2)}) async-start(bf16[16,8,32,256]{3,2,1,0:T(8,128)(2,1)} %shard_map.86), calls=%async_computation | async-start | bytes 4194304 | tf_op jit(solution)/shard_map/all_to_all | solution.py:168
  38.2 13.1 %collective-permute-start.1 = (bf16[256,512]{1,0:T(8,128)(2,1)}, bf16[256,512]{1,0:T(8,128)(2,1)S(1)}, u32[]{:S(2)}, u32[]{:S(2)}) collective-permute-start(bf16[256,512]{1,0:T(8,128)(2,1)} %targets.1), channel_id=1, source_target_pairs={{0,1},{1,0},{2,3},{3,2},{4,5},{5,4},{6,7},{7,6},{8,9},{9,8},{10,11... | collective-permute-start | bytes 786440 | tf_op jit(solution)/shard_map/ppermute | solution.py:171
  42.1 0.7 copy-start.12
  42.8 32.1 %collective-permute-start.3 = (bf16[128,1024]{1,0:T(8,128)(2,1)}, bf16[128,1024]{1,0:T(8,128)(2,1)}, u32[]{:S(2)}, u32[]{:S(2)}) collective-permute-start(bf16[128,1024]{1,0:T(8,128)(2,1)} %get-tuple-element.23), channel_id=1, source_target_pairs={{0,8},{8,0},{16,24},{24,16},{1,9},{9,1},{17,25},{25,17},{2,10},{10... | collective-permute-start | bytes 786440 | tf_op jit(solution)/shard_map/ppermute | solution.py:195
  45.4 29.6 %collective-permute-start.4 = (bf16[128,1024]{1,0:T(8,128)(2,1)}, bf16[128,1024]{1,0:T(8,128)(2,1)}, u32[]{:S(2)}, u32[]{:S(2)}) collective-permute-start(bf16[128,1024]{1,0:T(8,128)(2,1)} %get-tuple-element.24), channel_id=1, source_target_pairs={{0,16},{8,24},{16,0},{24,8},{1,17},{9,25},{17,1},{25,9},{2,18},{10... | collective-permute-start | bytes 786440 | tf_op jit(solution)/shard_map/ppermute | solution.py:195
  48.5 26.5 %collective-permute-start.5 = (bf16[128,1024]{1,0:T(8,128)(2,1)}, bf16[128,1024]{1,0:T(8,128)(2,1)}, u32[]{:S(2)}, u32[]{:S(2)}) collective-permute-start(bf16[128,1024]{1,0:T(8,128)(2,1)} %get-tuple-element.25), channel_id=1, source_target_pairs={{0,24},{8,16},{16,8},{24,0},{1,25},{9,17},{17,9},{25,1},{2,26},{10... | collective-permute-start | bytes 786440 | tf_op jit(solution)/shard_map/ppermute | solution.py:195
  51.3 1.6 %copy-start.2 = (bf16[256,4096]{1,0:T(8,128)(2,1)S(1)}, bf16[256,4096]{1,0:T(8,128)(2,1)}, u32[]{:S(2)}) copy-start(bf16[256,4096]{1,0:T(8,128)(2,1)} %own.1) | copy-start | bytes 6291460
  52.8 0.9 copy-start.11
  56.2 2.1 %copy-start = (bf16[512,4352]{1,0:T(8,128)(2,1)}, bf16[512,4352]{1,0:T(8,128)(2,1)S(1)}, u32[]{:S(2)}) copy-start(bf16[512,4352]{1,0:T(8,128)(2,1)S(1)} %get-tuple-element.21.both) | copy-start | bytes 13369348
  58.3 0.8 copy-start.5
  59.1 0.8 copy-start.9
  67.3 2.3 %copy-start.1 = (bf16[512,4352]{1,0:T(8,128)(2,1)S(1)}, bf16[512,4352]{1,0:T(8,128)(2,1)}, u32[]{:S(2)}) copy-start(bf16[512,4352]{1,0:T(8,128)(2,1)} %copy-done) | copy-start | bytes 13369348
  69.6 5.4 %copy-start.13 = (bf16[128,1024]{1,0:T(8,128)(2,1)S(1)}, bf16[128,1024]{1,0:T(8,128)(2,1)}, u32[]{:S(2)}) copy-start(bf16[128,1024]{1,0:T(8,128)(2,1)} %copy-done.12) | copy-start | bytes 786436
  69.6 6.7 %copy-start.10 = (bf16[2,256,512]{2,1,0:T(8,128)(2,1)S(1)}, bf16[2,256,512]{2,1,0:T(8,128)(2,1)}, u32[]{:S(2)}) copy-start(bf16[2,256,512]{2,1,0:T(8,128)(2,1)} %copy-done.9) | copy-start | bytes 1572868
  70.8 15.6 %copy-start.3 = (f32[512,512]{1,0:T(8,128)S(1)}, f32[512,512]{1,0:T(8,128)}, u32[]{:S(2)}) copy-start(f32[512,512]{1,0:T(8,128)} %w.1) | copy-start | bytes 3145732
  70.9 15.6 %copy-start.6 = (bf16[2,256,512]{2,1,0:T(8,128)(2,1)S(1)}, bf16[2,256,512]{2,1,0:T(8,128)(2,1)}, u32[]{:S(2)}) copy-start(bf16[2,256,512]{2,1,0:T(8,128)(2,1)} %copy-done.5) | copy-start | bytes 1572868
  70.9 5.4 %collective-permute-start.2 = (bf16[512,256]{1,0:T(8,128)(2,1)S(1)}, bf16[512,256]{1,0:T(8,128)(2,1)S(1)}, u32[]{:S(2)}, u32[]{:S(2)}) collective-permute-start(bf16[512,256]{1,0:T(8,128)(2,1)S(1)} %shard_map.87.err_own), channel_id=1, source_target_pairs={{0,1},{1,0},{2,3},{3,2},{4,5},{5,4},{6,7},{7,6},{8,9},{9,8},{10,11... | collective-permute-start | bytes 786440 | tf_op jit(solution)/shard_map/ppermute | solution.py:212
  77.3 22.6 %collective-permute-start.8 = (bf16[256,512]{1,0:T(8,128)(2,1)S(1)}, bf16[256,512]{1,0:T(8,128)(2,1)S(1)}, u32[]{:S(2)}, u32[]{:S(2)}) collective-permute-start(bf16[256,512]{1,0:T(8,128)(2,1)S(1)} %get-tuple-element.33), channel_id=1, source_target_pairs={{0,2},{1,7},{2,4},{3,1},{4,6},{5,3},{6,0},{7,5},{8,10},{9,15},{10,... | collective-permute-start | bytes 786440 | tf_op jit(solution)/shard_map/ppermute | solution.py:29
  81.1 27.1 %collective-permute-start.6 = (bf16[256,512]{1,0:T(8,128)(2,1)S(1)}, bf16[256,512]{1,0:T(8,128)(2,1)}, u32[]{:S(2)}, u32[]{:S(2)}) collective-permute-start(bf16[256,512]{1,0:T(8,128)(2,1)S(1)} %get-tuple-element.27.order), channel_id=1, source_target_pairs={{0,2},{1,7},{2,4},{3,1},{4,6},{5,3},{6,0},{7,5},{8,10},{9,15},{10,... | collective-permute-start | bytes 786440 | tf_op jit(solution)/shard_map/ppermute | solution.py:29
  88.8 0.8 copy-start.7
  89.6 0.7 copy-start.14
  90.3 0.7 copy-start.18
  91.0 17.3 %copy-start.15 = (bf16[256,512]{1,0:T(8,128)(2,1)S(1)}, bf16[256,512]{1,0:T(8,128)(2,1)}, u32[]{:S(2)}) copy-start(bf16[256,512]{1,0:T(8,128)(2,1)} %copy-done.14) | copy-start | bytes 786436
  91.0 23.0 %copy-start.20 = (f32[8,1024]{1,0:T(8,128)S(1)}, f32[8,1024]{1,0:T(8,128)}, u32[]{:S(2)}) copy-start(f32[8,1024]{1,0:T(8,128)} %param.9) | copy-start | bytes 98308
  91.0 23.0 %copy-start.21 = (f32[8,1024]{1,0:T(8,128)S(1)}, f32[8,1024]{1,0:T(8,128)}, u32[]{:S(2)}) copy-start(f32[8,1024]{1,0:T(8,128)} %param.11) | copy-start | bytes 98308
  91.0 21.9 %all-to-all-start.1 = ((f32[16,8,1024]{2,1,0:T(8,128)}), f32[16,8,1024]{2,1,0:T(8,128)}, u32[]{:S(2)}, u32[]{:S(2)}) async-start(f32[16,8,1024]{2,1,0:T(8,128)} %bitcast.3), calls=%async_computation.1 | async-start | bytes 1048576 | tf_op jit(solution)/shard_map/all_to_all | solution.py:255
  99.9 0.7 copy-start.16
  100.6 1.0 copy-start.8
  101.6 0.9 copy-start.17
  102.6 0.9 copy-start.19
  103.6 44.0 %collective-permute-start.9 = (bf16[512,512]{1,0:T(8,128)(2,1)S(1)}, bf16[512,512]{1,0:T(8,128)(2,1)S(1)}, u32[]{:S(2)}, u32[]{:S(2)}) collective-permute-start(bf16[512,512]{1,0:T(8,128)(2,1)S(1)} %shard_map.93), channel_id=1, source_target_pairs={{0,3},{1,6},{2,5},{3,0},{4,7},{5,2},{6,1},{7,4},{8,11},{9,14},{10,... | collective-permute-start | bytes 1572872 | tf_op jit(solution)/shard_map/ppermute | solution.py:29
  109.3 46.6 %collective-permute-start.7 = (bf16[512,512]{1,0:T(8,128)(2,1)S(1)}, bf16[512,512]{1,0:T(8,128)(2,1)S(1)}, u32[]{:S(2)}, u32[]{:S(2)}) collective-permute-start(bf16[512,512]{1,0:T(8,128)(2,1)S(1)} %shard_map.92), channel_id=1, source_target_pairs={{0,2},{1,7},{2,4},{3,1},{4,6},{5,3},{6,0},{7,5},{8,10},{9,15},{10,... | collective-permute-start | bytes 1572872 | tf_op jit(solution)/shard_map/ppermute | solution.py:29

commit v5 on v4

--- a/solution.py
+++ b/solution.py
@@ -88,16 +88,19 @@
     return jnp.concatenate([low, high], axis=1)
 
 
-def far_kernel(place, xt, err_own, err_mate, order, *outs):
-    del order
+def far_kernel(place, xt, err_own, err_mate, one, two, three, out):
+    del one, two, three
     errors = errors_of(place, err_own, err_mate)
-    for i, out in enumerate(outs):
-        out[...] = jnp.dot(xt[i], errors, preferred_element_type=jnp.float32).astype(out.dtype)
-
-
-def near_kernel(place, xt, own_xt, err_own, err_mate, w, part, order, via_a, near_a, via_b, near_b, base, same, *, rate):
-    del order
-    same[...] = part[...]
+    rows = xt.shape[1]
+    for i in range(2):
+        part = jnp.dot(xt[i], errors, preferred_element_type=jnp.float32)
+        out[i * rows : (i + 1) * rows, :] = part.astype(out.dtype)
+
+
+def near_kernel(place, xt, own_xt, err_own, err_mate, w, *refs, rate):
+    parts, (_, via_a, near_a, via_b, near_b, base, total) = refs[:ZL], refs[ZL:]
+    keep, one, two, three = (p[...].astype(jnp.float32) for p in parts)
+    total[...] = (keep + one) + (two + three)
     errors = errors_of(place, err_own, err_mate)
     for i, out in enumerate((via_a, near_a, via_b, near_b)):
         out[...] = jnp.dot(xt[i], errors, preferred_element_type=jnp.float32).astype(out.dtype)
@@ -107,19 +110,18 @@
         base[at, :] = w[at, :] - rate * jnp.dot(own_xt[h], errors, preferred_element_type=jnp.float32)
 
 
-def pass_kernel(via, near, far, out):
-    rows = far.shape[0]
-    out[:rows] = (via[...] + far[...].astype(jnp.float32)).astype(out.dtype)
-    out[rows:] = near[...]
-
-
-def finish_kernel(place, base, straight, crossed, out, *, rate):
-    rows = base.shape[0] // 2
-    for h in range(2):
-        first = place[1] ^ h
-        at = slice(h * rows, (h + 1) * rows)
-        grad = straight[pl.ds(pl.multiple_of(first * rows, rows), rows), :].astype(jnp.float32)
-        grad += crossed[pl.ds(pl.multiple_of((1 - first) * rows, rows), rows), :].astype(jnp.float32)
+def pass_kernel(via, far, out, *, half):
+    rows = via.shape[0]
+    out[...] = (via[...] + far[half * rows : (half + 1) * rows, :].astype(jnp.float32)).astype(out.dtype)
+
+
+def finish_kernel(place, base, near_a, near_b, sum_a, sum_b, out, *, rate):
+    rows = near_a.shape[0]
+    core = place[1]
+    for first, (plain, total) in ((True, (near_b, sum_a)), (False, (near_a, sum_b))):
+        half = core if first else 1 - core
+        at = pl.ds(pl.multiple_of(half * rows, rows), rows)
+        grad = plain[...].astype(jnp.float32) + total[...].astype(jnp.float32)
         out[at, :] = base[at, :] - rate * grad
 
 
@@ -134,12 +136,6 @@
             held[i, at : at + 2 * owned] = block[:, i].reshape(2 * owned, wide).astype(held.dtype)
     for j, out in enumerate((keep, one, two, three)):
         out[...] = held[place[2] ^ j]
-
-
-def reduce_kernel(keep, one, two, three, out):
-    out[...] = (keep[...].astype(jnp.float32) + one[...].astype(jnp.float32)) + (
-        two[...].astype(jnp.float32) + three[...].astype(jnp.float32)
-    )
 
 
 def on_device(tokens, w_key, targets, frag_outer, frag_local, frag_moment):
@@ -193,14 +189,6 @@
         compiler_params=PARAMS,
     )(place, frag_local, column)
     parts = [lax.ppermute(p, "zl", [(i, i ^ j) for i in range(ZL)]) if j else p for j, p in enumerate(parts)]
-    part = pl.pallas_call(
-        reduce_kernel,
-        out_shape=jax.ShapeDtypeStruct(block.shape, jnp.float32),
-        in_specs=[vmem] * ZL,
-        out_specs=vmem,
-        compiler_params=PARAMS,
-    )(*parts)
-
     err = pl.pallas_call(
         error_kernel,
         out_shape=jax.ShapeDtypeStruct((2 * rows, half), jnp.bfloat16),
@@ -215,42 +203,43 @@
     middle = jax.ShapeDtypeStruct((own_rows // 2, columns), jnp.float32)
     long = jax.ShapeDtypeStruct((own_rows, columns), jnp.bfloat16)
     full = jax.ShapeDtypeStruct((own_rows, columns), jnp.float32)
-    out_a, out_b = pl.pallas_call(
+    out = pl.pallas_call(
         far_kernel,
-        out_shape=(short,) * 2,
-        in_specs=[smem] + [vmem] * 3 + [anywhere],
-        out_specs=(vmem,) * 2,
-        compiler_params=PARAMS,
-    )(place, far_xt, err, err_mate, part)
-
-    far_a = round_z(out_a, 0)
-    far_b = round_z(out_b, 0)
+        out_shape=long,
+        in_specs=[smem] + [vmem] * 3 + [anywhere] * 3,
+        out_specs=vmem,
+        compiler_params=PARAMS,
+    )(place, far_xt, err, err_mate, *parts[1:])
+
+    far = round_z(out, 0)
     via_a, near_a, via_b, near_b, base, part = pl.pallas_call(
         functools.partial(near_kernel, rate=rate),
-        out_shape=(middle, short, middle, short, full, jax.ShapeDtypeStruct(part.shape, part.dtype)),
-        in_specs=[smem] + [vmem] * 6 + [anywhere],
+        out_shape=(middle, short, middle, short, full, jax.ShapeDtypeStruct(block.shape, jnp.float32)),
+        in_specs=[smem] + [vmem] * (5 + ZL) + [anywhere],
         out_specs=(vmem,) * 6,
         compiler_params=PARAMS,
-    )(place, near_xt, own_xt, err, err_mate, w_key, part, out_a)
-
-    def passed(via, near, far):
+    )(place, near_xt, own_xt, err, err_mate, w_key, *parts, out)
+    near_a = round_z(near_a, 0)
+    near_b = round_z(near_b, 1)
+
+    def passed(via, half):
         return pl.pallas_call(
-            pass_kernel,
-            out_shape=long,
-            in_specs=[vmem] * 3,
+            functools.partial(pass_kernel, half=half),
+            out_shape=short,
+            in_specs=[vmem] * 2,
             out_specs=vmem,
             compiler_params=PARAMS,
-        )(via, near, far)
-
-    straight = round_z(passed(via_a, near_a, far_a), 0)
-    crossed = round_z(passed(via_b, near_b, far_b), 1)
+        )(via, far)
+
+    sum_a = round_z(passed(via_a, 0), 0)
+    sum_b = round_z(passed(via_b, 1), 1)
     new_key = pl.pallas_call(
         functools.partial(finish_kernel, rate=rate),
         out_shape=full,
-        in_specs=[smem] + [vmem] * 3,
-        out_specs=vmem,
-        compiler_params=PARAMS,
-    )(place, base, straight, crossed)
+        in_specs=[smem] + [vmem] * 5,
+        out_specs=vmem,
+        compiler_params=PARAMS,
+    )(place, base, near_a, near_b, sum_a, sum_b)
 
     part = lax.all_to_all(part.reshape(spots, owned, wide), ("x", "y"), 0, 0, tiled=True)
     mean = frag_outer - part.sum(0) / (spots * ZL)

time: 159 us -> 157 us (0.987)
  the two profiles are of different devices: /device:TPU:65 before, /device:TPU:1 now
where the time goes in v5:
time: 157 us; the launch traced here: 155 us
  starting transfers between devices  57.7 us (37%)
  waiting for transfers between devices  46.4 us (30%)
  blocking collectives  21.4 us (14%)
  local copies, waits for them, and re-layouts  14.8 us (9%)
  Pallas kernels  12.5 us (8%)
  other arithmetic  1.79 us (1%)
    ppermute x5, waiting for transfers between devices, round_z(): return lax.ppermute(a, ('zh', 'c'), pairs)  38.7 us
    ppermute x5, starting transfers between devices, round_z(): return lax.ppermute(a, ('zh', 'c'), pairs)  21.4 us
    all_gather x1, blocking collectives, on_device(): column = lax.all_gather(mine, ('zh', 'c'), axis=0, tiled=True)  21.4 us
    unnamed x42, local copies, waits for them, and re-layouts  14 us
    ppermute x3, starting transfers between devices, on_device(): lax.ppermute(p, 'zl', [(i, i ^ j) for i in range(ZL)])  9.26 us
    ppermute x1, starting transfers between devices, on_device(): mate = lax.ppermute(tokens, 'c', SWAP)  8.79 us
    all_to_all x1, starting transfers between devices, on_device(): key = lax.all_to_all(copies, ('x', 'y'), 0, 0, tiled=True)  6.89 us
    all_to_all x1, waiting for transfers between devices, on_device(): key = lax.all_to_all(copies, ('x', 'y'), 0, 0, tiled=True)  6.55 us
  transfers between devices with their start and end apart: 13, of which 6 were waited for; matrix products, arithmetic and copies ran while one was open for 2% of the time, Pallas kernels for 6%

profile of v5, /device:TPU:1, one launch (start us, length us, event | category | flops | bytes accessed | tf_op | source)
XLA Modules:
  0.0 155.4 jit_solution(4141462666754048604)
XLA Ops:
  0.6 8.8 %collective-permute-start = (bf16[256,4096]{1,0:T(8,128)(2,1)}, bf16[256,4096]{1,0:T(8,128)(2,1)}, u32[]{:S(2)}, u32[]{:S(2)}) collective-permute-start(bf16[256,4096]{1,0:T(8,128)(2,1)} %own.1), channel_id=1, source_target_pairs={{0,1},{1,0},{2,3},{3,2},{4,5},{5,4},{6,7},{7,6},{8,9},{9,8},{10,11... | collective-permute-start | bytes 6291464 | tf_op jit(solution)/shard_map/ppermute | solution.py:166
  9.4 0.9 dynamic-slice_convert_fusion
  10.3 0.1 pad_add_fusion.place
  10.4 21.4 %all_gather.3.order.column = bf16[256,512]{1,0:T(8,128)(2,1)S(1)} all-gather(bf16[32,512]{1,0:T(8,128)(2,1)S(1)} %dynamic-slice_convert_fusion), channel_id=1, replica_groups=mesh['x'=4,'y'=4,'zl'=4,'zh'=4,'c'=2] {'zh','c'}, dimensions={0}, use_global_device_ids=true | all-gather | bytes 294912 | tf_op jit(solution)/shard_map/all_gather | solution.py:156
  31.7 2.1 %shard_map.86 = bf16[16,8,32,256]{3,2,1,0:T(8,128)(2,1)} custom-call(s32[3]{0:T(128)S(1)} %pad_add_fusion.place, bf16[256,512]{1,0:T(8,128)(2,1)S(1)} %all_gather.3.order.column), custom_call_target="tpu_custom_call" | custom-call | tf_op jit(solution)/shard_map/pallas_call | solution.py:157
  33.8 6.9 %all-to-all-start = ((bf16[16,8,32,256]{3,2,1,0:T(8,128)(2,1)}), bf16[16,8,32,256]{3,2,1,0:T(8,128)(2,1)S(1)}, u32[]{:S(2)}, u32[]{:S(2)}) async-start(bf16[16,8,32,256]{3,2,1,0:T(8,128)(2,1)} %shard_map.86), calls=%async_computation | async-start | bytes 4194304 | tf_op jit(solution)/shard_map/all_to_all | solution.py:164
  40.7 2.4 %collective-permute-start.1 = (bf16[256,512]{1,0:T(8,128)(2,1)}, bf16[256,512]{1,0:T(8,128)(2,1)S(1)}, u32[]{:S(2)}, u32[]{:S(2)}) collective-permute-start(bf16[256,512]{1,0:T(8,128)(2,1)} %targets.1), channel_id=1, source_target_pairs={{0,1},{1,0},{2,3},{3,2},{4,5},{5,4},{6,7},{7,6},{8,9},{9,8},{10,11... | collective-permute-start | bytes 786440 | tf_op jit(solution)/shard_map/ppermute | solution.py:167
  43.1 1.6 %shard_map.88 = (bf16[128,1024]{1,0:T(8,128)(2,1)S(1)}, bf16[128,1024]{1,0:T(8,128)(2,1)}, bf16[128,1024]{1,0:T(8,128)(2,1)}, bf16[128,1024]{1,0:T(8,128)(2,1)}) custom-call(s32[3]{0:T(128)S(1)} %pad_add_fusion.place, bf16[512,1024]{1,0:T(8,128)(2,1)S(1)} %copy-done.4, bf16[256,512]{1,0:T(8,128)(2,1)S(1)} %all_gather.3.order.column), custom_call_target="tpu_custom_call" | custom-call | tf_op jit(solution)/shard_map/pallas_call | solution.py:183
  44.7 0.7 copy-done.15
  45.4 2.6 %collective-permute-start.3 = (bf16[128,1024]{1,0:T(8,128)(2,1)}, bf16[128,1024]{1,0:T(8,128)(2,1)}, u32[]{:S(2)}, u32[]{:S(2)}) collective-permute-start(bf16[128,1024]{1,0:T(8,128)(2,1)} %get-tuple-element.21), channel_id=1, source_target_pairs={{0,8},{8,0},{16,24},{24,16},{1,9},{9,1},{17,25},{25,17},{2,10},{10... | collective-permute-start | bytes 786440 | tf_op jit(solution)/shard_map/ppermute | solution.py:191
  48.0 3.1 %collective-permute-start.4 = (bf16[128,1024]{1,0:T(8,128)(2,1)}, bf16[128,1024]{1,0:T(8,128)(2,1)}, u32[]{:S(2)}, u32[]{:S(2)}) collective-permute-start(bf16[128,1024]{1,0:T(8,128)(2,1)} %get-tuple-element.22), channel_id=1, source_target_pairs={{0,16},{8,24},{16,0},{24,8},{1,17},{9,25},{17,1},{25,9},{2,18},{10... | collective-permute-start | bytes 786440 | tf_op jit(solution)/shard_map/ppermute | solution.py:191
  51.1 3.5 %collective-permute-start.5 = (bf16[128,1024]{1,0:T(8,128)(2,1)}, bf16[128,1024]{1,0:T(8,128)(2,1)}, u32[]{:S(2)}, u32[]{:S(2)}) collective-permute-start(bf16[128,1024]{1,0:T(8,128)(2,1)} %get-tuple-element.23), channel_id=1, source_target_pairs={{0,24},{8,16},{16,8},{24,0},{1,25},{9,17},{17,9},{25,1},{2,26},{10... | collective-permute-start | bytes 786440 | tf_op jit(solution)/shard_map/ppermute | solution.py:191
  54.7 0.0 copy-start.2
  54.7 1.6 %copy-done.2 = bf16[256,4096]{1,0:T(8,128)(2,1)S(1)} copy-done((bf16[256,4096]{1,0:T(8,128)(2,1)S(1)}, bf16[256,4096]{1,0:T(8,128)(2,1)}, u32[]{:S(2)}) %copy-start.2) | copy-done | bytes 2097176
  56.3 0.9 copy-done.14
  57.2 2.4 %shard_map.85 = (bf16[2,256,512]{2,1,0:T(8,128)(2,1)S(1)}, bf16[4,256,512]{2,1,0:T(8,128)(2,1)S(1)}, bf16[2,256,512]{2,1,0:T(8,128)(2,1)S(1)}, bf16[512,4352]{1,0:T(8,128)(2,1)S(1)}) custom-call(s32[3]{0:T(128)S(1)} %pad_add_fusion.place, bf16[256,4096]{1,0:T(8,128)(2,1)S(1)} %copy-done.2, bf16[256,512]{1,0:T(8,128)(2,1)S(1)} %copy-done.14, ...), custom_call_target="tpu_custom_call" | custom-call | bytes 16777216 | tf_op jit(solution)/shard_map/pallas_call | solution.py:172
  59.7 2.0 %copy-done = bf16[512,4352]{1,0:T(8,128)(2,1)} copy-done((bf16[512,4352]{1,0:T(8,128)(2,1)}, bf16[512,4352]{1,0:T(8,128)(2,1)S(1)}, u32[]{:S(2)}) %copy-start) | copy-done | bytes 4456472
  61.7 0.8 copy-done.5
  62.5 0.8 copy-done.7
  63.3 6.6 %all-to-all-done.w = bf16[16,8,32,256]{3,2,1,0:T(8,128)(2,1)S(1)} async-done(((bf16[16,8,32,256]{3,2,1,0:T(8,128)(2,1)}), bf16[16,8,32,256]{3,2,1,0:T(8,128)(2,1)S(1)}, u32[]{:S(2)}, u32[]{:S(2)}) %all-to-all-start) | async-done | bytes 2097184 | tf_op jit(solution)/shard_map/all_to_all | solution.py:164
  69.9 2.3 %copy-done.1 = bf16[512,4352]{1,0:T(8,128)(2,1)S(1)} copy-done((bf16[512,4352]{1,0:T(8,128)(2,1)S(1)}, bf16[512,4352]{1,0:T(8,128)(2,1)}, u32[]{:S(2)}) %copy-start.1) | copy-done | bytes 4456472
  72.1 1.2 shard_map.87.err_own
  73.4 0.0 copy-start.3
  73.4 0.0 copy-start.6
  73.4 4.1 %collective-permute-start.2 = (bf16[512,256]{1,0:T(8,128)(2,1)S(1)}, bf16[512,256]{1,0:T(8,128)(2,1)S(1)}, u32[]{:S(2)}, u32[]{:S(2)}) collective-permute-start(bf16[512,256]{1,0:T(8,128)(2,1)S(1)} %shard_map.87.err_own), channel_id=1, source_target_pairs={{0,1},{1,0},{2,3},{3,2},{4,5},{5,4},{6,7},{7,6},{8,9},{9,8},{10,11... | collective-permute-start | bytes 786440 | tf_op jit(solution)/shard_map/ppermute | solution.py:200
  77.5 1.1 collective-permute-done.2.err_mate
  78.7 1.0 shard_map.89.refs_4_
  79.7 4.1 %collective-permute-start.8 = (bf16[512,512]{1,0:T(8,128)(2,1)S(1)}, bf16[512,512]{1,0:T(8,128)(2,1)S(1)}, u32[]{:S(2)}, u32[]{:S(2)}) collective-permute-start(bf16[512,512]{1,0:T(8,128)(2,1)S(1)} %shard_map.89.refs_4_), channel_id=1, source_target_pairs={{0,2},{1,7},{2,4},{3,1},{4,6},{5,3},{6,0},{7,5},{8,10},{9,15},{10,... | collective-permute-start | bytes 1572872 | tf_op jit(solution)/shard_map/ppermute | solution.py:29
  83.8 2.4 %shard_map.90 = (f32[256,512]{1,0:T(8,128)S(1)}, bf16[256,512]{1,0:T(8,128)(2,1)S(1)}, f32[256,512]{1,0:T(8,128)S(1)}, bf16[256,512]{1,0:T(8,128)(2,1)S(1)}, f32...) custom-call(s32[3]{0:T(128)S(1)} %pad_add_fusion.place, bf16[4,256,512]{2,1,0:T(8,128)(2,1)S(1)} %get-tuple-element.17.xt, ...), custom_call_target="tpu_custom_call" | custom-call | tf_op jit(solution)/shard_map/pallas_call | solution.py:215
  86.2 0.0 copy-start.10
  86.2 0.8 copy-done.10
  87.0 0.8 copy-done.12
  87.8 0.7 copy-done.17
  88.5 0.7 copy-done.18
  89.2 0.8 copy-done.9
  90.0 4.8 %all-to-all-start.1 = ((f32[16,8,1024]{2,1,0:T(8,128)}), f32[16,8,1024]{2,1,0:T(8,128)}, u32[]{:S(2)}, u32[]{:S(2)}) async-start(f32[16,8,1024]{2,1,0:T(8,128)} %bitcast.4), calls=%async_computation.1 | async-start | bytes 1048576 | tf_op jit(solution)/shard_map/all_to_all | solution.py:244
  94.8 5.1 %collective-permute-start.6 = (bf16[256,512]{1,0:T(8,128)(2,1)}, bf16[256,512]{1,0:T(8,128)(2,1)S(1)}, u32[]{:S(2)}, u32[]{:S(2)}) collective-permute-start(bf16[256,512]{1,0:T(8,128)(2,1)} %copy-done.18), channel_id=1, source_target_pairs={{0,2},{1,7},{2,4},{3,1},{4,6},{5,3},{6,0},{7,5},{8,10},{9,15},{10,... | collective-permute-start | bytes 786440 | tf_op jit(solution)/shard_map/ppermute | solution.py:29
  99.9 5.2 %collective-permute-start.7 = (bf16[256,512]{1,0:T(8,128)(2,1)}, bf16[256,512]{1,0:T(8,128)(2,1)S(1)}, u32[]{:S(2)}, u32[]{:S(2)}) collective-permute-start(bf16[256,512]{1,0:T(8,128)(2,1)} %copy-done.17), channel_id=1, source_target_pairs={{0,3},{1,6},{2,5},{3,0},{4,7},{5,2},{6,1},{7,4},{8,11},{9,14},{10,... | collective-permute-start | bytes 786440 | tf_op jit(solution)/shard_map/ppermute | solution.py:29
  105.1 14.9 %collective-permute-done.8.far = bf16[512,512]{1,0:T(8,128)(2,1)S(1)} collective-permute-done((bf16[512,512]{1,0:T(8,128)(2,1)S(1)}, bf16[512,512]{1,0:T(8,128)(2,1)S(1)}, u32[]{:S(2)}, u32[]{:S(2)}) %collective-permute-start.8) | collective-permute-done | bytes 524320 | tf_op jit(solution)/shard_map/ppermute | solution.py:29
  120.0 1.0 copy-done.13
  121.1 1.9 %collective-permute-start.10 = (bf16[256,512]{1,0:T(8,128)(2,1)S(1)}, bf16[256,512]{1,0:T(8,128)(2,1)S(1)}, u32[]{:S(2)}, u32[]{:S(2)}) collective-permute-start(bf16[256,512]{1,0:T(8,128)(2,1)S(1)} %shard_map.92), channel_id=1, source_target_pairs={{0,3},{1,6},{2,5},{3,0},{4,7},{5,2},{6,1},{7,4},{8,11},{9,14},{10,... | collective-permute-start | bytes 786440 | tf_op jit(solution)/shard_map/ppermute | solution.py:29
  123.1 5.1 %collective-permute-start.9 = (bf16[256,512]{1,0:T(8,128)(2,1)S(1)}, bf16[256,512]{1,0:T(8,128)(2,1)S(1)}, u32[]{:S(2)}, u32[]{:S(2)}) collective-permute-start(bf16[256,512]{1,0:T(8,128)(2,1)S(1)} %shard_map.91), channel_id=1, source_target_pairs={{0,2},{1,7},{2,4},{3,1},{4,6},{5,3},{6,0},{7,5},{8,10},{9,15},{10,... | collective-permute-start | bytes 786440 | tf_op jit(solution)/shard_map/ppermute | solution.py:29
  128.2 1.1 reduce_sum.9
  129.3 0.6 multiply_subtract_fusion
  130.0 0.4 collective-permute-done.6.near_a
  130.4 10.5 %collective-permute-done.7.near_b = bf16[256,512]{1,0:T(8,128)(2,1)S(1)} collective-permute-done((bf16[256,512]{1,0:T(8,128)(2,1)}, bf16[256,512]{1,0:T(8,128)(2,1)S(1)}, u32[]{:S(2)}, u32[]{:S(2)}) %collective-permute-start.7) | collective-permute-done | bytes 262176 | tf_op jit(solution)/shard_map/ppermute | solution.py:29
  141.0 12.8 %collective-permute-done.10.sum_b = bf16[256,512]{1,0:T(8,128)(2,1)S(1)} collective-permute-done((bf16[256,512]{1,0:T(8,128)(2,1)S(1)}, bf16[256,512]{1,0:T(8,128)(2,1)S(1)}, u32[]{:S(2)}, u32[]{:S(2)}) %collective-permute-start.10) | collective-permute-done | bytes 262176 | tf_op jit(solution)/shard_map/ppermute | solution.py:29
  153.8 1.7 %shard_map.93 = f32[512,512]{1,0:T(8,128)} custom-call(s32[3]{0:T(128)S(1)} %pad_add_fusion.place, f32[512,512]{1,0:T(8,128)S(1)} %get-tuple-element.25.base, bf16[256,512]{1,0:T(8,128)(2,1)S(1)} %collective-permute-done.6.near_a, bf16[256,512]{1,0:T(8,128)(2,1)S(1)} %collective-permute-done.7.near_b, bf16[256,512]{1,0:T(8,128)(2,1)S(1)} %collective-permute-done.9.sum_a, ...), custom_call_target="tpu_custom_call" | custom-call | tf_op jit(solution)/shard_map/pallas_call | solution.py:236
  (34 shorter events, 0.2 us)
Async XLA Ops:
  0.6 54.0 %collective-permute-start = (bf16[256,4096]{1,0:T(8,128)(2,1)}, bf16[256,4096]{1,0:T(8,128)(2,1)}, u32[]{:S(2)}, u32[]{:S(2)}) collective-permute-start(bf16[256,4096]{1,0:T(8,128)(2,1)} %own.1), channel_id=1, source_target_pairs={{0,1},{1,0},{2,3},{3,2},{4,5},{5,4},{6,7},{7,6},{8,9},{9,8},{10,11... | collective-permute-start | bytes 6291464 | tf_op jit(solution)/shard_map/ppermute | solution.py:166
  33.8 9.3 %copy-start.4 = (bf16[512,1024]{1,0:T(8,128)(2,1)S(1)}, bf16[512,1024]{1,0:T(8,128)(2,1)}, u32[]{:S(2)}) copy-start(bf16[512,1024]{1,0:T(8,128)(2,1)} %given.1) | copy-start | bytes 3145732
  33.8 36.0 %all-to-all-start = ((bf16[16,8,32,256]{3,2,1,0:T(8,128)(2,1)}), bf16[16,8,32,256]{3,2,1,0:T(8,128)(2,1)S(1)}, u32[]{:S(2)}, u32[]{:S(2)}) async-start(bf16[16,8,32,256]{3,2,1,0:T(8,128)(2,1)} %shard_map.86), calls=%async_computation | async-start | bytes 4194304 | tf_op jit(solution)/shard_map/all_to_all | solution.py:164
  40.7 13.9 %collective-permute-start.1 = (bf16[256,512]{1,0:T(8,128)(2,1)}, bf16[256,512]{1,0:T(8,128)(2,1)S(1)}, u32[]{:S(2)}, u32[]{:S(2)}) collective-permute-start(bf16[256,512]{1,0:T(8,128)(2,1)} %targets.1), channel_id=1, source_target_pairs={{0,1},{1,0},{2,3},{3,2},{4,5},{5,4},{6,7},{7,6},{8,9},{9,8},{10,11... | collective-permute-start | bytes 786440 | tf_op jit(solution)/shard_map/ppermute | solution.py:167
  44.7 0.7 copy-start.15
  45.4 32.1 %collective-permute-start.3 = (bf16[128,1024]{1,0:T(8,128)(2,1)}, bf16[128,1024]{1,0:T(8,128)(2,1)}, u32[]{:S(2)}, u32[]{:S(2)}) collective-permute-start(bf16[128,1024]{1,0:T(8,128)(2,1)} %get-tuple-element.21), channel_id=1, source_target_pairs={{0,8},{8,0},{16,24},{24,16},{1,9},{9,1},{17,25},{25,17},{2,10},{10... | collective-permute-start | bytes 786440 | tf_op jit(solution)/shard_map/ppermute | solution.py:191
  48.0 29.5 %collective-permute-start.4 = (bf16[128,1024]{1,0:T(8,128)(2,1)}, bf16[128,1024]{1,0:T(8,128)(2,1)}, u32[]{:S(2)}, u32[]{:S(2)}) collective-permute-start(bf16[128,1024]{1,0:T(8,128)(2,1)} %get-tuple-element.22), channel_id=1, source_target_pairs={{0,16},{8,24},{16,0},{24,8},{1,17},{9,25},{17,1},{25,9},{2,18},{10... | collective-permute-start | bytes 786440 | tf_op jit(solution)/shard_map/ppermute | solution.py:191
  51.1 26.4 %collective-permute-start.5 = (bf16[128,1024]{1,0:T(8,128)(2,1)}, bf16[128,1024]{1,0:T(8,128)(2,1)}, u32[]{:S(2)}, u32[]{:S(2)}) collective-permute-start(bf16[128,1024]{1,0:T(8,128)(2,1)} %get-tuple-element.23), channel_id=1, source_target_pairs={{0,24},{8,16},{16,8},{24,0},{1,25},{9,17},{17,9},{25,1},{2,26},{10... | collective-permute-start | bytes 786440 | tf_op jit(solution)/shard_map/ppermute | solution.py:191
  54.7 1.6 %copy-start.2 = (bf16[256,4096]{1,0:T(8,128)(2,1)S(1)}, bf16[256,4096]{1,0:T(8,128)(2,1)}, u32[]{:S(2)}) copy-start(bf16[256,4096]{1,0:T(8,128)(2,1)} %own.1) | copy-start | bytes 6291460
  56.3 0.9 copy-start.14
  59.7 2.1 %copy-start = (bf16[512,4352]{1,0:T(8,128)(2,1)}, bf16[512,4352]{1,0:T(8,128)(2,1)S(1)}, u32[]{:S(2)}) copy-start(bf16[512,4352]{1,0:T(8,128)(2,1)S(1)} %get-tuple-element.19.both) | copy-start | bytes 13369348
  61.7 0.8 copy-start.5
  62.5 0.8 copy-start.7
  69.9 2.3 %copy-start.1 = (bf16[512,4352]{1,0:T(8,128)(2,1)S(1)}, bf16[512,4352]{1,0:T(8,128)(2,1)}, u32[]{:S(2)}) copy-start(bf16[512,4352]{1,0:T(8,128)(2,1)} %copy-done) | copy-start | bytes 13369348
  72.1 6.5 %copy-start.8 = (bf16[2,256,512]{2,1,0:T(8,128)(2,1)S(1)}, bf16[2,256,512]{2,1,0:T(8,128)(2,1)}, u32[]{:S(2)}) copy-start(bf16[2,256,512]{2,1,0:T(8,128)(2,1)} %copy-done.7) | copy-start | bytes 1572868
  73.4 10.4 %copy-start.3 = (f32[512,512]{1,0:T(8,128)S(1)}, f32[512,512]{1,0:T(8,128)}, u32[]{:S(2)}) copy-start(f32[512,512]{1,0:T(8,128)} %w.1) | copy-start | bytes 3145732
  73.4 10.4 %copy-start.6 = (bf16[2,256,512]{2,1,0:T(8,128)(2,1)S(1)}, bf16[2,256,512]{2,1,0:T(8,128)(2,1)}, u32[]{:S(2)}) copy-start(bf16[2,256,512]{2,1,0:T(8,128)(2,1)} %copy-done.5) | copy-start | bytes 1572868
  73.4 10.4 %copy-start.16 = (bf16[128,1024]{1,0:T(8,128)(2,1)S(1)}, bf16[128,1024]{1,0:T(8,128)(2,1)}, u32[]{:S(2)}) copy-start(bf16[128,1024]{1,0:T(8,128)(2,1)} %copy-done.15) | copy-start | bytes 786436
  73.4 5.2 %collective-permute-start.2 = (bf16[512,256]{1,0:T(8,128)(2,1)S(1)}, bf16[512,256]{1,0:T(8,128)(2,1)S(1)}, u32[]{:S(2)}, u32[]{:S(2)}) collective-permute-start(bf16[512,256]{1,0:T(8,128)(2,1)S(1)} %shard_map.87.err_own), channel_id=1, source_target_pairs={{0,1},{1,0},{2,3},{3,2},{4,5},{5,4},{6,7},{7,6},{8,9},{9,8},{10,11... | collective-permute-start | bytes 786440 | tf_op jit(solution)/shard_map/ppermute | solution.py:200
  79.7 40.4 %collective-permute-start.8 = (bf16[512,512]{1,0:T(8,128)(2,1)S(1)}, bf16[512,512]{1,0:T(8,128)(2,1)S(1)}, u32[]{:S(2)}, u32[]{:S(2)}) collective-permute-start(bf16[512,512]{1,0:T(8,128)(2,1)S(1)} %shard_map.89.refs_4_), channel_id=1, source_target_pairs={{0,2},{1,7},{2,4},{3,1},{4,6},{5,3},{6,0},{7,5},{8,10},{9,15},{10,... | collective-permute-start | bytes 1572872 | tf_op jit(solution)/shard_map/ppermute | solution.py:29
  86.2 0.8 copy-start.10
  87.0 0.8 copy-start.12
  87.8 0.7 copy-start.17
  88.5 0.7 copy-start.18
  89.2 0.8 copy-start.9
  90.0 33.1 %copy-start.11 = (f32[256,512]{1,0:T(8,128)S(1)}, f32[256,512]{1,0:T(8,128)}, u32[]{:S(2)}) copy-start(f32[256,512]{1,0:T(8,128)} %copy-done.10) | copy-start | bytes 1572868
  90.0 39.4 %copy-start.19 = (f32[8,1024]{1,0:T(8,128)S(1)}, f32[8,1024]{1,0:T(8,128)}, u32[]{:S(2)}) copy-start(f32[8,1024]{1,0:T(8,128)} %param.9) | copy-start | bytes 98308
  90.0 39.4 %copy-start.20 = (f32[8,1024]{1,0:T(8,128)S(1)}, f32[8,1024]{1,0:T(8,128)}, u32[]{:S(2)}) copy-start(f32[8,1024]{1,0:T(8,128)} %param.11) | copy-start | bytes 98308
  90.0 38.3 %all-to-all-start.1 = ((f32[16,8,1024]{2,1,0:T(8,128)}), f32[16,8,1024]{2,1,0:T(8,128)}, u32[]{:S(2)}, u32[]{:S(2)}) async-start(f32[16,8,1024]{2,1,0:T(8,128)} %bitcast.4), calls=%async_computation.1 | async-start | bytes 1048576 | tf_op jit(solution)/shard_map/all_to_all | solution.py:244
  94.8 35.6 %collective-permute-start.6 = (bf16[256,512]{1,0:T(8,128)(2,1)}, bf16[256,512]{1,0:T(8,128)(2,1)S(1)}, u32[]{:S(2)}, u32[]{:S(2)}) collective-permute-start(bf16[256,512]{1,0:T(8,128)(2,1)} %copy-done.18), channel_id=1, source_target_pairs={{0,2},{1,7},{2,4},{3,1},{4,6},{5,3},{6,0},{7,5},{8,10},{9,15},{10,... | collective-permute-start | bytes 786440 | tf_op jit(solution)/shard_map/ppermute | solution.py:29
  99.9 41.1 %collective-permute-start.7 = (bf16[256,512]{1,0:T(8,128)(2,1)}, bf16[256,512]{1,0:T(8,128)(2,1)S(1)}, u32[]{:S(2)}, u32[]{:S(2)}) collective-permute-start(bf16[256,512]{1,0:T(8,128)(2,1)} %copy-done.17), channel_id=1, source_target_pairs={{0,3},{1,6},{2,5},{3,0},{4,7},{5,2},{6,1},{7,4},{8,11},{9,14},{10,... | collective-permute-start | bytes 786440 | tf_op jit(solution)/shard_map/ppermute | solution.py:29
  120.0 1.0 copy-start.13
  121.1 32.6 %collective-permute-start.10 = (bf16[256,512]{1,0:T(8,128)(2,1)S(1)}, bf16[256,512]{1,0:T(8,128)(2,1)S(1)}, u32[]{:S(2)}, u32[]{:S(2)}) collective-permute-start(bf16[256,512]{1,0:T(8,128)(2,1)S(1)} %shard_map.92), channel_id=1, source_target_pairs={{0,3},{1,6},{2,5},{3,0},{4,7},{5,2},{6,1},{7,4},{8,11},{9,14},{10,... | collective-permute-start | bytes 786440 | tf_op jit(solution)/shard_map/ppermute | solution.py:29
  123.1 30.6 %collective-permute-start.9 = (bf16[256,512]{1,0:T(8,128)(2,1)S(1)}, bf16[256,512]{1,0:T(8,128)(2,1)S(1)}, u32[]{:S(2)}, u32[]{:S(2)}) collective-permute-start(bf16[256,512]{1,0:T(8,128)(2,1)S(1)} %shard_map.91), channel_id=1, source_target_pairs={{0,2},{1,7},{2,4},{3,1},{4,6},{5,3},{6,0},{7,5},{8,10},{9,15},{10,... | collective-permute-start | bytes 786440 | tf_op jit(solution)/shard_map/ppermute | solution.py:29

commit v6 on v5

--- a/solution.py
+++ b/solution.py
@@ -54,14 +54,6 @@
             out[j, :, tokens:] = mate[:, columns].T
 
 
-def spread_kernel(place, column, out):
-    width = out.shape[3]
-    at = place[1] * width
-    part = column[:, pl.ds(pl.multiple_of(at, width), width)].reshape(out.shape[1:])
-    for i in range(out.shape[0]):
-        out[i] = part
-
-
 def error_kernel(both, w, out):
     shards, depth = w.shape[1], w.shape[0] * w.shape[2]
     tokens = both.shape[0] // 2
@@ -115,14 +107,18 @@
     out[...] = (via[...] + far[half * rows : (half + 1) * rows, :].astype(jnp.float32)).astype(out.dtype)
 
 
-def finish_kernel(place, base, near_a, near_b, sum_a, sum_b, out, *, rate):
+def fold_kernel(place, base, near_a, near_b, out, *, rate):
     rows = near_a.shape[0]
-    core = place[1]
-    for first, (plain, total) in ((True, (near_b, sum_a)), (False, (near_a, sum_b))):
-        half = core if first else 1 - core
+    for half, near in ((place[1], near_b), (1 - place[1], near_a)):
         at = pl.ds(pl.multiple_of(half * rows, rows), rows)
-        grad = plain[...].astype(jnp.float32) + total[...].astype(jnp.float32)
-        out[at, :] = base[at, :] - rate * grad
+        out[at, :] = base[at, :] - rate * near[...].astype(jnp.float32)
+
+
+def finish_kernel(place, base, sum_a, sum_b, out, *, rate):
+    rows = sum_a.shape[0]
+    for half, total in ((place[1], sum_a), (1 - place[1], sum_b)):
+        at = pl.ds(pl.multiple_of(half * rows, rows), rows)
+        out[at, :] = base[at, :] - rate * total[...].astype(jnp.float32)
 
 
 def sort_kernel(place, given, order, keep, one, two, three, held):
@@ -154,13 +150,8 @@
     piece = own_rows // spots
     mine = lax.dynamic_slice_in_dim(w_key, spot * piece, piece, 0).astype(jnp.bfloat16)
     column = lax.all_gather(mine, ("zh", "c"), axis=0, tiled=True)
-    copies = pl.pallas_call(
-        spread_kernel,
-        out_shape=jax.ShapeDtypeStruct((spots, ZH * 2, piece, half), jnp.bfloat16),
-        in_specs=[smem, vmem],
-        out_specs=vmem,
-        compiler_params=PARAMS,
-    )(place, column)
+    part = lax.dynamic_slice_in_dim(column, core * half, half, 1).reshape(ZH * 2, piece, half)
+    copies = jnp.broadcast_to(part[None], (spots,) + part.shape)
     key = lax.all_to_all(copies, ("x", "y"), 0, 0, tiled=True)
 
     mate = lax.ppermute(tokens, "c", SWAP)
@@ -233,13 +224,20 @@
 
     sum_a = round_z(passed(via_a, 0), 0)
     sum_b = round_z(passed(via_b, 1), 1)
+    base = pl.pallas_call(
+        functools.partial(fold_kernel, rate=rate),
+        out_shape=full,
+        in_specs=[smem] + [vmem] * 3,
+        out_specs=vmem,
+        compiler_params=PARAMS,
+    )(place, base, near_a, near_b)
     new_key = pl.pallas_call(
         functools.partial(finish_kernel, rate=rate),
         out_shape=full,
-        in_specs=[smem] + [vmem] * 5,
-        out_specs=vmem,
-        compiler_params=PARAMS,
-    )(place, base, near_a, near_b, sum_a, sum_b)
+        in_specs=[smem] + [vmem] * 3,
+        out_specs=vmem,
+        compiler_params=PARAMS,
+    )(place, base, sum_a, sum_b)
 
     part = lax.all_to_all(part.reshape(spots, owned, wide), ("x", "y"), 0, 0, tiled=True)
     mean = frag_outer - part.sum(0) / (spots * ZL)

time: 157 us -> 157 us (level)
  local copies, waits for them, and re-layouts: 14.8 us -> 16.5 us
    broadcast_in_dim x0 -> x1, local copies, waits for them, and re-layouts: none -> 1.62 us  [on_device(): copies = jnp.broadcast_to(part[None], (spots,) + part.shape)]
  transfers between devices with their start and end apart: 13 -> 13, of which waited for: 6 -> 6; matrix products, arithmetic and copies ran while one was open for 2% -> 3% of each run, Pallas kernels for 6% -> 5%
where the time goes in v6:
time: 157 us; the launch traced here: 155 us
  starting transfers between devices  58 us (37%)
  waiting for transfers between devices  45 us (29%)
  blocking collectives  21.4 us (14%)
  local copies, waits for them, and re-layouts  16.5 us (11%)
  Pallas kernels  11 us (7%)
  other arithmetic  1.79 us (1%)
    ppermute x5, waiting for transfers between devices, round_z(): return lax.ppermute(a, ('zh', 'c'), pairs)  37.4 us
    ppermute x5, starting transfers between devices, round_z(): return lax.ppermute(a, ('zh', 'c'), pairs)  21.7 us
    all_gather x1, blocking collectives, on_device(): column = lax.all_gather(mine, ('zh', 'c'), axis=0, tiled=True)  21.4 us
    unnamed x42, local copies, waits for them, and re-layouts  14 us
    ppermute x3, starting transfers between devices, on_device(): lax.ppermute(p, 'zl', [(i, i ^ j) for i in range(ZL)])  9.26 us
    ppermute x1, starting transfers between devices, on_device(): mate = lax.ppermute(tokens, 'c', SWAP)  8.79 us
    all_to_all x1, starting transfers between devices, on_device(): key = lax.all_to_all(copies, ('x', 'y'), 0, 0, tiled=True)  6.89 us
    all_to_all x1, waiting for transfers between devices, on_device(): key = lax.all_to_all(copies, ('x', 'y'), 0, 0, tiled=True)  6.47 us
  transfers between devices with their start and end apart: 13, of which 6 were waited for; matrix products, arithmetic and copies ran while one was open for 3% of the time, Pallas kernels for 5%

profile of v6, /device:TPU:1, one launch (start us, length us, event | category | flops | bytes accessed | tf_op | source)
XLA Modules:
  0.0 154.5 jit_solution(3792137328944171753)
XLA Ops:
  0.6 8.8 %collective-permute-start = (bf16[256,4096]{1,0:T(8,128)(2,1)}, bf16[256,4096]{1,0:T(8,128)(2,1)}, u32[]{:S(2)}, u32[]{:S(2)}) collective-permute-start(bf16[256,4096]{1,0:T(8,128)(2,1)} %own.1), channel_id=1, source_target_pairs={{0,1},{1,0},{2,3},{3,2},{4,5},{5,4},{6,7},{7,6},{8,9},{9,8},{10,11... | collective-permute-start | bytes 6291464 | tf_op jit(solution)/shard_map/ppermute | solution.py:157
  9.4 0.9 dynamic-slice_convert_fusion
  10.3 21.4 %all_gather.3.order = bf16[256,512]{1,0:T(8,128)(2,1)S(1)} all-gather(bf16[32,512]{1,0:T(8,128)(2,1)S(1)} %dynamic-slice_convert_fusion), channel_id=1, replica_groups=mesh['x'=4,'y'=4,'zl'=4,'zh'=4,'c'=2] {'zh','c'}, dimensions={0}, use_global_device_ids=true | all-gather | bytes 294912 | tf_op jit(solution)/shard_map/all_gather | solution.py:152
  31.7 1.6 %broadcast_in_dim.8 = bf16[16,8,32,256]{3,2,1,0:T(8,128)(2,1)} broadcast(bf16[8,32,256]{2,1,0:T(8,128)(2,1)S(1)} %bitcast.6), dimensions={1,2,3} | broadcast | bytes 2228224 | tf_op jit(solution)/shard_map/broadcast_in_dim | solution.py:154
  33.3 6.9 %all-to-all-start = ((bf16[16,8,32,256]{3,2,1,0:T(8,128)(2,1)}), bf16[16,8,32,256]{3,2,1,0:T(8,128)(2,1)S(1)}, u32[]{:S(2)}, u32[]{:S(2)}) async-start(bf16[16,8,32,256]{3,2,1,0:T(8,128)(2,1)} %broadcast_in_dim.8), calls=%async_computation | async-start | bytes 4194304 | tf_op jit(solution)/shard_map/all_to_all | solution.py:155
  40.2 2.4 %collective-permute-start.1 = (bf16[256,512]{1,0:T(8,128)(2,1)}, bf16[256,512]{1,0:T(8,128)(2,1)}, u32[]{:S(2)}, u32[]{:S(2)}) collective-permute-start(bf16[256,512]{1,0:T(8,128)(2,1)} %targets.1), channel_id=1, source_target_pairs={{0,1},{1,0},{2,3},{3,2},{4,5},{5,4},{6,7},{7,6},{8,9},{9,8},{10,11... | collective-permute-start | bytes 786440 | tf_op jit(solution)/shard_map/ppermute | solution.py:158
  42.5 0.1 pad_add_fusion.place
  42.6 1.6 %shard_map.87 = (bf16[128,1024]{1,0:T(8,128)(2,1)S(1)}, bf16[128,1024]{1,0:T(8,128)(2,1)}, bf16[128,1024]{1,0:T(8,128)(2,1)}, bf16[128,1024]{1,0:T(8,128)(2,1)}) custom-call(s32[3]{0:T(128)S(1)} %pad_add_fusion.place, bf16[512,1024]{1,0:T(8,128)(2,1)S(1)} %copy-done.4, bf16[256,512]{1,0:T(8,128)(2,1)S(1)} %all_gather.3.order), custom_call_target="tpu_custom_call" | custom-call | tf_op jit(solution)/shard_map/pallas_call | solution.py:174
  44.2 0.7 copy-done.15
  44.9 2.6 %collective-permute-start.3 = (bf16[128,1024]{1,0:T(8,128)(2,1)}, bf16[128,1024]{1,0:T(8,128)(2,1)}, u32[]{:S(2)}, u32[]{:S(2)}) collective-permute-start(bf16[128,1024]{1,0:T(8,128)(2,1)} %get-tuple-element.21), channel_id=1, source_target_pairs={{0,8},{8,0},{16,24},{24,16},{1,9},{9,1},{17,25},{25,17},{2,10},{10... | collective-permute-start | bytes 786440 | tf_op jit(solution)/shard_map/ppermute | solution.py:182
  47.5 3.1 %collective-permute-start.4 = (bf16[128,1024]{1,0:T(8,128)(2,1)}, bf16[128,1024]{1,0:T(8,128)(2,1)}, u32[]{:S(2)}, u32[]{:S(2)}) collective-permute-start(bf16[128,1024]{1,0:T(8,128)(2,1)} %get-tuple-element.22), channel_id=1, source_target_pairs={{0,16},{8,24},{16,0},{24,8},{1,17},{9,25},{17,1},{25,9},{2,18},{10... | collective-permute-start | bytes 786440 | tf_op jit(solution)/shard_map/ppermute | solution.py:182
  50.6 3.5 %collective-permute-start.5 = (bf16[128,1024]{1,0:T(8,128)(2,1)}, bf16[128,1024]{1,0:T(8,128)(2,1)}, u32[]{:S(2)}, u32[]{:S(2)}) collective-permute-start(bf16[128,1024]{1,0:T(8,128)(2,1)} %get-tuple-element.23), channel_id=1, source_target_pairs={{0,24},{8,16},{16,8},{24,0},{1,25},{9,17},{17,9},{25,1},{2,26},{10... | collective-permute-start | bytes 786440 | tf_op jit(solution)/shard_map/ppermute | solution.py:182
  54.2 0.0 copy-start.2
  54.2 1.6 %copy-done.2 = bf16[256,4096]{1,0:T(8,128)(2,1)S(1)} copy-done((bf16[256,4096]{1,0:T(8,128)(2,1)S(1)}, bf16[256,4096]{1,0:T(8,128)(2,1)}, u32[]{:S(2)}) %copy-start.2) | copy-done | bytes 2097176
  55.8 0.9 copy-done.14
  56.7 2.4 %shard_map.85 = (bf16[2,256,512]{2,1,0:T(8,128)(2,1)S(1)}, bf16[4,256,512]{2,1,0:T(8,128)(2,1)S(1)}, bf16[2,256,512]{2,1,0:T(8,128)(2,1)S(1)}, bf16[512,4352]{1,0:T(8,128)(2,1)S(1)}) custom-call(s32[3]{0:T(128)S(1)} %pad_add_fusion.place, bf16[256,4096]{1,0:T(8,128)(2,1)S(1)} %copy-done.2, bf16[256,512]{1,0:T(8,128)(2,1)S(1)} %copy-done.14, ...), custom_call_target="tpu_custom_call" | custom-call | bytes 16777216 | tf_op jit(solution)/shard_map/pallas_call | solution.py:163
  59.2 2.0 %copy-done = bf16[512,4352]{1,0:T(8,128)(2,1)} copy-done((bf16[512,4352]{1,0:T(8,128)(2,1)}, bf16[512,4352]{1,0:T(8,128)(2,1)S(1)}, u32[]{:S(2)}) %copy-start) | copy-done | bytes 4456472
  61.3 0.8 copy-done.5
  62.0 0.8 copy-done.7
  62.8 6.5 %all-to-all-done.w = bf16[16,8,32,256]{3,2,1,0:T(8,128)(2,1)S(1)} async-done(((bf16[16,8,32,256]{3,2,1,0:T(8,128)(2,1)}), bf16[16,8,32,256]{3,2,1,0:T(8,128)(2,1)S(1)}, u32[]{:S(2)}, u32[]{:S(2)}) %all-to-all-start) | async-done | bytes 2097184 | tf_op jit(solution)/shard_map/all_to_all | solution.py:155
  69.3 2.3 %copy-done.1 = bf16[512,4352]{1,0:T(8,128)(2,1)S(1)} copy-done((bf16[512,4352]{1,0:T(8,128)(2,1)S(1)}, bf16[512,4352]{1,0:T(8,128)(2,1)}, u32[]{:S(2)}) %copy-start.1) | copy-done | bytes 4456472
  71.6 1.2 shard_map.86.err_own
  72.8 0.0 copy-start.3
  72.8 0.0 copy-start.6
  72.9 4.1 %collective-permute-start.2 = (bf16[512,256]{1,0:T(8,128)(2,1)S(1)}, bf16[512,256]{1,0:T(8,128)(2,1)S(1)}, u32[]{:S(2)}, u32[]{:S(2)}) collective-permute-start(bf16[512,256]{1,0:T(8,128)(2,1)S(1)} %shard_map.86.err_own), channel_id=1, source_target_pairs={{0,1},{1,0},{2,3},{3,2},{4,5},{5,4},{6,7},{7,6},{8,9},{9,8},{10,11... | collective-permute-start | bytes 786440 | tf_op jit(solution)/shard_map/ppermute | solution.py:191
  77.0 1.1 collective-permute-done.2.err_mate
  78.1 1.0 shard_map.88.refs_4_
  79.1 4.1 %collective-permute-start.8 = (bf16[512,512]{1,0:T(8,128)(2,1)S(1)}, bf16[512,512]{1,0:T(8,128)(2,1)S(1)}, u32[]{:S(2)}, u32[]{:S(2)}) collective-permute-start(bf16[512,512]{1,0:T(8,128)(2,1)S(1)} %shard_map.88.refs_4_), channel_id=1, source_target_pairs={{0,2},{1,7},{2,4},{3,1},{4,6},{5,3},{6,0},{7,5},{8,10},{9,15},{10,... | collective-permute-start | bytes 1572872 | tf_op jit(solution)/shard_map/ppermute | solution.py:29
  83.2 2.4 %shard_map.89 = (f32[256,512]{1,0:T(8,128)S(1)}, bf16[256,512]{1,0:T(8,128)(2,1)S(1)}, f32[256,512]{1,0:T(8,128)S(1)}, bf16[256,512]{1,0:T(8,128)(2,1)S(1)}, f32...) custom-call(s32[3]{0:T(128)S(1)} %pad_add_fusion.place, bf16[4,256,512]{2,1,0:T(8,128)(2,1)S(1)} %get-tuple-element.17.xt, ...), custom_call_target="tpu_custom_call" | custom-call | tf_op jit(solution)/shard_map/pallas_call | solution.py:206
  85.6 0.8 copy-done.9
  86.4 0.8 copy-done.10
  87.2 0.8 copy-done.12
  88.0 0.7 copy-done.17
  88.7 0.7 copy-done.18
  89.4 4.8 %all-to-all-start.1 = ((f32[16,8,1024]{2,1,0:T(8,128)}), f32[16,8,1024]{2,1,0:T(8,128)}, u32[]{:S(2)}, u32[]{:S(2)}) async-start(f32[16,8,1024]{2,1,0:T(8,128)} %bitcast.5), calls=%async_computation.1 | async-start | bytes 1048576 | tf_op jit(solution)/shard_map/all_to_all | solution.py:242
  94.2 5.1 %collective-permute-start.6 = (bf16[256,512]{1,0:T(8,128)(2,1)}, bf16[256,512]{1,0:T(8,128)(2,1)S(1)}, u32[]{:S(2)}, u32[]{:S(2)}) collective-permute-start(bf16[256,512]{1,0:T(8,128)(2,1)} %copy-done.18), channel_id=1, source_target_pairs={{0,2},{1,7},{2,4},{3,1},{4,6},{5,3},{6,0},{7,5},{8,10},{9,15},{10,... | collective-permute-start | bytes 786440 | tf_op jit(solution)/shard_map/ppermute | solution.py:29
  99.3 5.2 %collective-permute-start.7 = (bf16[256,512]{1,0:T(8,128)(2,1)}, bf16[256,512]{1,0:T(8,128)(2,1)S(1)}, u32[]{:S(2)}, u32[]{:S(2)}) collective-permute-start(bf16[256,512]{1,0:T(8,128)(2,1)} %copy-done.17), channel_id=1, source_target_pairs={{0,3},{1,6},{2,5},{3,0},{4,7},{5,2},{6,1},{7,4},{8,11},{9,14},{10,... | collective-permute-start | bytes 786440 | tf_op jit(solution)/shard_map/ppermute | solution.py:29
  104.5 15.1 %collective-permute-done.8.far = bf16[512,512]{1,0:T(8,128)(2,1)S(1)} collective-permute-done((bf16[512,512]{1,0:T(8,128)(2,1)S(1)}, bf16[512,512]{1,0:T(8,128)(2,1)S(1)}, u32[]{:S(2)}, u32[]{:S(2)}) %collective-permute-start.8) | collective-permute-done | bytes 524320 | tf_op jit(solution)/shard_map/ppermute | solution.py:29
  119.7 1.0 copy-done.13
  120.7 1.9 %collective-permute-start.10 = (bf16[256,512]{1,0:T(8,128)(2,1)S(1)}, bf16[256,512]{1,0:T(8,128)(2,1)S(1)}, u32[]{:S(2)}, u32[]{:S(2)}) collective-permute-start(bf16[256,512]{1,0:T(8,128)(2,1)S(1)} %shard_map.92), channel_id=1, source_target_pairs={{0,3},{1,6},{2,5},{3,0},{4,7},{5,2},{6,1},{7,4},{8,11},{9,14},{10,... | collective-permute-start | bytes 786440 | tf_op jit(solution)/shard_map/ppermute | solution.py:29
  122.8 5.4 %collective-permute-start.9 = (bf16[256,512]{1,0:T(8,128)(2,1)S(1)}, bf16[256,512]{1,0:T(8,128)(2,1)S(1)}, u32[]{:S(2)}, u32[]{:S(2)}) collective-permute-start(bf16[256,512]{1,0:T(8,128)(2,1)S(1)} %shard_map.91), channel_id=1, source_target_pairs={{0,2},{1,7},{2,4},{3,1},{4,6},{5,3},{6,0},{7,5},{8,10},{9,15},{10,... | collective-permute-start | bytes 786440 | tf_op jit(solution)/shard_map/ppermute | solution.py:29
  128.2 1.6 %collective-permute-done.6.near_a = bf16[256,512]{1,0:T(8,128)(2,1)S(1)} collective-permute-done((bf16[256,512]{1,0:T(8,128)(2,1)}, bf16[256,512]{1,0:T(8,128)(2,1)S(1)}, u32[]{:S(2)}, u32[]{:S(2)}) %collective-permute-start.6) | collective-permute-done | bytes 262176 | tf_op jit(solution)/shard_map/ppermute | solution.py:29
  129.8 17.1 %collective-permute-done.7.near_b = bf16[256,512]{1,0:T(8,128)(2,1)S(1)} collective-permute-done((bf16[256,512]{1,0:T(8,128)(2,1)}, bf16[256,512]{1,0:T(8,128)(2,1)S(1)}, u32[]{:S(2)}, u32[]{:S(2)}) %collective-permute-start.7) | collective-permute-done | bytes 262176 | tf_op jit(solution)/shard_map/ppermute | solution.py:29
  146.9 0.7 shard_map.90.base
  147.6 1.1 reduce_sum.9
  148.7 0.6 multiply_subtract_fusion
  149.3 3.6 %collective-permute-done.10.sum_b = bf16[256,512]{1,0:T(8,128)(2,1)S(1)} collective-permute-done((bf16[256,512]{1,0:T(8,128)(2,1)S(1)}, bf16[256,512]{1,0:T(8,128)(2,1)S(1)}, u32[]{:S(2)}, u32[]{:S(2)}) %collective-permute-start.10) | collective-permute-done | bytes 262176 | tf_op jit(solution)/shard_map/ppermute | solution.py:29
  152.9 1.6 %shard_map.93 = f32[512,512]{1,0:T(8,128)} custom-call(s32[3]{0:T(128)S(1)} %pad_add_fusion.place, f32[512,512]{1,0:T(8,128)S(1)} %shard_map.90.base, bf16[256,512]{1,0:T(8,128)(2,1)S(1)} %collective-permute-done.9.sum_a, bf16[256,512]{1,0:T(8,128)(2,1)S(1)} %collective-permute-done.10.sum_b), custom_call_target="tpu_custom_call" | custom-call | tf_op jit(solution)/shard_map/pallas_call | solution.py:234
  (36 shorter events, 0.2 us)
Async XLA Ops:
  0.6 53.6 %collective-permute-start = (bf16[256,4096]{1,0:T(8,128)(2,1)}, bf16[256,4096]{1,0:T(8,128)(2,1)}, u32[]{:S(2)}, u32[]{:S(2)}) collective-permute-start(bf16[256,4096]{1,0:T(8,128)(2,1)} %own.1), channel_id=1, source_target_pairs={{0,1},{1,0},{2,3},{3,2},{4,5},{5,4},{6,7},{7,6},{8,9},{9,8},{10,11... | collective-permute-start | bytes 6291464 | tf_op jit(solution)/shard_map/ppermute | solution.py:157
  33.3 9.3 %copy-start.4 = (bf16[512,1024]{1,0:T(8,128)(2,1)S(1)}, bf16[512,1024]{1,0:T(8,128)(2,1)}, u32[]{:S(2)}) copy-start(bf16[512,1024]{1,0:T(8,128)(2,1)} %given.1) | copy-start | bytes 3145732
  33.3 36.0 %all-to-all-start = ((bf16[16,8,32,256]{3,2,1,0:T(8,128)(2,1)}), bf16[16,8,32,256]{3,2,1,0:T(8,128)(2,1)S(1)}, u32[]{:S(2)}, u32[]{:S(2)}) async-start(bf16[16,8,32,256]{3,2,1,0:T(8,128)(2,1)} %broadcast_in_dim.8), calls=%async_computation | async-start | bytes 4194304 | tf_op jit(solution)/shard_map/all_to_all | solution.py:155
  40.2 14.0 %collective-permute-start.1 = (bf16[256,512]{1,0:T(8,128)(2,1)}, bf16[256,512]{1,0:T(8,128)(2,1)}, u32[]{:S(2)}, u32[]{:S(2)}) collective-permute-start(bf16[256,512]{1,0:T(8,128)(2,1)} %targets.1), channel_id=1, source_target_pairs={{0,1},{1,0},{2,3},{3,2},{4,5},{5,4},{6,7},{7,6},{8,9},{9,8},{10,11... | collective-permute-start | bytes 786440 | tf_op jit(solution)/shard_map/ppermute | solution.py:158
  44.2 0.7 copy-start.15
  44.9 32.1 %collective-permute-start.3 = (bf16[128,1024]{1,0:T(8,128)(2,1)}, bf16[128,1024]{1,0:T(8,128)(2,1)}, u32[]{:S(2)}, u32[]{:S(2)}) collective-permute-start(bf16[128,1024]{1,0:T(8,128)(2,1)} %get-tuple-element.21), channel_id=1, source_target_pairs={{0,8},{8,0},{16,24},{24,16},{1,9},{9,1},{17,25},{25,17},{2,10},{10... | collective-permute-start | bytes 786440 | tf_op jit(solution)/shard_map/ppermute | solution.py:182
  47.5 29.4 %collective-permute-start.4 = (bf16[128,1024]{1,0:T(8,128)(2,1)}, bf16[128,1024]{1,0:T(8,128)(2,1)}, u32[]{:S(2)}, u32[]{:S(2)}) collective-permute-start(bf16[128,1024]{1,0:T(8,128)(2,1)} %get-tuple-element.22), channel_id=1, source_target_pairs={{0,16},{8,24},{16,0},{24,8},{1,17},{9,25},{17,1},{25,9},{2,18},{10... | collective-permute-start | bytes 786440 | tf_op jit(solution)/shard_map/ppermute | solution.py:182
  50.6 26.4 %collective-permute-start.5 = (bf16[128,1024]{1,0:T(8,128)(2,1)}, bf16[128,1024]{1,0:T(8,128)(2,1)}, u32[]{:S(2)}, u32[]{:S(2)}) collective-permute-start(bf16[128,1024]{1,0:T(8,128)(2,1)} %get-tuple-element.23), channel_id=1, source_target_pairs={{0,24},{8,16},{16,8},{24,0},{1,25},{9,17},{17,9},{25,1},{2,26},{10... | collective-permute-start | bytes 786440 | tf_op jit(solution)/shard_map/ppermute | solution.py:182
  54.2 1.6 %copy-start.2 = (bf16[256,4096]{1,0:T(8,128)(2,1)S(1)}, bf16[256,4096]{1,0:T(8,128)(2,1)}, u32[]{:S(2)}) copy-start(bf16[256,4096]{1,0:T(8,128)(2,1)} %own.1) | copy-start | bytes 6291460
  55.8 0.9 copy-start.14
  59.2 2.1 %copy-start = (bf16[512,4352]{1,0:T(8,128)(2,1)}, bf16[512,4352]{1,0:T(8,128)(2,1)S(1)}, u32[]{:S(2)}) copy-start(bf16[512,4352]{1,0:T(8,128)(2,1)S(1)} %get-tuple-element.19.both) | copy-start | bytes 13369348
  61.3 0.8 copy-start.5
  62.0 0.8 copy-start.7
  69.3 2.3 %copy-start.1 = (bf16[512,4352]{1,0:T(8,128)(2,1)S(1)}, bf16[512,4352]{1,0:T(8,128)(2,1)}, u32[]{:S(2)}) copy-start(bf16[512,4352]{1,0:T(8,128)(2,1)} %copy-done) | copy-start | bytes 13369348
  71.6 6.5 %copy-start.8 = (bf16[2,256,512]{2,1,0:T(8,128)(2,1)S(1)}, bf16[2,256,512]{2,1,0:T(8,128)(2,1)}, u32[]{:S(2)}) copy-start(bf16[2,256,512]{2,1,0:T(8,128)(2,1)} %copy-done.7) | copy-start | bytes 1572868
  72.8 10.4 %copy-start.3 = (f32[512,512]{1,0:T(8,128)S(1)}, f32[512,512]{1,0:T(8,128)}, u32[]{:S(2)}) copy-start(f32[512,512]{1,0:T(8,128)} %w.1) | copy-start | bytes 3145732
  72.8 10.4 %copy-start.6 = (bf16[2,256,512]{2,1,0:T(8,128)(2,1)S(1)}, bf16[2,256,512]{2,1,0:T(8,128)(2,1)}, u32[]{:S(2)}) copy-start(bf16[2,256,512]{2,1,0:T(8,128)(2,1)} %copy-done.5) | copy-start | bytes 1572868
  72.9 10.4 %copy-start.16 = (bf16[128,1024]{1,0:T(8,128)(2,1)S(1)}, bf16[128,1024]{1,0:T(8,128)(2,1)}, u32[]{:S(2)}) copy-start(bf16[128,1024]{1,0:T(8,128)(2,1)} %copy-done.15) | copy-start | bytes 786436
  72.9 5.2 %collective-permute-start.2 = (bf16[512,256]{1,0:T(8,128)(2,1)S(1)}, bf16[512,256]{1,0:T(8,128)(2,1)S(1)}, u32[]{:S(2)}, u32[]{:S(2)}) collective-permute-start(bf16[512,256]{1,0:T(8,128)(2,1)S(1)} %shard_map.86.err_own), channel_id=1, source_target_pairs={{0,1},{1,0},{2,3},{3,2},{4,5},{5,4},{6,7},{7,6},{8,9},{9,8},{10,11... | collective-permute-start | bytes 786440 | tf_op jit(solution)/shard_map/ppermute | solution.py:191
  79.1 40.5 %collective-permute-start.8 = (bf16[512,512]{1,0:T(8,128)(2,1)S(1)}, bf16[512,512]{1,0:T(8,128)(2,1)S(1)}, u32[]{:S(2)}, u32[]{:S(2)}) collective-permute-start(bf16[512,512]{1,0:T(8,128)(2,1)S(1)} %shard_map.88.refs_4_), channel_id=1, source_target_pairs={{0,2},{1,7},{2,4},{3,1},{4,6},{5,3},{6,0},{7,5},{8,10},{9,15},{10,... | collective-permute-start | bytes 1572872 | tf_op jit(solution)/shard_map/ppermute | solution.py:29
  85.6 0.8 copy-start.9
  86.4 0.8 copy-start.10
  87.2 0.8 copy-start.12
  88.0 0.7 copy-start.17
  88.7 0.7 copy-start.18
  89.4 33.3 %copy-start.11 = (f32[256,512]{1,0:T(8,128)S(1)}, f32[256,512]{1,0:T(8,128)}, u32[]{:S(2)}) copy-start(f32[256,512]{1,0:T(8,128)} %copy-done.10) | copy-start | bytes 1572868
  89.4 58.2 %all-to-all-start.1 = ((f32[16,8,1024]{2,1,0:T(8,128)}), f32[16,8,1024]{2,1,0:T(8,128)}, u32[]{:S(2)}, u32[]{:S(2)}) async-start(f32[16,8,1024]{2,1,0:T(8,128)} %bitcast.5), calls=%async_computation.1 | async-start | bytes 1048576 | tf_op jit(solution)/shard_map/all_to_all | solution.py:242
  94.2 35.6 %collective-permute-start.6 = (bf16[256,512]{1,0:T(8,128)(2,1)}, bf16[256,512]{1,0:T(8,128)(2,1)S(1)}, u32[]{:S(2)}, u32[]{:S(2)}) collective-permute-start(bf16[256,512]{1,0:T(8,128)(2,1)} %copy-done.18), channel_id=1, source_target_pairs={{0,2},{1,7},{2,4},{3,1},{4,6},{5,3},{6,0},{7,5},{8,10},{9,15},{10,... | collective-permute-start | bytes 786440 | tf_op jit(solution)/shard_map/ppermute | solution.py:29
  99.3 47.6 %collective-permute-start.7 = (bf16[256,512]{1,0:T(8,128)(2,1)}, bf16[256,512]{1,0:T(8,128)(2,1)S(1)}, u32[]{:S(2)}, u32[]{:S(2)}) collective-permute-start(bf16[256,512]{1,0:T(8,128)(2,1)} %copy-done.17), channel_id=1, source_target_pairs={{0,3},{1,6},{2,5},{3,0},{4,7},{5,2},{6,1},{7,4},{8,11},{9,14},{10,... | collective-permute-start | bytes 786440 | tf_op jit(solution)/shard_map/ppermute | solution.py:29
  119.6 1.0 copy-start.13
  120.7 32.2 %collective-permute-start.10 = (bf16[256,512]{1,0:T(8,128)(2,1)S(1)}, bf16[256,512]{1,0:T(8,128)(2,1)S(1)}, u32[]{:S(2)}, u32[]{:S(2)}) collective-permute-start(bf16[256,512]{1,0:T(8,128)(2,1)S(1)} %shard_map.92), channel_id=1, source_target_pairs={{0,3},{1,6},{2,5},{3,0},{4,7},{5,2},{6,1},{7,4},{8,11},{9,14},{10,... | collective-permute-start | bytes 786440 | tf_op jit(solution)/shard_map/ppermute | solution.py:29
  122.7 26.0 %copy-start.19 = (f32[8,1024]{1,0:T(8,128)S(1)}, f32[8,1024]{1,0:T(8,128)}, u32[]{:S(2)}) copy-start(f32[8,1024]{1,0:T(8,128)} %param.9) | copy-start | bytes 98308
  122.7 26.0 %copy-start.20 = (f32[8,1024]{1,0:T(8,128)S(1)}, f32[8,1024]{1,0:T(8,128)}, u32[]{:S(2)}) copy-start(f32[8,1024]{1,0:T(8,128)} %param.11) | copy-start | bytes 98308
  122.8 30.2 %collective-permute-start.9 = (bf16[256,512]{1,0:T(8,128)(2,1)S(1)}, bf16[256,512]{1,0:T(8,128)(2,1)S(1)}, u32[]{:S(2)}, u32[]{:S(2)}) collective-permute-start(bf16[256,512]{1,0:T(8,128)(2,1)S(1)} %shard_map.91), channel_id=1, source_target_pairs={{0,2},{1,7},{2,4},{3,1},{4,6},{5,3},{6,0},{7,5},{8,10},{9,15},{10,... | collective-permute-start | bytes 786440 | tf_op jit(solution)/shard_map/ppermute | solution.py:29

commit v7 on v6

--- a/solution.py
+++ b/solution.py
@@ -22,11 +22,12 @@
 
 def round_z(a, cross):
     pairs = []
-    for zh in range(ZH):
-        for core in range(2):
-            there = (zh + 1 - 2 * core) % ZH
-            pairs.append((zh * 2 + core, there * 2 + (core ^ cross)))
-    return lax.ppermute(a, ("zh", "c"), pairs)
+    for zl in range(ZL):
+        for zh in range(ZH):
+            for core in range(2):
+                there = (zh + 1 - 2 * (core ^ (zl & 1))) % ZH
+                pairs.append(((zl * ZH + zh) * 2 + core, (zl * ZH + there) * 2 + (core ^ cross)))
+    return lax.ppermute(a, ("zl", "zh", "c"), pairs)
 
 
 def transpose_kernel(place, own, targets, mate, goal, order, far_xt, near_xt, own_xt, both):
@@ -42,7 +43,7 @@
     both[:tokens, deep:] = targets[:, columns]
     both[tokens:, deep:] = goal[:, columns]
     far = lax.rem(zh + 2, ZH)
-    near = lax.rem(zh + 1 + 2 * core, ZH)
+    near = lax.rem(zh + 1 + 2 * (core ^ (place[2] & 1)), ZH)
     for out, places in (
         (far_xt, ((far, core, core), (far, other, core))),
         (near_xt, ((near, core, core), (near, core, other), (near, other, core), (near, other, other))),

time: 157 us -> 157 us (level)
  the two profiles are of different devices: /device:TPU:1 before, /device:TPU:33 now
where the time goes in v7:
time: 157 us; the launch traced here: 156 us
  starting transfers between devices  59.2 us (38%)
  waiting for transfers between devices  40.5 us (26%)
  blocking collectives  25.8 us (16%)
  local copies, waits for them, and re-layouts  16.4 us (10%)
  Pallas kernels  11 us (7%)
  other arithmetic  1.79 us (1%)
    ppermute x5, waiting for transfers between devices, round_z(): return lax.ppermute(a, ('zl', 'zh', 'c'), pairs)  32 us
    ppermute x5, starting transfers between devices, round_z(): return lax.ppermute(a, ('zl', 'zh', 'c'), pairs)  30.1 us
    all_gather x1, blocking collectives, on_device(): column = lax.all_gather(mine, ('zh', 'c'), axis=0, tiled=True)  25.8 us
    unnamed x42, local copies, waits for them, and re-layouts  14 us
    ppermute x3, starting transfers between devices, on_device(): lax.ppermute(p, 'zl', [(i, i ^ j) for i in range(ZL)])  8.36 us
    all_to_all x1, waiting for transfers between devices, on_device(): key = lax.all_to_all(copies, ('x', 'y'), 0, 0, tiled=True)  7.37 us
    all_to_all x1, starting transfers between devices, on_device(): key = lax.all_to_all(copies, ('x', 'y'), 0, 0, tiled=True)  6.89 us
    all_to_all x1, starting transfers between devices, on_device(): lax.all_to_all(part.reshape(spots, owned, wide), ('x', 'y'), 0, 0, tiled=...  4.85 us
  transfers between devices with their start and end apart: 13, of which 5 were waited for; matrix products, arithmetic and copies ran while one was open for 3% of the time, Pallas kernels for 5%

profile of v7, /device:TPU:33, one launch (start us, length us, event | category | flops | bytes accessed | tf_op | source)
XLA Modules:
  0.0 155.7 jit_solution(12719744421326658563)
XLA Ops:
  0.6 2.6 %collective-permute-start = (bf16[256,4096]{1,0:T(8,128)(2,1)}, bf16[256,4096]{1,0:T(8,128)(2,1)}, u32[]{:S(2)}, u32[]{:S(2)}) collective-permute-start(bf16[256,4096]{1,0:T(8,128)(2,1)} %own.1), channel_id=1, source_target_pairs={{0,1},{1,0},{2,3},{3,2},{4,5},{5,4},{6,7},{7,6},{8,9},{9,8},{10,11... | collective-permute-start | bytes 6291464 | tf_op jit(solution)/shard_map/ppermute | solution.py:158
  3.2 0.9 dynamic-slice_convert_fusion
  4.1 25.8 %all_gather.3.order = bf16[256,512]{1,0:T(8,128)(2,1)S(1)} all-gather(bf16[32,512]{1,0:T(8,128)(2,1)S(1)} %dynamic-slice_convert_fusion), channel_id=1, replica_groups=mesh['x'=4,'y'=4,'zl'=4,'zh'=4,'c'=2] {'zh','c'}, dimensions={0}, use_global_device_ids=true | all-gather | bytes 294912 | tf_op jit(solution)/shard_map/all_gather | solution.py:153
  29.9 1.6 %broadcast_in_dim.8 = bf16[16,8,32,256]{3,2,1,0:T(8,128)(2,1)} broadcast(bf16[8,32,256]{2,1,0:T(8,128)(2,1)S(1)} %bitcast.6), dimensions={1,2,3} | broadcast | bytes 2228224 | tf_op jit(solution)/shard_map/broadcast_in_dim | solution.py:155
  31.5 6.9 %all-to-all-start = ((bf16[16,8,32,256]{3,2,1,0:T(8,128)(2,1)}), bf16[16,8,32,256]{3,2,1,0:T(8,128)(2,1)S(1)}, u32[]{:S(2)}, u32[]{:S(2)}) async-start(bf16[16,8,32,256]{3,2,1,0:T(8,128)(2,1)} %broadcast_in_dim.8), calls=%async_computation | async-start | bytes 4194304 | tf_op jit(solution)/shard_map/all_to_all | solution.py:156
  38.4 2.4 %collective-permute-start.1 = (bf16[256,512]{1,0:T(8,128)(2,1)}, bf16[256,512]{1,0:T(8,128)(2,1)}, u32[]{:S(2)}, u32[]{:S(2)}) collective-permute-start(bf16[256,512]{1,0:T(8,128)(2,1)} %targets.1), channel_id=1, source_target_pairs={{0,1},{1,0},{2,3},{3,2},{4,5},{5,4},{6,7},{7,6},{8,9},{9,8},{10,11... | collective-permute-start | bytes 786440 | tf_op jit(solution)/shard_map/ppermute | solution.py:159
  40.8 0.1 pad_add_fusion.place
  40.9 1.6 %shard_map.87 = (bf16[128,1024]{1,0:T(8,128)(2,1)S(1)}, bf16[128,1024]{1,0:T(8,128)(2,1)}, bf16[128,1024]{1,0:T(8,128)(2,1)}, bf16[128,1024]{1,0:T(8,128)(2,1)}) custom-call(s32[3]{0:T(128)S(1)} %pad_add_fusion.place, bf16[512,1024]{1,0:T(8,128)(2,1)S(1)} %copy-done.4, bf16[256,512]{1,0:T(8,128)(2,1)S(1)} %all_gather.3.order), custom_call_target="tpu_custom_call" | custom-call | tf_op jit(solution)/shard_map/pallas_call | solution.py:175
  42.5 0.7 copy-done.15
  43.2 2.6 %collective-permute-start.3 = (bf16[128,1024]{1,0:T(8,128)(2,1)}, bf16[128,1024]{1,0:T(8,128)(2,1)}, u32[]{:S(2)}, u32[]{:S(2)}) collective-permute-start(bf16[128,1024]{1,0:T(8,128)(2,1)} %get-tuple-element.21), channel_id=1, source_target_pairs={{0,8},{8,0},{16,24},{24,16},{1,9},{9,1},{17,25},{25,17},{2,10},{10... | collective-permute-start | bytes 786440 | tf_op jit(solution)/shard_map/ppermute | solution.py:183
  45.8 3.2 %collective-permute-start.4 = (bf16[128,1024]{1,0:T(8,128)(2,1)}, bf16[128,1024]{1,0:T(8,128)(2,1)}, u32[]{:S(2)}, u32[]{:S(2)}) collective-permute-start(bf16[128,1024]{1,0:T(8,128)(2,1)} %get-tuple-element.22), channel_id=1, source_target_pairs={{0,16},{8,24},{16,0},{24,8},{1,17},{9,25},{17,1},{25,9},{2,18},{10... | collective-permute-start | bytes 786440 | tf_op jit(solution)/shard_map/ppermute | solution.py:183
  49.0 2.5 %collective-permute-start.5 = (bf16[128,1024]{1,0:T(8,128)(2,1)}, bf16[128,1024]{1,0:T(8,128)(2,1)}, u32[]{:S(2)}, u32[]{:S(2)}) collective-permute-start(bf16[128,1024]{1,0:T(8,128)(2,1)} %get-tuple-element.23), channel_id=1, source_target_pairs={{0,24},{8,16},{16,8},{24,0},{1,25},{9,17},{17,9},{25,1},{2,26},{10... | collective-permute-start | bytes 786440 | tf_op jit(solution)/shard_map/ppermute | solution.py:183
  51.6 0.0 copy-start.2
  51.6 1.6 %copy-done.2 = bf16[256,4096]{1,0:T(8,128)(2,1)S(1)} copy-done((bf16[256,4096]{1,0:T(8,128)(2,1)S(1)}, bf16[256,4096]{1,0:T(8,128)(2,1)}, u32[]{:S(2)}) %copy-start.2) | copy-done | bytes 2097176
  53.2 0.9 copy-done.14
  54.1 2.4 %shard_map.85 = (bf16[2,256,512]{2,1,0:T(8,128)(2,1)S(1)}, bf16[4,256,512]{2,1,0:T(8,128)(2,1)S(1)}, bf16[2,256,512]{2,1,0:T(8,128)(2,1)S(1)}, bf16[512,4352]{1,0:T(8,128)(2,1)S(1)}) custom-call(s32[3]{0:T(128)S(1)} %pad_add_fusion.place, bf16[256,4096]{1,0:T(8,128)(2,1)S(1)} %copy-done.2, bf16[256,512]{1,0:T(8,128)(2,1)S(1)} %copy-done.14, ...), custom_call_target="tpu_custom_call" | custom-call | bytes 16777216 | tf_op jit(solution)/shard_map/pallas_call | solution.py:164
  56.6 2.0 %copy-done = bf16[512,4352]{1,0:T(8,128)(2,1)} copy-done((bf16[512,4352]{1,0:T(8,128)(2,1)}, bf16[512,4352]{1,0:T(8,128)(2,1)S(1)}, u32[]{:S(2)}) %copy-start) | copy-done | bytes 4456472
  58.6 0.8 copy-done.5
  59.4 0.8 copy-done.7
  60.2 7.4 %all-to-all-done.w = bf16[16,8,32,256]{3,2,1,0:T(8,128)(2,1)S(1)} async-done(((bf16[16,8,32,256]{3,2,1,0:T(8,128)(2,1)}), bf16[16,8,32,256]{3,2,1,0:T(8,128)(2,1)S(1)}, u32[]{:S(2)}, u32[]{:S(2)}) %all-to-all-start) | async-done | bytes 2097184 | tf_op jit(solution)/shard_map/all_to_all | solution.py:156
  67.6 2.3 %copy-done.1 = bf16[512,4352]{1,0:T(8,128)(2,1)S(1)} copy-done((bf16[512,4352]{1,0:T(8,128)(2,1)S(1)}, bf16[512,4352]{1,0:T(8,128)(2,1)}, u32[]{:S(2)}) %copy-start.1) | copy-done | bytes 4456472
  69.8 1.2 shard_map.86.err_own
  71.1 0.0 copy-start.3
  71.1 0.0 copy-start.6
  71.1 4.1 %collective-permute-start.2 = (bf16[512,256]{1,0:T(8,128)(2,1)S(1)}, bf16[512,256]{1,0:T(8,128)(2,1)S(1)}, u32[]{:S(2)}, u32[]{:S(2)}) collective-permute-start(bf16[512,256]{1,0:T(8,128)(2,1)S(1)} %shard_map.86.err_own), channel_id=1, source_target_pairs={{0,1},{1,0},{2,3},{3,2},{4,5},{5,4},{6,7},{7,6},{8,9},{9,8},{10,11... | collective-permute-start | bytes 786440 | tf_op jit(solution)/shard_map/ppermute | solution.py:192
  75.3 1.1 collective-permute-done.2.err_mate
  76.4 1.0 shard_map.88.refs_4_
  77.4 3.9 %collective-permute-start.8 = (bf16[512,512]{1,0:T(8,128)(2,1)S(1)}, bf16[512,512]{1,0:T(8,128)(2,1)S(1)}, u32[]{:S(2)}, u32[]{:S(2)}) collective-permute-start(bf16[512,512]{1,0:T(8,128)(2,1)S(1)} %shard_map.88.refs_4_), channel_id=1, source_target_pairs={{0,2},{1,7},{2,4},{3,1},{4,6},{5,3},{6,0},{7,5},{8,14},{9,11},{10,... | collective-permute-start | bytes 1572872 | tf_op jit(solution)/shard_map/ppermute | solution.py:30
  81.4 2.4 %shard_map.89 = (f32[256,512]{1,0:T(8,128)S(1)}, bf16[256,512]{1,0:T(8,128)(2,1)S(1)}, f32[256,512]{1,0:T(8,128)S(1)}, bf16[256,512]{1,0:T(8,128)(2,1)S(1)}, f32...) custom-call(s32[3]{0:T(128)S(1)} %pad_add_fusion.place, bf16[4,256,512]{2,1,0:T(8,128)(2,1)S(1)} %get-tuple-element.17.xt, ...), custom_call_target="tpu_custom_call" | custom-call | tf_op jit(solution)/shard_map/pallas_call | solution.py:207
  83.7 0.8 copy-done.9
  84.5 0.8 copy-done.10
  85.3 0.8 copy-done.12
  86.1 0.7 copy-done.17
  86.8 0.7 copy-done.18
  87.5 4.8 %all-to-all-start.1 = ((f32[16,8,1024]{2,1,0:T(8,128)}), f32[16,8,1024]{2,1,0:T(8,128)}, u32[]{:S(2)}, u32[]{:S(2)}) async-start(f32[16,8,1024]{2,1,0:T(8,128)} %bitcast.5), calls=%async_computation.1 | async-start | bytes 1048576 | tf_op jit(solution)/shard_map/all_to_all | solution.py:243
  92.4 5.2 %collective-permute-start.6 = (bf16[256,512]{1,0:T(8,128)(2,1)}, bf16[256,512]{1,0:T(8,128)(2,1)S(1)}, u32[]{:S(2)}, u32[]{:S(2)}) collective-permute-start(bf16[256,512]{1,0:T(8,128)(2,1)} %copy-done.18), channel_id=1, source_target_pairs={{0,2},{1,7},{2,4},{3,1},{4,6},{5,3},{6,0},{7,5},{8,14},{9,11},{10,... | collective-permute-start | bytes 786440 | tf_op jit(solution)/shard_map/ppermute | solution.py:30
  97.6 5.0 %collective-permute-start.7 = (bf16[256,512]{1,0:T(8,128)(2,1)}, bf16[256,512]{1,0:T(8,128)(2,1)S(1)}, u32[]{:S(2)}, u32[]{:S(2)}) collective-permute-start(bf16[256,512]{1,0:T(8,128)(2,1)} %copy-done.17), channel_id=1, source_target_pairs={{0,3},{1,6},{2,5},{3,0},{4,7},{5,2},{6,1},{7,4},{8,15},{9,10},{10,... | collective-permute-start | bytes 786440 | tf_op jit(solution)/shard_map/ppermute | solution.py:30
  102.7 1.0 copy-done.13
  103.8 11.6 %collective-permute-start.10 = (bf16[256,512]{1,0:T(8,128)(2,1)S(1)}, bf16[256,512]{1,0:T(8,128)(2,1)S(1)}, u32[]{:S(2)}, u32[]{:S(2)}) collective-permute-start(bf16[256,512]{1,0:T(8,128)(2,1)S(1)} %shard_map.92), channel_id=1, source_target_pairs={{0,3},{1,6},{2,5},{3,0},{4,7},{5,2},{6,1},{7,4},{8,15},{9,10},{10,... | collective-permute-start | bytes 786440 | tf_op jit(solution)/shard_map/ppermute | solution.py:30
  115.4 0.0 copy-start.19
  115.5 4.2 %collective-permute-start.9 = (bf16[256,512]{1,0:T(8,128)(2,1)S(1)}, bf16[256,512]{1,0:T(8,128)(2,1)S(1)}, u32[]{:S(2)}, u32[]{:S(2)}) collective-permute-start(bf16[256,512]{1,0:T(8,128)(2,1)S(1)} %shard_map.91), channel_id=1, source_target_pairs={{0,2},{1,7},{2,4},{3,1},{4,6},{5,3},{6,0},{7,5},{8,14},{9,11},{10,... | collective-permute-start | bytes 786440 | tf_op jit(solution)/shard_map/ppermute | solution.py:30
  119.7 25.9 %collective-permute-done.6.near_a = bf16[256,512]{1,0:T(8,128)(2,1)S(1)} collective-permute-done((bf16[256,512]{1,0:T(8,128)(2,1)}, bf16[256,512]{1,0:T(8,128)(2,1)S(1)}, u32[]{:S(2)}, u32[]{:S(2)}) %collective-permute-start.6) | collective-permute-done | bytes 262176 | tf_op jit(solution)/shard_map/ppermute | solution.py:30
  145.6 0.7 shard_map.90.base
  146.3 1.1 reduce_sum.9
  147.4 0.6 multiply_subtract_fusion
  148.1 0.1 collective-permute-done.10.sum_b
  148.1 6.0 %collective-permute-done.9.sum_a = bf16[256,512]{1,0:T(8,128)(2,1)S(1)} collective-permute-done((bf16[256,512]{1,0:T(8,128)(2,1)S(1)}, bf16[256,512]{1,0:T(8,128)(2,1)S(1)}, u32[]{:S(2)}, u32[]{:S(2)}) %collective-permute-start.9) | collective-permute-done | bytes 262176 | tf_op jit(solution)/shard_map/ppermute | solution.py:30
  154.1 1.6 %shard_map.93 = f32[512,512]{1,0:T(8,128)} custom-call(s32[3]{0:T(128)S(1)} %pad_add_fusion.place, f32[512,512]{1,0:T(8,128)S(1)} %shard_map.90.base, bf16[256,512]{1,0:T(8,128)(2,1)S(1)} %collective-permute-done.9.sum_a, bf16[256,512]{1,0:T(8,128)(2,1)S(1)} %collective-permute-done.10.sum_b), custom_call_target="tpu_custom_call" | custom-call | tf_op jit(solution)/shard_map/pallas_call | solution.py:235
  (36 shorter events, 0.2 us)
Async XLA Ops:
  0.6 50.9 %collective-permute-start = (bf16[256,4096]{1,0:T(8,128)(2,1)}, bf16[256,4096]{1,0:T(8,128)(2,1)}, u32[]{:S(2)}, u32[]{:S(2)}) collective-permute-start(bf16[256,4096]{1,0:T(8,128)(2,1)} %own.1), channel_id=1, source_target_pairs={{0,1},{1,0},{2,3},{3,2},{4,5},{5,4},{6,7},{7,6},{8,9},{9,8},{10,11... | collective-permute-start | bytes 6291464 | tf_op jit(solution)/shard_map/ppermute | solution.py:158
  31.5 9.3 %copy-start.4 = (bf16[512,1024]{1,0:T(8,128)(2,1)S(1)}, bf16[512,1024]{1,0:T(8,128)(2,1)}, u32[]{:S(2)}) copy-start(bf16[512,1024]{1,0:T(8,128)(2,1)} %given.1) | copy-start | bytes 3145732
  31.5 36.0 %all-to-all-start = ((bf16[16,8,32,256]{3,2,1,0:T(8,128)(2,1)}), bf16[16,8,32,256]{3,2,1,0:T(8,128)(2,1)S(1)}, u32[]{:S(2)}, u32[]{:S(2)}) async-start(bf16[16,8,32,256]{3,2,1,0:T(8,128)(2,1)} %broadcast_in_dim.8), calls=%async_computation | async-start | bytes 4194304 | tf_op jit(solution)/shard_map/all_to_all | solution.py:156
  38.4 13.1 %collective-permute-start.1 = (bf16[256,512]{1,0:T(8,128)(2,1)}, bf16[256,512]{1,0:T(8,128)(2,1)}, u32[]{:S(2)}, u32[]{:S(2)}) collective-permute-start(bf16[256,512]{1,0:T(8,128)(2,1)} %targets.1), channel_id=1, source_target_pairs={{0,1},{1,0},{2,3},{3,2},{4,5},{5,4},{6,7},{7,6},{8,9},{9,8},{10,11... | collective-permute-start | bytes 786440 | tf_op jit(solution)/shard_map/ppermute | solution.py:159
  42.5 0.7 copy-start.15
  43.2 32.1 %collective-permute-start.3 = (bf16[128,1024]{1,0:T(8,128)(2,1)}, bf16[128,1024]{1,0:T(8,128)(2,1)}, u32[]{:S(2)}, u32[]{:S(2)}) collective-permute-start(bf16[128,1024]{1,0:T(8,128)(2,1)} %get-tuple-element.21), channel_id=1, source_target_pairs={{0,8},{8,0},{16,24},{24,16},{1,9},{9,1},{17,25},{25,17},{2,10},{10... | collective-permute-start | bytes 786440 | tf_op jit(solution)/shard_map/ppermute | solution.py:183
  45.8 29.5 %collective-permute-start.4 = (bf16[128,1024]{1,0:T(8,128)(2,1)}, bf16[128,1024]{1,0:T(8,128)(2,1)}, u32[]{:S(2)}, u32[]{:S(2)}) collective-permute-start(bf16[128,1024]{1,0:T(8,128)(2,1)} %get-tuple-element.22), channel_id=1, source_target_pairs={{0,16},{8,24},{16,0},{24,8},{1,17},{9,25},{17,1},{25,9},{2,18},{10... | collective-permute-start | bytes 786440 | tf_op jit(solution)/shard_map/ppermute | solution.py:183
  49.0 26.3 %collective-permute-start.5 = (bf16[128,1024]{1,0:T(8,128)(2,1)}, bf16[128,1024]{1,0:T(8,128)(2,1)}, u32[]{:S(2)}, u32[]{:S(2)}) collective-permute-start(bf16[128,1024]{1,0:T(8,128)(2,1)} %get-tuple-element.23), channel_id=1, source_target_pairs={{0,24},{8,16},{16,8},{24,0},{1,25},{9,17},{17,9},{25,1},{2,26},{10... | collective-permute-start | bytes 786440 | tf_op jit(solution)/shard_map/ppermute | solution.py:183
  51.6 1.6 %copy-start.2 = (bf16[256,4096]{1,0:T(8,128)(2,1)S(1)}, bf16[256,4096]{1,0:T(8,128)(2,1)}, u32[]{:S(2)}) copy-start(bf16[256,4096]{1,0:T(8,128)(2,1)} %own.1) | copy-start | bytes 6291460
  53.2 0.9 copy-start.14
  56.6 2.1 %copy-start = (bf16[512,4352]{1,0:T(8,128)(2,1)}, bf16[512,4352]{1,0:T(8,128)(2,1)S(1)}, u32[]{:S(2)}) copy-start(bf16[512,4352]{1,0:T(8,128)(2,1)S(1)} %get-tuple-element.19.both) | copy-start | bytes 13369348
  58.6 0.8 copy-start.5
  59.4 0.8 copy-start.7
  67.6 2.3 %copy-start.1 = (bf16[512,4352]{1,0:T(8,128)(2,1)S(1)}, bf16[512,4352]{1,0:T(8,128)(2,1)}, u32[]{:S(2)}) copy-start(bf16[512,4352]{1,0:T(8,128)(2,1)} %copy-done) | copy-start | bytes 13369348
  69.8 6.5 %copy-start.8 = (bf16[2,256,512]{2,1,0:T(8,128)(2,1)S(1)}, bf16[2,256,512]{2,1,0:T(8,128)(2,1)}, u32[]{:S(2)}) copy-start(bf16[2,256,512]{2,1,0:T(8,128)(2,1)} %copy-done.7) | copy-start | bytes 1572868
  71.1 10.2 %copy-start.3 = (f32[512,512]{1,0:T(8,128)S(1)}, f32[512,512]{1,0:T(8,128)}, u32[]{:S(2)}) copy-start(f32[512,512]{1,0:T(8,128)} %w.1) | copy-start | bytes 3145732
  71.1 10.2 %copy-start.6 = (bf16[2,256,512]{2,1,0:T(8,128)(2,1)S(1)}, bf16[2,256,512]{2,1,0:T(8,128)(2,1)}, u32[]{:S(2)}) copy-start(bf16[2,256,512]{2,1,0:T(8,128)(2,1)} %copy-done.5) | copy-start | bytes 1572868
  71.1 10.2 %copy-start.16 = (bf16[128,1024]{1,0:T(8,128)(2,1)S(1)}, bf16[128,1024]{1,0:T(8,128)(2,1)}, u32[]{:S(2)}) copy-start(bf16[128,1024]{1,0:T(8,128)(2,1)} %copy-done.15) | copy-start | bytes 786436
  71.1 5.2 %collective-permute-start.2 = (bf16[512,256]{1,0:T(8,128)(2,1)S(1)}, bf16[512,256]{1,0:T(8,128)(2,1)S(1)}, u32[]{:S(2)}, u32[]{:S(2)}) collective-permute-start(bf16[512,256]{1,0:T(8,128)(2,1)S(1)} %shard_map.86.err_own), channel_id=1, source_target_pairs={{0,1},{1,0},{2,3},{3,2},{4,5},{5,4},{6,7},{7,6},{8,9},{9,8},{10,11... | collective-permute-start | bytes 786440 | tf_op jit(solution)/shard_map/ppermute | solution.py:192
  77.4 25.3 %collective-permute-start.8 = (bf16[512,512]{1,0:T(8,128)(2,1)S(1)}, bf16[512,512]{1,0:T(8,128)(2,1)S(1)}, u32[]{:S(2)}, u32[]{:S(2)}) collective-permute-start(bf16[512,512]{1,0:T(8,128)(2,1)S(1)} %shard_map.88.refs_4_), channel_id=1, source_target_pairs={{0,2},{1,7},{2,4},{3,1},{4,6},{5,3},{6,0},{7,5},{8,14},{9,11},{10,... | collective-permute-start | bytes 1572872 | tf_op jit(solution)/shard_map/ppermute | solution.py:30
  83.7 0.8 copy-start.9
  84.5 0.8 copy-start.10
  85.3 0.8 copy-start.12
  86.1 0.7 copy-start.17
  86.8 0.7 copy-start.18
  87.5 27.9 %copy-start.11 = (f32[256,512]{1,0:T(8,128)S(1)}, f32[256,512]{1,0:T(8,128)}, u32[]{:S(2)}) copy-start(f32[256,512]{1,0:T(8,128)} %copy-done.10) | copy-start | bytes 1572868
  87.5 58.8 %all-to-all-start.1 = ((f32[16,8,1024]{2,1,0:T(8,128)}), f32[16,8,1024]{2,1,0:T(8,128)}, u32[]{:S(2)}, u32[]{:S(2)}) async-start(f32[16,8,1024]{2,1,0:T(8,128)} %bitcast.5), calls=%async_computation.1 | async-start | bytes 1048576 | tf_op jit(solution)/shard_map/all_to_all | solution.py:243
  92.4 53.3 %collective-permute-start.6 = (bf16[256,512]{1,0:T(8,128)(2,1)}, bf16[256,512]{1,0:T(8,128)(2,1)S(1)}, u32[]{:S(2)}, u32[]{:S(2)}) collective-permute-start(bf16[256,512]{1,0:T(8,128)(2,1)} %copy-done.18), channel_id=1, source_target_pairs={{0,2},{1,7},{2,4},{3,1},{4,6},{5,3},{6,0},{7,5},{8,14},{9,11},{10,... | collective-permute-start | bytes 786440 | tf_op jit(solution)/shard_map/ppermute | solution.py:30
  97.6 48.0 %collective-permute-start.7 = (bf16[256,512]{1,0:T(8,128)(2,1)}, bf16[256,512]{1,0:T(8,128)(2,1)S(1)}, u32[]{:S(2)}, u32[]{:S(2)}) collective-permute-start(bf16[256,512]{1,0:T(8,128)(2,1)} %copy-done.17), channel_id=1, source_target_pairs={{0,3},{1,6},{2,5},{3,0},{4,7},{5,2},{6,1},{7,4},{8,15},{9,10},{10,... | collective-permute-start | bytes 786440 | tf_op jit(solution)/shard_map/ppermute | solution.py:30
  102.7 1.0 copy-start.13
  103.8 44.4 %collective-permute-start.10 = (bf16[256,512]{1,0:T(8,128)(2,1)S(1)}, bf16[256,512]{1,0:T(8,128)(2,1)S(1)}, u32[]{:S(2)}, u32[]{:S(2)}) collective-permute-start(bf16[256,512]{1,0:T(8,128)(2,1)S(1)} %shard_map.92), channel_id=1, source_target_pairs={{0,3},{1,6},{2,5},{3,0},{4,7},{5,2},{6,1},{7,4},{8,15},{9,10},{10,... | collective-permute-start | bytes 786440 | tf_op jit(solution)/shard_map/ppermute | solution.py:30
  115.4 32.0 %copy-start.19 = (f32[8,1024]{1,0:T(8,128)S(1)}, f32[8,1024]{1,0:T(8,128)}, u32[]{:S(2)}) copy-start(f32[8,1024]{1,0:T(8,128)} %param.9) | copy-start | bytes 98308
  115.4 32.0 %copy-start.20 = (f32[8,1024]{1,0:T(8,128)S(1)}, f32[8,1024]{1,0:T(8,128)}, u32[]{:S(2)}) copy-start(f32[8,1024]{1,0:T(8,128)} %param.11) | copy-start | bytes 98308
  115.5 38.6 %collective-permute-start.9 = (bf16[256,512]{1,0:T(8,128)(2,1)S(1)}, bf16[256,512]{1,0:T(8,128)(2,1)S(1)}, u32[]{:S(2)}, u32[]{:S(2)}) collective-permute-start(bf16[256,512]{1,0:T(8,128)(2,1)S(1)} %shard_map.91), channel_id=1, source_target_pairs={{0,2},{1,7},{2,4},{3,1},{4,6},{5,3},{6,0},{7,5},{8,14},{9,11},{10,... | collective-permute-start | bytes 786440 | tf_op jit(solution)/shard_map/ppermute | solution.py:30

commit v8 on v7

--- a/solution.py
+++ b/solution.py
@@ -72,47 +72,65 @@
         out[at, :] = errors.astype(jnp.bfloat16)
 
 
-def errors_of(place, err_own, err_mate):
-    tokens = err_own.shape[0] // 2
-    mine = err_own[...]
-    other = jnp.concatenate([err_mate[tokens:, :], err_mate[:tokens, :]], axis=0)
+def swapped(err_mate):
+    tokens = err_mate.shape[0] // 2
+    return jnp.concatenate([err_mate[tokens:, :], err_mate[:tokens, :]], axis=0)
+
+
+def in_order(place, mine, other):
     low = jnp.where(place[1] == 0, mine, other)
     high = jnp.where(place[1] == 0, other, mine)
     return jnp.concatenate([low, high], axis=1)
 
 
-def far_kernel(place, xt, err_own, err_mate, one, two, three, out):
-    del one, two, three
-    errors = errors_of(place, err_own, err_mate)
+def product(xt, errors):
+    return jnp.dot(xt, errors, preferred_element_type=jnp.float32)
+
+
+def far_kernel(xt, err_own, out):
     rows = xt.shape[1]
     for i in range(2):
-        part = jnp.dot(xt[i], errors, preferred_element_type=jnp.float32)
-        out[i * rows : (i + 1) * rows, :] = part.astype(out.dtype)
+        out[i * rows : (i + 1) * rows, :] = product(xt[i], err_own[...]).astype(out.dtype)
+
+
+def second_kernel(place, far_xt, near_xt, err_own, err_mate, one, two, three, out):
+    del one, two, three
+    other = swapped(err_mate)
+    rows, half = far_xt.shape[1], err_own.shape[1]
+    near = product(near_xt[1], in_order(place, err_own[...], other)).astype(out.dtype)
+    for i in range(2):
+        at = slice(i * rows, (i + 1) * rows)
+        out[at, :half] = product(far_xt[i], other).astype(out.dtype)
+        out[at, half:] = near[:, i * half : (i + 1) * half]
 
 
 def near_kernel(place, xt, own_xt, err_own, err_mate, w, *refs, rate):
-    parts, (_, via_a, near_a, via_b, near_b, base, total) = refs[:ZL], refs[ZL:]
+    parts, (_, via_a, via_b, near_b, base, total) = refs[:ZL], refs[ZL:]
     keep, one, two, three = (p[...].astype(jnp.float32) for p in parts)
     total[...] = (keep + one) + (two + three)
-    errors = errors_of(place, err_own, err_mate)
-    for i, out in enumerate((via_a, near_a, via_b, near_b)):
-        out[...] = jnp.dot(xt[i], errors, preferred_element_type=jnp.float32).astype(out.dtype)
+    errors = in_order(place, err_own[...], swapped(err_mate))
+    for i, out in ((0, via_a), (2, via_b), (3, near_b)):
+        out[...] = product(xt[i], errors).astype(out.dtype)
     rows = xt.shape[1]
     for h in range(2):
         at = slice(h * rows, (h + 1) * rows)
-        base[at, :] = w[at, :] - rate * jnp.dot(own_xt[h], errors, preferred_element_type=jnp.float32)
-
-
-def pass_kernel(via, far, out, *, half):
+        base[at, :] = w[at, :] - rate * product(own_xt[h], errors)
+
+
+def pass_kernel(place, via, far, second, out, *, half):
     rows = via.shape[0]
-    out[...] = (via[...] + far[half * rows : (half + 1) * rows, :].astype(jnp.float32)).astype(out.dtype)
-
-
-def fold_kernel(place, base, near_a, near_b, out, *, rate):
-    rows = near_a.shape[0]
-    for half, near in ((place[1], near_b), (1 - place[1], near_a)):
+    at = slice(half * rows, (half + 1) * rows)
+    width = far.shape[1]
+    grad = in_order(place, far[at, :].astype(jnp.float32), second[at, :width].astype(jnp.float32))
+    out[...] = (via[...] + grad).astype(out.dtype)
+
+
+def fold_kernel(place, base, second, near_b, out, *, rate):
+    rows, width = near_b.shape
+    near_a = jnp.concatenate([second[:rows, width // 2 :], second[rows:, width // 2 :]], axis=1)
+    for half, near in ((place[1], near_b[...]), (1 - place[1], near_a)):
         at = pl.ds(pl.multiple_of(half * rows, rows), rows)
-        out[at, :] = base[at, :] - rate * near[...].astype(jnp.float32)
+        out[at, :] = base[at, :] - rate * near.astype(jnp.float32)
 
 
 def finish_kernel(place, base, sum_a, sum_b, out, *, rate):
@@ -120,6 +138,11 @@
     for half, total in ((place[1], sum_a), (1 - place[1], sum_b)):
         at = pl.ds(pl.multiple_of(half * rows, rows), rows)
         out[at, :] = base[at, :] - rate * total[...].astype(jnp.float32)
+
+
+def copy_kernel(given, order, out):
+    del order
+    out[...] = given[...]
 
 
 def sort_kernel(place, given, order, keep, one, two, three, held):
@@ -189,39 +212,53 @@
         compiler_params=PARAMS,
         cost_estimate=cost(4 * rows * width * half, 8 * rows * width),
     )(both, key)
-    err_mate = lax.ppermute(err, "c", SWAP)
     rate = INNER_RATE / width
     short = jax.ShapeDtypeStruct((own_rows // 2, columns), jnp.bfloat16)
     middle = jax.ShapeDtypeStruct((own_rows // 2, columns), jnp.float32)
     long = jax.ShapeDtypeStruct((own_rows, columns), jnp.bfloat16)
     full = jax.ShapeDtypeStruct((own_rows, columns), jnp.float32)
+    far = pl.pallas_call(
+        far_kernel,
+        out_shape=jax.ShapeDtypeStruct((own_rows, half), jnp.bfloat16),
+        in_specs=[vmem] * 2,
+        out_specs=vmem,
+        compiler_params=PARAMS,
+    )(far_xt, err)
+    far = round_z(far, 0)
+    err_mate = lax.ppermute(err, "c", SWAP)
     out = pl.pallas_call(
-        far_kernel,
+        second_kernel,
         out_shape=long,
-        in_specs=[smem] + [vmem] * 3 + [anywhere] * 3,
-        out_specs=vmem,
-        compiler_params=PARAMS,
-    )(place, far_xt, err, err_mate, *parts[1:])
-
-    far = round_z(out, 0)
-    via_a, near_a, via_b, near_b, base, part = pl.pallas_call(
+        in_specs=[smem] + [vmem] * 4 + [anywhere] * 3,
+        out_specs=vmem,
+        compiler_params=PARAMS,
+        cost_estimate=cost(0, 64 * rows * width),
+    )(place, far_xt, near_xt, err, err_mate, *parts[1:])
+    second = round_z(out, 0)
+    via_a, via_b, near_b, base, part = pl.pallas_call(
         functools.partial(near_kernel, rate=rate),
-        out_shape=(middle, short, middle, short, full, jax.ShapeDtypeStruct(block.shape, jnp.float32)),
+        out_shape=(middle, middle, short, full, jax.ShapeDtypeStruct(block.shape, jnp.float32)),
         in_specs=[smem] + [vmem] * (5 + ZL) + [anywhere],
-        out_specs=(vmem,) * 6,
+        out_specs=(vmem,) * 5,
         compiler_params=PARAMS,
     )(place, near_xt, own_xt, err, err_mate, w_key, *parts, out)
-    near_a = round_z(near_a, 0)
     near_b = round_z(near_b, 1)
+    part = pl.pallas_call(
+        copy_kernel,
+        out_shape=jax.ShapeDtypeStruct(block.shape, jnp.float32),
+        in_specs=[vmem, anywhere],
+        out_specs=vmem,
+        compiler_params=PARAMS,
+    )(part, far)
 
     def passed(via, half):
         return pl.pallas_call(
             functools.partial(pass_kernel, half=half),
             out_shape=short,
-            in_specs=[vmem] * 2,
+            in_specs=[smem] + [vmem] * 3,
             out_specs=vmem,
             compiler_params=PARAMS,
-        )(via, far)
+        )(place, via, far, second)
 
     sum_a = round_z(passed(via_a, 0), 0)
     sum_b = round_z(passed(via_b, 1), 1)
@@ -231,7 +268,7 @@
         in_specs=[smem] + [vmem] * 3,
         out_specs=vmem,
         compiler_params=PARAMS,
-    )(place, base, near_a, near_b)
+    )(place, base, second, near_b)
     new_key = pl.pallas_call(
         functools.partial(finish_kernel, rate=rate),
         out_shape=full,

time: 157 us -> 156 us (level)
  the two profiles are of different devices: /device:TPU:33 before, /device:TPU:32 now
where the time goes in v8:
time: 156 us; the launch traced here: 155 us
  starting transfers between devices  50.2 us (32%)
  waiting for transfers between devices  48 us (31%)
  blocking collectives  26 us (17%)
  local copies, waits for them, and re-layouts  14.5 us (9%)
  Pallas kernels  13.5 us (9%)
  other arithmetic  1.79 us (1%)
    ppermute x5, waiting for transfers between devices, round_z(): return lax.ppermute(a, ('zl', 'zh', 'c'), pairs)  39.4 us
    all_gather x1, blocking collectives, on_device(): column = lax.all_gather(mine, ('zh', 'c'), axis=0, tiled=True)  26 us
    ppermute x5, starting transfers between devices, round_z(): return lax.ppermute(a, ('zl', 'zh', 'c'), pairs)  23 us
    unnamed x40, local copies, waits for them, and re-layouts  12 us
    ppermute x3, starting transfers between devices, on_device(): lax.ppermute(p, 'zl', [(i, i ^ j) for i in range(ZL)])  9.2 us
    all_to_all x1, waiting for transfers between devices, on_device(): key = lax.all_to_all(copies, ('x', 'y'), 0, 0, tiled=True)  8.54 us
    all_to_all x1, starting transfers between devices, on_device(): key = lax.all_to_all(copies, ('x', 'y'), 0, 0, tiled=True)  7.17 us
    all_to_all x1, starting transfers between devices, on_device(): lax.all_to_all(part.reshape(spots, owned, wide), ('x', 'y'), 0, 0, tiled=...  4.98 us
  transfers between devices with their start and end apart: 13, of which 6 were waited for; matrix products, arithmetic and copies ran while one was open for 3% of the time, Pallas kernels for 8%

profile of v8, /device:TPU:32, one launch (start us, length us, event | category | flops | bytes accessed | tf_op | source)
XLA Modules:
  0.0 154.8 jit_solution(7550985182316608580)
XLA Ops:
  0.6 1.9 %collective-permute-start = (bf16[256,4096]{1,0:T(8,128)(2,1)}, bf16[256,4096]{1,0:T(8,128)(2,1)}, u32[]{:S(2)}, u32[]{:S(2)}) collective-permute-start(bf16[256,4096]{1,0:T(8,128)(2,1)} %own.1), channel_id=1, source_target_pairs={{0,1},{1,0},{2,3},{3,2},{4,5},{5,4},{6,7},{7,6},{8,9},{9,8},{10,11... | collective-permute-start | bytes 6291464 | tf_op jit(solution)/shard_map/ppermute | solution.py:181
  2.6 0.9 dynamic-slice_convert_fusion
  3.4 26.0 %all_gather.3.order = bf16[256,512]{1,0:T(8,128)(2,1)S(1)} all-gather(bf16[32,512]{1,0:T(8,128)(2,1)S(1)} %dynamic-slice_convert_fusion), channel_id=1, replica_groups=mesh['x'=4,'y'=4,'zl'=4,'zh'=4,'c'=2] {'zh','c'}, dimensions={0}, use_global_device_ids=true | all-gather | bytes 294912 | tf_op jit(solution)/shard_map/all_gather | solution.py:176
  29.4 1.6 %broadcast_in_dim.8 = bf16[16,8,32,256]{3,2,1,0:T(8,128)(2,1)} broadcast(bf16[8,32,256]{2,1,0:T(8,128)(2,1)S(1)} %bitcast.5), dimensions={1,2,3} | broadcast | bytes 2228224 | tf_op jit(solution)/shard_map/broadcast_in_dim | solution.py:178
  31.0 7.2 %all-to-all-start = ((bf16[16,8,32,256]{3,2,1,0:T(8,128)(2,1)}), bf16[16,8,32,256]{3,2,1,0:T(8,128)(2,1)S(1)}, u32[]{:S(2)}, u32[]{:S(2)}) async-start(bf16[16,8,32,256]{3,2,1,0:T(8,128)(2,1)} %broadcast_in_dim.8), calls=%async_computation | async-start | bytes 4194304 | tf_op jit(solution)/shard_map/all_to_all | solution.py:179
  38.2 2.0 %collective-permute-start.1 = (bf16[256,512]{1,0:T(8,128)(2,1)}, bf16[256,512]{1,0:T(8,128)(2,1)}, u32[]{:S(2)}, u32[]{:S(2)}) collective-permute-start(bf16[256,512]{1,0:T(8,128)(2,1)} %targets.1), channel_id=1, source_target_pairs={{0,1},{1,0},{2,3},{3,2},{4,5},{5,4},{6,7},{7,6},{8,9},{9,8},{10,11... | collective-permute-start | bytes 786440 | tf_op jit(solution)/shard_map/ppermute | solution.py:182
  40.2 0.1 pad_add_fusion.place
  40.3 1.6 %shard_map.87 = (bf16[128,1024]{1,0:T(8,128)(2,1)S(1)}, bf16[128,1024]{1,0:T(8,128)(2,1)}, bf16[128,1024]{1,0:T(8,128)(2,1)}, bf16[128,1024]{1,0:T(8,128)(2,1)}) custom-call(s32[3]{0:T(128)S(1)} %pad_add_fusion.place, bf16[512,1024]{1,0:T(8,128)(2,1)S(1)} %copy-done.8, bf16[256,512]{1,0:T(8,128)(2,1)S(1)} %all_gather.3.order), custom_call_target="tpu_custom_call" | custom-call | tf_op jit(solution)/shard_map/pallas_call | solution.py:198
  41.8 0.7 copy-done.16
  42.6 2.9 %collective-permute-start.3 = (bf16[128,1024]{1,0:T(8,128)(2,1)}, bf16[128,1024]{1,0:T(8,128)(2,1)}, u32[]{:S(2)}, u32[]{:S(2)}) collective-permute-start(bf16[128,1024]{1,0:T(8,128)(2,1)} %get-tuple-element.20), channel_id=1, source_target_pairs={{0,8},{8,0},{16,24},{24,16},{1,9},{9,1},{17,25},{25,17},{2,10},{10... | collective-permute-start | bytes 786440 | tf_op jit(solution)/shard_map/ppermute | solution.py:206
  45.5 3.5 %collective-permute-start.4 = (bf16[128,1024]{1,0:T(8,128)(2,1)}, bf16[128,1024]{1,0:T(8,128)(2,1)}, u32[]{:S(2)}, u32[]{:S(2)}) collective-permute-start(bf16[128,1024]{1,0:T(8,128)(2,1)} %get-tuple-element.21), channel_id=1, source_target_pairs={{0,16},{8,24},{16,0},{24,8},{1,17},{9,25},{17,1},{25,9},{2,18},{10... | collective-permute-start | bytes 786440 | tf_op jit(solution)/shard_map/ppermute | solution.py:206
  49.0 2.8 %collective-permute-start.5 = (bf16[128,1024]{1,0:T(8,128)(2,1)}, bf16[128,1024]{1,0:T(8,128)(2,1)}, u32[]{:S(2)}, u32[]{:S(2)}) collective-permute-start(bf16[128,1024]{1,0:T(8,128)(2,1)} %get-tuple-element.22), channel_id=1, source_target_pairs={{0,24},{8,16},{16,8},{24,0},{1,25},{9,17},{17,9},{25,1},{2,26},{10... | collective-permute-start | bytes 786440 | tf_op jit(solution)/shard_map/ppermute | solution.py:206
  51.8 1.6 %copy-done.2 = bf16[256,4096]{1,0:T(8,128)(2,1)S(1)} copy-done((bf16[256,4096]{1,0:T(8,128)(2,1)S(1)}, bf16[256,4096]{1,0:T(8,128)(2,1)}, u32[]{:S(2)}) %copy-start.2) | copy-done | bytes 2097176
  53.4 0.9 copy-done.15
  54.3 2.4 %shard_map.85 = (bf16[2,256,512]{2,1,0:T(8,128)(2,1)S(1)}, bf16[4,256,512]{2,1,0:T(8,128)(2,1)S(1)}, bf16[2,256,512]{2,1,0:T(8,128)(2,1)S(1)}, bf16[512,4352]{1,0:T(8,128)(2,1)S(1)}) custom-call(s32[3]{0:T(128)S(1)} %pad_add_fusion.place, bf16[256,4096]{1,0:T(8,128)(2,1)S(1)} %copy-done.2, bf16[256,512]{1,0:T(8,128)(2,1)S(1)} %copy-done.15, ...), custom_call_target="tpu_custom_call" | custom-call | bytes 16777216 | tf_op jit(solution)/shard_map/pallas_call | solution.py:187
  56.8 2.0 %copy-done = bf16[512,4352]{1,0:T(8,128)(2,1)} copy-done((bf16[512,4352]{1,0:T(8,128)(2,1)}, bf16[512,4352]{1,0:T(8,128)(2,1)S(1)}, u32[]{:S(2)}) %copy-start) | copy-done | bytes 4456472
  58.8 0.8 copy-done.3
  59.6 0.8 copy-done.9
  60.4 8.5 %all-to-all-done.w = bf16[16,8,32,256]{3,2,1,0:T(8,128)(2,1)S(1)} async-done(((bf16[16,8,32,256]{3,2,1,0:T(8,128)(2,1)}), bf16[16,8,32,256]{3,2,1,0:T(8,128)(2,1)S(1)}, u32[]{:S(2)}, u32[]{:S(2)}) %all-to-all-start) | async-done | bytes 2097184 | tf_op jit(solution)/shard_map/all_to_all | solution.py:179
  69.0 2.3 %copy-done.1 = bf16[512,4352]{1,0:T(8,128)(2,1)S(1)} copy-done((bf16[512,4352]{1,0:T(8,128)(2,1)S(1)}, bf16[512,4352]{1,0:T(8,128)(2,1)}, u32[]{:S(2)}) %copy-start.1) | copy-done | bytes 4456472
  71.2 1.2 shard_map.86.err_own
  72.5 1.9 %collective-permute-start.2 = (bf16[512,256]{1,0:T(8,128)(2,1)S(1)}, bf16[512,256]{1,0:T(8,128)(2,1)S(1)}, u32[]{:S(2)}, u32[]{:S(2)}) collective-permute-start(bf16[512,256]{1,0:T(8,128)(2,1)S(1)} %shard_map.86.err_own), channel_id=1, source_target_pairs={{0,1},{1,0},{2,3},{3,2},{4,5},{5,4},{6,7},{7,6},{8,9},{9,8},{10,11... | collective-permute-start | bytes 786440 | tf_op jit(solution)/shard_map/ppermute | solution.py:228
  74.4 0.0 copy-start.10
  74.5 0.3 shard_map.91
  74.8 4.4 %collective-permute-start.8 = (bf16[512,256]{1,0:T(8,128)(2,1)S(1)}, bf16[512,256]{1,0:T(8,128)(2,1)S(1)}, u32[]{:S(2)}, u32[]{:S(2)}) collective-permute-start(bf16[512,256]{1,0:T(8,128)(2,1)S(1)} %shard_map.91), channel_id=1, source_target_pairs={{0,2},{1,7},{2,4},{3,1},{4,6},{5,3},{6,0},{7,5},{8,14},{9,11},{10,... | collective-permute-start | bytes 786440 | tf_op jit(solution)/shard_map/ppermute | solution.py:30
  79.2 1.0 shard_map.88.refs_4_
  80.2 5.5 %collective-permute-start.6 = (bf16[512,512]{1,0:T(8,128)(2,1)S(1)}, bf16[512,512]{1,0:T(8,128)(2,1)S(1)}, u32[]{:S(2)}, u32[]{:S(2)}) collective-permute-start(bf16[512,512]{1,0:T(8,128)(2,1)S(1)} %shard_map.88.refs_4_), channel_id=1, source_target_pairs={{0,2},{1,7},{2,4},{3,1},{4,6},{5,3},{6,0},{7,5},{8,14},{9,11},{10,... | collective-permute-start | bytes 1572872 | tf_op jit(solution)/shard_map/ppermute | solution.py:30
  85.7 2.6 %shard_map.89 = (f32[256,512]{1,0:T(8,128)S(1)}, f32[256,512]{1,0:T(8,128)S(1)}, bf16[256,512]{1,0:T(8,128)(2,1)}, f32[512,512]{1,0:T(8,128)S(1)}, f32[128,1024]{1,0:T(8,128)S(1)}) custom-call(s32[3]{0:T(128)S(1)} %pad_add_fusion.place, bf16[4,256,512]{2,1,0:T(8,128)(2,1)S(1)} %get-tuple-element.16.near_xt.xt, bf16[2,256,512]{2,1,0:T(8,128)(2,1)S(1)} %copy-done.10, ...), custom_call_target="tpu_custom_call" | custom-call | tf_op jit(solution)/shard_map/pallas_call | solution.py:238
  88.4 1.0 copy-done.6
  89.3 0.8 copy-done.13
  90.1 21.1 %collective-permute-done.8.far.order = bf16[512,256]{1,0:T(8,128)(2,1)S(1)} collective-permute-done((bf16[512,256]{1,0:T(8,128)(2,1)S(1)}, bf16[512,256]{1,0:T(8,128)(2,1)S(1)}, u32[]{:S(2)}, u32[]{:S(2)}) %collective-permute-start.8) | collective-permute-done | bytes 262176 | tf_op jit(solution)/shard_map/ppermute | solution.py:30
  111.2 0.8 shard_map.95
  112.1 5.0 %all-to-all-start.1 = ((f32[16,8,1024]{2,1,0:T(8,128)}), f32[16,8,1024]{2,1,0:T(8,128)}, u32[]{:S(2)}, u32[]{:S(2)}) async-start(f32[16,8,1024]{2,1,0:T(8,128)} %bitcast.4), calls=%async_computation.1 | async-start | bytes 1048576 | tf_op jit(solution)/shard_map/all_to_all | solution.py:280
  117.1 0.0 copy-start.19
  117.1 2.1 %collective-permute-start.7 = (bf16[256,512]{1,0:T(8,128)(2,1)}, bf16[256,512]{1,0:T(8,128)(2,1)S(1)}, u32[]{:S(2)}, u32[]{:S(2)}) collective-permute-start(bf16[256,512]{1,0:T(8,128)(2,1)} %get-tuple-element.25), channel_id=1, source_target_pairs={{0,3},{1,6},{2,5},{3,0},{4,7},{5,2},{6,1},{7,4},{8,15},{9,10},{10,... | collective-permute-start | bytes 786440 | tf_op jit(solution)/shard_map/ppermute | solution.py:30
  119.1 2.1 %collective-permute-done.6.second = bf16[512,512]{1,0:T(8,128)(2,1)S(1)} collective-permute-done((bf16[512,512]{1,0:T(8,128)(2,1)S(1)}, bf16[512,512]{1,0:T(8,128)(2,1)S(1)}, u32[]{:S(2)}, u32[]{:S(2)}) %collective-permute-start.6) | collective-permute-done | bytes 524320 | tf_op jit(solution)/shard_map/ppermute | solution.py:30
  121.2 0.6 shard_map.93
  121.8 5.5 %collective-permute-start.10 = (bf16[256,512]{1,0:T(8,128)(2,1)S(1)}, bf16[256,512]{1,0:T(8,128)(2,1)S(1)}, u32[]{:S(2)}, u32[]{:S(2)}) collective-permute-start(bf16[256,512]{1,0:T(8,128)(2,1)S(1)} %shard_map.93), channel_id=1, source_target_pairs={{0,3},{1,6},{2,5},{3,0},{4,7},{5,2},{6,1},{7,4},{8,15},{9,10},{10,... | collective-permute-start | bytes 786440 | tf_op jit(solution)/shard_map/ppermute | solution.py:30
  127.3 1.0 copy-done.12
  128.4 0.6 shard_map.92
  129.0 5.6 %collective-permute-start.9 = (bf16[256,512]{1,0:T(8,128)(2,1)S(1)}, bf16[256,512]{1,0:T(8,128)(2,1)S(1)}, u32[]{:S(2)}, u32[]{:S(2)}) collective-permute-start(bf16[256,512]{1,0:T(8,128)(2,1)S(1)} %shard_map.92), channel_id=1, source_target_pairs={{0,2},{1,7},{2,4},{3,1},{4,6},{5,3},{6,0},{7,5},{8,14},{9,11},{10,... | collective-permute-start | bytes 786440 | tf_op jit(solution)/shard_map/ppermute | solution.py:30
  134.6 1.1 reduce_sum.9
  135.7 0.6 multiply_subtract_fusion
  136.3 8.6 %collective-permute-done.7.near_b = bf16[256,512]{1,0:T(8,128)(2,1)S(1)} collective-permute-done((bf16[256,512]{1,0:T(8,128)(2,1)}, bf16[256,512]{1,0:T(8,128)(2,1)S(1)}, u32[]{:S(2)}, u32[]{:S(2)}) %collective-permute-start.7) | collective-permute-done | bytes 262176 | tf_op jit(solution)/shard_map/ppermute | solution.py:30
  144.9 0.6 shard_map.90.base
  145.6 2.4 %collective-permute-done.10.sum_b = bf16[256,512]{1,0:T(8,128)(2,1)S(1)} collective-permute-done((bf16[256,512]{1,0:T(8,128)(2,1)S(1)}, bf16[256,512]{1,0:T(8,128)(2,1)S(1)}, u32[]{:S(2)}, u32[]{:S(2)}) %collective-permute-start.10) | collective-permute-done | bytes 262176 | tf_op jit(solution)/shard_map/ppermute | solution.py:30
  148.0 5.2 %collective-permute-done.9.sum_a = bf16[256,512]{1,0:T(8,128)(2,1)S(1)} collective-permute-done((bf16[256,512]{1,0:T(8,128)(2,1)S(1)}, bf16[256,512]{1,0:T(8,128)(2,1)S(1)}, u32[]{:S(2)}, u32[]{:S(2)}) %collective-permute-start.9) | collective-permute-done | bytes 262176 | tf_op jit(solution)/shard_map/ppermute | solution.py:30
  153.2 1.6 %shard_map.94 = f32[512,512]{1,0:T(8,128)} custom-call(s32[3]{0:T(128)S(1)} %pad_add_fusion.place, f32[512,512]{1,0:T(8,128)S(1)} %shard_map.90.base, bf16[256,512]{1,0:T(8,128)(2,1)S(1)} %collective-permute-done.9.sum_a, bf16[256,512]{1,0:T(8,128)(2,1)S(1)} %collective-permute-done.10.sum_b), custom_call_target="tpu_custom_call" | custom-call | tf_op jit(solution)/shard_map/pallas_call | solution.py:272
  (36 shorter events, 0.1 us)
Async XLA Ops:
  0.6 51.2 %collective-permute-start = (bf16[256,4096]{1,0:T(8,128)(2,1)}, bf16[256,4096]{1,0:T(8,128)(2,1)}, u32[]{:S(2)}, u32[]{:S(2)}) collective-permute-start(bf16[256,4096]{1,0:T(8,128)(2,1)} %own.1), channel_id=1, source_target_pairs={{0,1},{1,0},{2,3},{3,2},{4,5},{5,4},{6,7},{7,6},{8,9},{9,8},{10,11... | collective-permute-start | bytes 6291464 | tf_op jit(solution)/shard_map/ppermute | solution.py:181
  31.0 9.2 %copy-start.8 = (bf16[512,1024]{1,0:T(8,128)(2,1)S(1)}, bf16[512,1024]{1,0:T(8,128)(2,1)}, u32[]{:S(2)}) copy-start(bf16[512,1024]{1,0:T(8,128)(2,1)} %given.1) | copy-start | bytes 3145732
  31.0 37.9 %all-to-all-start = ((bf16[16,8,32,256]{3,2,1,0:T(8,128)(2,1)}), bf16[16,8,32,256]{3,2,1,0:T(8,128)(2,1)S(1)}, u32[]{:S(2)}, u32[]{:S(2)}) async-start(bf16[16,8,32,256]{3,2,1,0:T(8,128)(2,1)} %broadcast_in_dim.8), calls=%async_computation | async-start | bytes 4194304 | tf_op jit(solution)/shard_map/all_to_all | solution.py:179
  38.2 13.6 %collective-permute-start.1 = (bf16[256,512]{1,0:T(8,128)(2,1)}, bf16[256,512]{1,0:T(8,128)(2,1)}, u32[]{:S(2)}, u32[]{:S(2)}) collective-permute-start(bf16[256,512]{1,0:T(8,128)(2,1)} %targets.1), channel_id=1, source_target_pairs={{0,1},{1,0},{2,3},{3,2},{4,5},{5,4},{6,7},{7,6},{8,9},{9,8},{10,11... | collective-permute-start | bytes 786440 | tf_op jit(solution)/shard_map/ppermute | solution.py:182
  41.8 0.7 copy-start.16
  42.6 36.6 %collective-permute-start.3 = (bf16[128,1024]{1,0:T(8,128)(2,1)}, bf16[128,1024]{1,0:T(8,128)(2,1)}, u32[]{:S(2)}, u32[]{:S(2)}) collective-permute-start(bf16[128,1024]{1,0:T(8,128)(2,1)} %get-tuple-element.20), channel_id=1, source_target_pairs={{0,8},{8,0},{16,24},{24,16},{1,9},{9,1},{17,25},{25,17},{2,10},{10... | collective-permute-start | bytes 786440 | tf_op jit(solution)/shard_map/ppermute | solution.py:206
  45.5 33.7 %collective-permute-start.4 = (bf16[128,1024]{1,0:T(8,128)(2,1)}, bf16[128,1024]{1,0:T(8,128)(2,1)}, u32[]{:S(2)}, u32[]{:S(2)}) collective-permute-start(bf16[128,1024]{1,0:T(8,128)(2,1)} %get-tuple-element.21), channel_id=1, source_target_pairs={{0,16},{8,24},{16,0},{24,8},{1,17},{9,25},{17,1},{25,9},{2,18},{10... | collective-permute-start | bytes 786440 | tf_op jit(solution)/shard_map/ppermute | solution.py:206
  49.0 30.2 %collective-permute-start.5 = (bf16[128,1024]{1,0:T(8,128)(2,1)}, bf16[128,1024]{1,0:T(8,128)(2,1)}, u32[]{:S(2)}, u32[]{:S(2)}) collective-permute-start(bf16[128,1024]{1,0:T(8,128)(2,1)} %get-tuple-element.22), channel_id=1, source_target_pairs={{0,24},{8,16},{16,8},{24,0},{1,25},{9,17},{17,9},{25,1},{2,26},{10... | collective-permute-start | bytes 786440 | tf_op jit(solution)/shard_map/ppermute | solution.py:206
  51.8 1.6 %copy-start.2 = (bf16[256,4096]{1,0:T(8,128)(2,1)S(1)}, bf16[256,4096]{1,0:T(8,128)(2,1)}, u32[]{:S(2)}) copy-start(bf16[256,4096]{1,0:T(8,128)(2,1)} %own.1) | copy-start | bytes 6291460
  53.4 0.9 copy-start.15
  56.8 2.0 %copy-start = (bf16[512,4352]{1,0:T(8,128)(2,1)}, bf16[512,4352]{1,0:T(8,128)(2,1)S(1)}, u32[]{:S(2)}) copy-start(bf16[512,4352]{1,0:T(8,128)(2,1)S(1)} %get-tuple-element.18.both) | copy-start | bytes 13369348
  58.8 0.8 copy-start.3
  59.6 0.8 copy-start.9
  69.0 2.3 %copy-start.1 = (bf16[512,4352]{1,0:T(8,128)(2,1)S(1)}, bf16[512,4352]{1,0:T(8,128)(2,1)}, u32[]{:S(2)}) copy-start(bf16[512,4352]{1,0:T(8,128)(2,1)} %copy-done) | copy-start | bytes 13369348
  71.2 3.2 %copy-start.4 = (bf16[2,256,512]{2,1,0:T(8,128)(2,1)S(1)}, bf16[2,256,512]{2,1,0:T(8,128)(2,1)}, u32[]{:S(2)}) copy-start(bf16[2,256,512]{2,1,0:T(8,128)(2,1)} %copy-done.3) | copy-start | bytes 1572868
  72.5 6.7 %collective-permute-start.2 = (bf16[512,256]{1,0:T(8,128)(2,1)S(1)}, bf16[512,256]{1,0:T(8,128)(2,1)S(1)}, u32[]{:S(2)}, u32[]{:S(2)}) collective-permute-start(bf16[512,256]{1,0:T(8,128)(2,1)S(1)} %shard_map.86.err_own), channel_id=1, source_target_pairs={{0,1},{1,0},{2,3},{3,2},{4,5},{5,4},{6,7},{7,6},{8,9},{9,8},{10,11... | collective-permute-start | bytes 786440 | tf_op jit(solution)/shard_map/ppermute | solution.py:228
  74.4 11.3 %copy-start.5 = (f32[512,512]{1,0:T(8,128)S(1)}, f32[512,512]{1,0:T(8,128)}, u32[]{:S(2)}) copy-start(f32[512,512]{1,0:T(8,128)} %w.1) | copy-start | bytes 3145732
  74.4 11.3 %copy-start.10 = (bf16[2,256,512]{2,1,0:T(8,128)(2,1)S(1)}, bf16[2,256,512]{2,1,0:T(8,128)(2,1)}, u32[]{:S(2)}) copy-start(bf16[2,256,512]{2,1,0:T(8,128)(2,1)} %copy-done.9) | copy-start | bytes 1572868
  74.4 11.3 %copy-start.17 = (bf16[128,1024]{1,0:T(8,128)(2,1)S(1)}, bf16[128,1024]{1,0:T(8,128)(2,1)}, u32[]{:S(2)}) copy-start(bf16[128,1024]{1,0:T(8,128)(2,1)} %copy-done.16) | copy-start | bytes 786436
  74.8 36.5 %collective-permute-start.8 = (bf16[512,256]{1,0:T(8,128)(2,1)S(1)}, bf16[512,256]{1,0:T(8,128)(2,1)S(1)}, u32[]{:S(2)}, u32[]{:S(2)}) collective-permute-start(bf16[512,256]{1,0:T(8,128)(2,1)S(1)} %shard_map.91), channel_id=1, source_target_pairs={{0,2},{1,7},{2,4},{3,1},{4,6},{5,3},{6,0},{7,5},{8,14},{9,11},{10,... | collective-permute-start | bytes 786440 | tf_op jit(solution)/shard_map/ppermute | solution.py:30
  80.2 41.0 %collective-permute-start.6 = (bf16[512,512]{1,0:T(8,128)(2,1)S(1)}, bf16[512,512]{1,0:T(8,128)(2,1)S(1)}, u32[]{:S(2)}, u32[]{:S(2)}) collective-permute-start(bf16[512,512]{1,0:T(8,128)(2,1)S(1)} %shard_map.88.refs_4_), channel_id=1, source_target_pairs={{0,2},{1,7},{2,4},{3,1},{4,6},{5,3},{6,0},{7,5},{8,14},{9,11},{10,... | collective-permute-start | bytes 1572872 | tf_op jit(solution)/shard_map/ppermute | solution.py:30
  88.4 1.0 copy-start.6
  89.3 0.8 copy-start.13
  90.1 21.9 %copy-start.11 = (f32[256,512]{1,0:T(8,128)}, f32[256,512]{1,0:T(8,128)S(1)}, u32[]{:S(2)}) copy-start(f32[256,512]{1,0:T(8,128)S(1)} %get-tuple-element.26.via) | copy-start | bytes 1572868
  111.2 10.0 %copy-start.14 = (f32[256,512]{1,0:T(8,128)S(1)}, f32[256,512]{1,0:T(8,128)}, u32[]{:S(2)}) copy-start(f32[256,512]{1,0:T(8,128)} %copy-done.13) | copy-start | bytes 1572868
  112.1 22.5 %all-to-all-start.1 = ((f32[16,8,1024]{2,1,0:T(8,128)}), f32[16,8,1024]{2,1,0:T(8,128)}, u32[]{:S(2)}, u32[]{:S(2)}) async-start(f32[16,8,1024]{2,1,0:T(8,128)} %bitcast.4), calls=%async_computation.1 | async-start | bytes 1048576 | tf_op jit(solution)/shard_map/all_to_all | solution.py:280
  117.0 18.6 %copy-start.18 = (f32[8,1024]{1,0:T(8,128)S(1)}, f32[8,1024]{1,0:T(8,128)}, u32[]{:S(2)}) copy-start(f32[8,1024]{1,0:T(8,128)} %param.9) | copy-start | bytes 98308
  117.1 18.6 %copy-start.19 = (f32[8,1024]{1,0:T(8,128)S(1)}, f32[8,1024]{1,0:T(8,128)}, u32[]{:S(2)}) copy-start(f32[8,1024]{1,0:T(8,128)} %param.11) | copy-start | bytes 98308
  117.1 27.9 %copy-start.7 = (f32[512,512]{1,0:T(8,128)S(1)}, f32[512,512]{1,0:T(8,128)}, u32[]{:S(2)}) copy-start(f32[512,512]{1,0:T(8,128)} %copy-done.6) | copy-start | bytes 3145732
  117.1 27.8 %collective-permute-start.7 = (bf16[256,512]{1,0:T(8,128)(2,1)}, bf16[256,512]{1,0:T(8,128)(2,1)S(1)}, u32[]{:S(2)}, u32[]{:S(2)}) collective-permute-start(bf16[256,512]{1,0:T(8,128)(2,1)} %get-tuple-element.25), channel_id=1, source_target_pairs={{0,3},{1,6},{2,5},{3,0},{4,7},{5,2},{6,1},{7,4},{8,15},{9,10},{10,... | collective-permute-start | bytes 786440 | tf_op jit(solution)/shard_map/ppermute | solution.py:30
  121.8 26.2 %collective-permute-start.10 = (bf16[256,512]{1,0:T(8,128)(2,1)S(1)}, bf16[256,512]{1,0:T(8,128)(2,1)S(1)}, u32[]{:S(2)}, u32[]{:S(2)}) collective-permute-start(bf16[256,512]{1,0:T(8,128)(2,1)S(1)} %shard_map.93), channel_id=1, source_target_pairs={{0,3},{1,6},{2,5},{3,0},{4,7},{5,2},{6,1},{7,4},{8,15},{9,10},{10,... | collective-permute-start | bytes 786440 | tf_op jit(solution)/shard_map/ppermute | solution.py:30
  127.3 1.0 copy-start.12
  129.0 24.2 %collective-permute-start.9 = (bf16[256,512]{1,0:T(8,128)(2,1)S(1)}, bf16[256,512]{1,0:T(8,128)(2,1)S(1)}, u32[]{:S(2)}, u32[]{:S(2)}) collective-permute-start(bf16[256,512]{1,0:T(8,128)(2,1)S(1)} %shard_map.92), channel_id=1, source_target_pairs={{0,2},{1,7},{2,4},{3,1},{4,6},{5,3},{6,0},{7,5},{8,14},{9,11},{10,... | collective-permute-start | bytes 786440 | tf_op jit(solution)/shard_map/ppermute | solution.py:30
